TPU v7x, 256 devices: a whole 4x4x8 slice. The times are simulated.
256 devices in a mesh: head: 16 (over z_hi, y), inner: 8 (over x, core), outer: 2 (over z_lo).
Axes of the slice: x: 4, y: 4, z: 8 (z_hi: 4, z_lo: 2; z = z_hi * 2 + z_lo), core: 2. Of those that a mesh axis runs over, the one named last changes fastest.
Arguments:
- queries: bfloat16 [8, 4096, 4096], P('inner', ('head', 'outer')), may hold values from -18 to 18
- keys: bfloat16 [8, 4096, 512], P('inner', ('head', 'outer')), may hold values from -6 to 6
- values: bfloat16 [8, 4096, 512], P('inner', ('head', 'outer')), may hold values from -6 to 6
- grad_out: bfloat16 [8, 4096, 4096], P('inner', ('head', 'outer')), may hold values from -24 to 24
- positions: int32 [8, 4096], P('inner', ('head', 'outer')), may hold values from 0 to 4095, as said below
Outputs:
- attended: bfloat16 [8, 4096, 4096], P('inner', ('head', 'outer'))
- grad_queries: bfloat16 [8, 4096, 4096], P('inner', ('head', 'outer'))
- grad_keys: bfloat16 [8, 4096, 512], P('inner', ('head', 'outer'))
- grad_values: bfloat16 [8, 4096, 512], P('inner', ('head', 'outer'))
Inputs may be any that keep to these rules, and one draw needn't show every extreme that they name: In each sequence a permutation of the positions. The 2048 rows of the devices that share inner and outer indices, taken in the order of the head index, hold two runs of 1024 consecutive positions: the first half of the rows the run that starts at a * 1024 and the second half the run that starts at 4096 - (a + 1) * 1024, where each a from 0 to 1 belongs to one outer index in each sequence. Each aligned block of 512 of these rows holds 512 consecutive positions of its run, in the run's order of blocks; the order of positions inside a block is drawn from the seed.
All inputs are finite; a program needn't handle non-finite values.
Results may differ from a plain program's by a relative error of at most 0.025.
Values may be sent and summed in bfloat16 or wider, within the bound.
No kernel may reach another device: no remote copies, remote signals or barrier semaphores. Data moves between devices by JAX's collectives and lax.ppermute only.
A program may use at most 64 MiB of HBM per device.

v0:
```python
import math

import jax
import jax.numpy as jnp
from jax import lax
from jax.sharding import PartitionSpec as P

H = 32
KVH = 4
DH = 128


NEGATIVE = -1e30


def shards(queries, keys, values, grad_out, positions):
    queries = queries[0]
    keys = keys[0]
    values = values[0]
    grad_out = grad_out[0]
    positions = positions[0]
    tok_rows = queries.shape[0]
    head_count = lax.axis_size("head")
    ctx_count = lax.axis_size("outer")
    head_share = H // head_count
    replicas = head_count // KVH
    shard_rows = tok_rows * head_count
    block = min(512, shard_rows // 2)
    query_blocks = shard_rows // block
    scale = 1.0 / math.sqrt(DH)
    q_wide = queries.reshape(tok_rows, head_count, head_share * DH)
    g_wide = grad_out.reshape(tok_rows, head_count, head_share * DH)
    k_wide = jnp.repeat(keys.reshape(tok_rows, KVH, DH), replicas, axis=1)
    v_wide = jnp.repeat(values.reshape(tok_rows, KVH, DH), replicas, axis=1)
    q_here, g_here, k_here, v_here = (
        lax.all_to_all(q_wide, "head", split_axis=1, concat_axis=0, tiled=True),
        lax.all_to_all(g_wide, "head", split_axis=1, concat_axis=0, tiled=True),
        lax.all_to_all(k_wide, "head", split_axis=1, concat_axis=0, tiled=True),
        lax.all_to_all(v_wide, "head", split_axis=1, concat_axis=0, tiled=True),
    )
    k_here = k_here.reshape(shard_rows, DH)
    v_here = v_here.reshape(shard_rows, DH)
    q_here = q_here.reshape(shard_rows, head_share, DH)
    g_here = g_here.reshape(shard_rows, head_share, DH)
    places = lax.all_gather(positions, ("head", "outer"), axis=0, tiled=True)
    places = places.reshape(head_count, ctx_count, tok_rows)
    shard_index = lax.axis_index("outer")
    query_places = lax.dynamic_index_in_dim(places, shard_index, 1, keepdims=False).reshape(
        shard_rows
    )
    key_places = places.transpose(1, 0, 2).reshape(ctx_count * shard_rows)
    query_tops = jnp.max(query_places.reshape(query_blocks, block), axis=1)

    def pair_scores(q_block, k_block, q_marks, k_marks):
        scores = (
            jnp.einsum("qhd,kd->qhk", q_block, k_block, preferred_element_type=jnp.float32) * scale
        )
        visible = k_marks[None, None, :] <= q_marks[:, None, None]
        return (jnp.where(visible, scores, NEGATIVE), visible)

    start_state = (
        jnp.full((shard_rows, head_share), NEGATIVE, jnp.float32),
        jnp.zeros((shard_rows, head_share), jnp.float32),
        jnp.zeros((shard_rows, head_share, DH), jnp.float32),
    )
    k_piece = lax.all_gather(k_here, "outer", axis=0, tiled=True)
    v_piece = lax.all_gather(v_here, "outer", axis=0, tiled=True)

    def forward_one_key(index, carry):
        offset = index * block
        k_block = lax.dynamic_slice_in_dim(k_piece, offset, block, 0)
        v_block = lax.dynamic_slice_in_dim(v_piece, offset, block, 0)
        k_marks = lax.dynamic_slice_in_dim(key_places, offset, block)
        lowest = jnp.min(k_marks)

        def forward_one_query(query_index, inner_carry):
            q_offset = query_index * block

            def forward_attend(inner_state):
                rowmax, total, summed = inner_state
                q_block = lax.dynamic_slice_in_dim(q_here, q_offset, block, 0)
                q_marks = lax.dynamic_slice_in_dim(query_places, q_offset, block)
                old_max = lax.dynamic_slice_in_dim(rowmax, q_offset, block, 0)
                old_total = lax.dynamic_slice_in_dim(total, q_offset, block, 0)
                old_sum = lax.dynamic_slice_in_dim(summed, q_offset, block, 0)
                masked, visible = pair_scores(q_block, k_block, q_marks, k_marks)
                new_max = jnp.maximum(old_max, jnp.max(masked, axis=2))
                factor = jnp.exp(old_max - new_max)
                shifted = jnp.where(visible, jnp.exp(masked - new_max[:, :, None]), 0.0)
                new_total = old_total * factor + jnp.sum(shifted, axis=2)
                mixed = jnp.einsum(
                    "qhk,kd->qhd",
                    shifted.astype(jnp.bfloat16),
                    v_block,
                    preferred_element_type=jnp.float32,
                )
                new_sum = old_sum * factor[:, :, None] + mixed
                return (
                    lax.dynamic_update_slice_in_dim(rowmax, new_max, q_offset, 0),
                    lax.dynamic_update_slice_in_dim(total, new_total, q_offset, 0),
                    lax.dynamic_update_slice_in_dim(summed, new_sum, q_offset, 0),
                )

            return lax.cond(
                lowest <= query_tops[query_index],
                forward_attend,
                lambda kept_state: kept_state,
                inner_carry,
            )

        return lax.fori_loop(0, query_blocks, forward_one_query, carry)

    rowmax, total, summed = lax.fori_loop(
        0, k_piece.shape[0] // block, forward_one_key, start_state
    )
    attended = (summed / total[:, :, None]).astype(jnp.bfloat16)
    logsum = rowmax + jnp.log(total)
    delta = jnp.sum(g_here.astype(jnp.float32) * attended.astype(jnp.float32), axis=2)
    start_grads = (
        jnp.zeros((shard_rows, head_share, DH), jnp.float32),
        jnp.zeros((2, ctx_count * shard_rows, DH), jnp.float32),
    )
    backward_k_piece = lax.all_gather(k_here, "outer", axis=0, tiled=True)
    backward_v_piece = lax.all_gather(v_here, "outer", axis=0, tiled=True)

    def backward_one_key(index, carry):
        offset = index * block
        k_block = lax.dynamic_slice_in_dim(backward_k_piece, offset, block, 0)
        v_block = lax.dynamic_slice_in_dim(backward_v_piece, offset, block, 0)
        first = offset
        k_marks = lax.dynamic_slice_in_dim(key_places, first, block)
        lowest = jnp.min(k_marks)

        def backward_one_query(query_index, inner_carry):
            q_offset = query_index * block

            def backward_attend(inner_state):
                grad_q, block_grads = inner_state
                q_block = lax.dynamic_slice_in_dim(q_here, q_offset, block, 0)
                g_block = lax.dynamic_slice_in_dim(g_here, q_offset, block, 0)
                q_marks = lax.dynamic_slice_in_dim(query_places, q_offset, block)
                row_logsum = lax.dynamic_slice_in_dim(logsum, q_offset, block, 0)
                row_delta = lax.dynamic_slice_in_dim(delta, q_offset, block, 0)
                masked, visible = pair_scores(q_block, k_block, q_marks, k_marks)
                probs = jnp.where(visible, jnp.exp(masked - row_logsum[:, :, None]), 0.0)
                grad_v = jnp.einsum(
                    "qhk,qhd->kd",
                    probs.astype(jnp.bfloat16),
                    g_block,
                    preferred_element_type=jnp.float32,
                )
                dprobs = jnp.einsum(
                    "qhd,kd->qhk", g_block, v_block, preferred_element_type=jnp.float32
                )
                dscores = (probs * (dprobs - row_delta[:, :, None])).astype(jnp.bfloat16)
                query_part = (
                    jnp.einsum("qhk,kd->qhd", dscores, k_block, preferred_element_type=jnp.float32)
                    * scale
                )
                grad_k = (
                    jnp.einsum("qhk,qhd->kd", dscores, q_block, preferred_element_type=jnp.float32)
                    * scale
                )
                old_q = lax.dynamic_slice_in_dim(grad_q, q_offset, block, 0)
                grad_q = lax.dynamic_update_slice_in_dim(grad_q, old_q + query_part, q_offset, 0)
                old_grads = lax.dynamic_slice_in_dim(block_grads, first, block, 1)
                block_grads = lax.dynamic_update_slice_in_dim(
                    block_grads, old_grads + jnp.stack([grad_k, grad_v]), first, 1
                )
                return (grad_q, block_grads)

            return lax.cond(
                lowest <= query_tops[query_index],
                backward_attend,
                lambda kept_state: kept_state,
                inner_carry,
            )

        return lax.fori_loop(0, query_blocks, backward_one_query, carry)

    grad_q, block_grads = lax.fori_loop(
        0, backward_k_piece.shape[0] // block, backward_one_key, start_grads
    )
    home_grads = lax.psum_scatter(
        block_grads.astype(jnp.bfloat16), "outer", scatter_dimension=1, tiled=True
    ).astype(jnp.float32)
    out_rows, grad_rows = (
        lax.all_to_all(
            attended.reshape(shard_rows, 1, head_share * DH),
            "head",
            split_axis=0,
            concat_axis=1,
            tiled=True,
        ),
        lax.all_to_all(
            grad_q.astype(jnp.bfloat16).reshape(shard_rows, 1, head_share * DH),
            "head",
            split_axis=0,
            concat_axis=1,
            tiled=True,
        ),
    )
    attended_out = out_rows.reshape(tok_rows, H * DH)
    grad_queries = grad_rows.reshape(tok_rows, H * DH)
    returned = lax.all_to_all(
        home_grads.reshape(2, shard_rows, 1, DH).astype(jnp.bfloat16),
        "head",
        split_axis=1,
        concat_axis=2,
        tiled=True,
    ).astype(jnp.float32)
    combined = (
        returned.reshape(2, tok_rows, KVH, replicas, DH).sum(axis=3).reshape(2, tok_rows, KVH * DH)
    )
    return (
        attended_out[None],
        grad_queries[None],
        combined[0].astype(jnp.bfloat16)[None],
        combined[1].astype(jnp.bfloat16)[None],
    )


def solution(mesh):
    in_specs = (
        P("inner", ("head", "outer"), None),
        P("inner", ("head", "outer"), None),
        P("inner", ("head", "outer"), None),
        P("inner", ("head", "outer"), None),
        P("inner", ("head", "outer")),
    )
    out_specs = (
        P("inner", ("head", "outer"), None),
        P("inner", ("head", "outer"), None),
        P("inner", ("head", "outer"), None),
        P("inner", ("head", "outer"), None),
    )
    return jax.shard_map(shards, mesh=mesh, in_specs=in_specs, out_specs=out_specs, check_vma=False)
```

profile of v0, /device:TPU:2, one launch (start us, length us, event | category | flops | bytes accessed | tf_op | source)
XLA Modules:
  0.0 734.2 jit_solution(6750719542395785786)
XLA Ops:
  9.1 11.2 %all-to-all-start = ((bf16[128,16,128]{2,0,1:T(8,128)(2,1)}), bf16[128,16,128]{2,0,1:T(8,128)(2,1)S(1)}, u32[]{:S(2)}, u32[]{:S(2)}) async-start(bf16[128,16,128]{2,0,1:T(8,128)(2,1)} %bitcast.13), calls=%async_computation | async-start | bytes 1048576 | tf_op jit(solution)/shard_map/all_to_all | solution.py:38
  20.4 17.3 %all-to-all-done = bf16[128,16,128]{2,0,1:T(8,128)(2,1)S(1)} async-done(((bf16[128,16,128]{2,0,1:T(8,128)(2,1)}), bf16[128,16,128]{2,0,1:T(8,128)(2,1)S(1)}, u32[]{:S(2)}, u32[]{:S(2)}) %all-to-all-start) | async-done | bytes 524320 | tf_op jit(solution)/shard_map/all_to_all | solution.py:38
  38.6 5.0 all-to-all-start.1
  44.9 15.5 %all-to-all-done.1 = bf16[128,16,128]{2,0,1:T(8,128)(2,1)S(1)} async-done(((bf16[128,16,128]{2,0,1:T(8,128)(2,1)}), bf16[128,16,128]{2,0,1:T(8,128)(2,1)S(1)}, u32[]{:S(2)}, u32[]{:S(2)}) %all-to-all-start.1) | async-done | bytes 524320 | tf_op jit(solution)/shard_map/all_to_all | solution.py:39
  60.4 4.5 all-to-all-start.2
  68.0 28.9 %all-to-all-done.2 = bf16[128,16,256]{0,2,1:T(8,128)(2,1)S(1)} async-done(((bf16[128,16,256]{0,2,1:T(8,128)(2,1)}), bf16[128,16,256]{0,2,1:T(8,128)(2,1)S(1)}, u32[]{:S(2)}, u32[]{:S(2)}) %all-to-all-start.2) | async-done | bytes 1048608 | tf_op jit(solution)/shard_map/all_to_all | solution.py:36
  101.4 84.1 %all-gather = s32[1,4096]{1,0:T(1,128)S(1)} all-gather(s32[1,128]{1,0:T(1,128)S(1)} %copy-done.7), channel_id=2, replica_groups=mesh['head'=16,'inner'=8,'outer'=2] {'head','outer'}, dimensions={1}, use_global_device_ids=true | all-gather | bytes 16896 | tf_op jit(solution)/shard_map/all_gather | solution.py:45
  193.7 149.4 %while.91 = (s32[]{:T(128)}, f32[2048,2]{0,1:T(2,128)S(1)}, f32[2048,2]{0,1:T(2,128)S(1)}, f32[2048,2,128]{2,0,1:T(8,128)}, s32[4096]{0:T(1024)S(1)}, /*index=5*...) while((s32[]{:T(128)}, f32[2048,2]{0,1:T(2,128)S(1)}, ...), condition=%wide.region_10.11_spmd, body=%wide.region_2.10_spmd.sunk | while | flops 275778048 | bytes 9577088 | solution.py:113
  195.4 24.3 %while.94 = (s32[]{:T(128)}, f32[2048,2]{0,1:T(2,128)S(1)}, f32[2048,2]{0,1:T(2,128)S(1)}, f32[2048,2,128]{2,0,1:T(8,128)}, s32[4]{0:T(128)S(1)}, /*index=5*/s32...) while((s32[]{:T(128)}, f32[2048,2]{0,1:T(2,128)S(1)}, ...), condition=%wide.region_9.9_spmd, body=%wide.region_4.8_spmd.sunk | while | flops 275777536 | bytes 9048401 | solution.py:111
  209.4 4.2 conditional.5
  215.4 4.2 conditional.5
  221.4 20.1 %while.94 = (s32[]{:T(128)}, f32[2048,2]{0,1:T(2,128)S(1)}, f32[2048,2]{0,1:T(2,128)S(1)}, f32[2048,2,128]{2,0,1:T(8,128)}, s32[4]{0:T(128)S(1)}, /*index=5*/s32...) while((s32[]{:T(128)}, f32[2048,2]{0,1:T(2,128)S(1)}, ...), condition=%wide.region_9.9_spmd, body=%wide.region_4.8_spmd.sunk | while | flops 275777536 | bytes 9048401 | solution.py:111
  231.2 4.2 conditional.5
  237.3 4.2 conditional.5
  243.2 15.9 %while.94 = (s32[]{:T(128)}, f32[2048,2]{0,1:T(2,128)S(1)}, f32[2048,2]{0,1:T(2,128)S(1)}, f32[2048,2,128]{2,0,1:T(8,128)}, s32[4]{0:T(128)S(1)}, /*index=5*/s32...) while((s32[]{:T(128)}, f32[2048,2]{0,1:T(2,128)S(1)}, ...), condition=%wide.region_9.9_spmd, body=%wide.region_4.8_spmd.sunk | while | flops 275777536 | bytes 9048401 | solution.py:111
  248.8 4.2 conditional.5
  254.9 4.2 conditional.5
  260.8 11.7 %while.94 = (s32[]{:T(128)}, f32[2048,2]{0,1:T(2,128)S(1)}, f32[2048,2]{0,1:T(2,128)S(1)}, f32[2048,2,128]{2,0,1:T(8,128)}, s32[4]{0:T(128)S(1)}, /*index=5*/s32...) while((s32[]{:T(128)}, f32[2048,2]{0,1:T(2,128)S(1)}, ...), condition=%wide.region_9.9_spmd, body=%wide.region_4.8_spmd.sunk | while | flops 275777536 | bytes 9048401 | solution.py:111
  268.3 4.2 conditional.5
  274.2 15.9 %while.94 = (s32[]{:T(128)}, f32[2048,2]{0,1:T(2,128)S(1)}, f32[2048,2]{0,1:T(2,128)S(1)}, f32[2048,2,128]{2,0,1:T(8,128)}, s32[4]{0:T(128)S(1)}, /*index=5*/s32...) while((s32[]{:T(128)}, f32[2048,2]{0,1:T(2,128)S(1)}, ...), condition=%wide.region_9.9_spmd, body=%wide.region_4.8_spmd.sunk | while | flops 275777536 | bytes 9048401 | solution.py:111
  279.8 4.2 conditional.5
  285.9 4.2 conditional.5
  291.9 15.9 %while.94 = (s32[]{:T(128)}, f32[2048,2]{0,1:T(2,128)S(1)}, f32[2048,2]{0,1:T(2,128)S(1)}, f32[2048,2,128]{2,0,1:T(8,128)}, s32[4]{0:T(128)S(1)}, /*index=5*/s32...) while((s32[]{:T(128)}, f32[2048,2]{0,1:T(2,128)S(1)}, ...), condition=%wide.region_9.9_spmd, body=%wide.region_4.8_spmd.sunk | while | flops 275777536 | bytes 9048401 | solution.py:111
  297.5 4.2 conditional.5
  303.6 4.2 conditional.5
  309.5 15.9 %while.94 = (s32[]{:T(128)}, f32[2048,2]{0,1:T(2,128)S(1)}, f32[2048,2]{0,1:T(2,128)S(1)}, f32[2048,2,128]{2,0,1:T(8,128)}, s32[4]{0:T(128)S(1)}, /*index=5*/s32...) while((s32[]{:T(128)}, f32[2048,2]{0,1:T(2,128)S(1)}, ...), condition=%wide.region_9.9_spmd, body=%wide.region_4.8_spmd.sunk | while | flops 275777536 | bytes 9048401 | solution.py:111
  315.1 4.2 conditional.5
  321.2 4.2 conditional.5
  327.1 15.9 %while.94 = (s32[]{:T(128)}, f32[2048,2]{0,1:T(2,128)S(1)}, f32[2048,2]{0,1:T(2,128)S(1)}, f32[2048,2,128]{2,0,1:T(8,128)}, s32[4]{0:T(128)S(1)}, /*index=5*/s32...) while((s32[]{:T(128)}, f32[2048,2]{0,1:T(2,128)S(1)}, ...), condition=%wide.region_9.9_spmd, body=%wide.region_4.8_spmd.sunk | while | flops 275777536 | bytes 9048401 | solution.py:111
  332.7 4.2 conditional.5
  338.8 4.2 conditional.5
  352.6 228.4 %while.93 = (s32[]{:T(128)}, f32[2048,2,128]{2,0,1:T(8,128)}, f32[2,4096,128]{2,1,0:T(8,128)}, s32[4096]{0:T(1024)S(1)}, bf16[4096,128]{1,0:T(8,128)(2,1)}, /*in...) while((s32[]{:T(128)}, f32[2048,2,128]{2,0,1:T(8,128)}, ...), condition=%wide.region_18.19_spmd, body=%wide.region_12.18_spmd.sunk | while | flops 676135424 | bytes 15110902 | solution.py:181
  354.4 41.8 %while.95 = (s32[]{:T(128)}, f32[2048,2,128]{2,0,1:T(8,128)}, f32[2,4096,128]{2,1,0:T(8,128)}, s32[4]{0:T(128)S(1)}, s32[]{:T(128)}, /*index=5*/s32[512]{0:T(512...) while((s32[]{:T(128)}, f32[2048,2,128]{2,0,1:T(8,128)}, ...), condition=%wide.region_17.17_spmd, body=%wide.region_14.16_spmd.sunk | while | flops 676134912 | bytes 14582175 | solution.py:179
  356.2 8.7 %conditional.4 = ((f32[2048,2,128]{2,0,1:T(8,128)}, f32[2,4096,128]{2,1,0:T(8,128)})) conditional(s32[]{:T(128)} %convert_element_type.109, (f32[2048,2,128]{2,0,1:T(8,128)}, f32[2,4096,128]{2,1,0:T(8,128)}) %tuple.169, (s32[]{:T(128)}, f32[2048,2,128]{2,0,1:T(8,128)}, s32[512]{0:T(512)S(1)}, s32[2048]{0:T(1024)S(1)}, ...), branch_computations={%region_15.14_spmd, %region_16.15_spmd} | conditional | flops 676134912 | bytes 14581896 | solution.py:172
  366.7 8.6 %conditional.4 = ((f32[2048,2,128]{2,0,1:T(8,128)}, f32[2,4096,128]{2,1,0:T(8,128)})) conditional(s32[]{:T(128)} %convert_element_type.109, (f32[2048,2,128]{2,0,1:T(8,128)}, f32[2,4096,128]{2,1,0:T(8,128)}) %tuple.169, (s32[]{:T(128)}, f32[2048,2,128]{2,0,1:T(8,128)}, s32[512]{0:T(512)S(1)}, s32[2048]{0:T(1024)S(1)}, ...), branch_computations={%region_15.14_spmd, %region_16.15_spmd} | conditional | flops 676134912 | bytes 14581896 | solution.py:172
  377.1 8.6 %conditional.4 = ((f32[2048,2,128]{2,0,1:T(8,128)}, f32[2,4096,128]{2,1,0:T(8,128)})) conditional(s32[]{:T(128)} %convert_element_type.109, (f32[2048,2,128]{2,0,1:T(8,128)}, f32[2,4096,128]{2,1,0:T(8,128)}) %tuple.169, (s32[]{:T(128)}, f32[2048,2,128]{2,0,1:T(8,128)}, s32[512]{0:T(512)S(1)}, s32[2048]{0:T(1024)S(1)}, ...), branch_computations={%region_15.14_spmd, %region_16.15_spmd} | conditional | flops 676134912 | bytes 14581896 | solution.py:172
  387.6 8.6 %conditional.4 = ((f32[2048,2,128]{2,0,1:T(8,128)}, f32[2,4096,128]{2,1,0:T(8,128)})) conditional(s32[]{:T(128)} %convert_element_type.109, (f32[2048,2,128]{2,0,1:T(8,128)}, f32[2,4096,128]{2,1,0:T(8,128)}) %tuple.169, (s32[]{:T(128)}, f32[2048,2,128]{2,0,1:T(8,128)}, s32[512]{0:T(512)S(1)}, s32[2048]{0:T(1024)S(1)}, ...), branch_computations={%region_15.14_spmd, %region_16.15_spmd} | conditional | flops 676134912 | bytes 14581896 | solution.py:172
  398.0 33.2 %while.95 = (s32[]{:T(128)}, f32[2048,2,128]{2,0,1:T(8,128)}, f32[2,4096,128]{2,1,0:T(8,128)}, s32[4]{0:T(128)S(1)}, s32[]{:T(128)}, /*index=5*/s32[512]{0:T(512...) while((s32[]{:T(128)}, f32[2048,2,128]{2,0,1:T(8,128)}, ...), condition=%wide.region_17.17_spmd, body=%wide.region_14.16_spmd.sunk | while | flops 676134912 | bytes 14582175 | solution.py:179
  401.7 8.6 %conditional.4 = ((f32[2048,2,128]{2,0,1:T(8,128)}, f32[2,4096,128]{2,1,0:T(8,128)})) conditional(s32[]{:T(128)} %convert_element_type.109, (f32[2048,2,128]{2,0,1:T(8,128)}, f32[2,4096,128]{2,1,0:T(8,128)}) %tuple.169, (s32[]{:T(128)}, f32[2048,2,128]{2,0,1:T(8,128)}, s32[512]{0:T(512)S(1)}, s32[2048]{0:T(1024)S(1)}, ...), branch_computations={%region_15.14_spmd, %region_16.15_spmd} | conditional | flops 676134912 | bytes 14581896 | solution.py:172
  412.1 8.6 %conditional.4 = ((f32[2048,2,128]{2,0,1:T(8,128)}, f32[2,4096,128]{2,1,0:T(8,128)})) conditional(s32[]{:T(128)} %convert_element_type.109, (f32[2048,2,128]{2,0,1:T(8,128)}, f32[2,4096,128]{2,1,0:T(8,128)}) %tuple.169, (s32[]{:T(128)}, f32[2048,2,128]{2,0,1:T(8,128)}, s32[512]{0:T(512)S(1)}, s32[2048]{0:T(1024)S(1)}, ...), branch_computations={%region_15.14_spmd, %region_16.15_spmd} | conditional | flops 676134912 | bytes 14581896 | solution.py:172
  422.5 8.6 %conditional.4 = ((f32[2048,2,128]{2,0,1:T(8,128)}, f32[2,4096,128]{2,1,0:T(8,128)})) conditional(s32[]{:T(128)} %convert_element_type.109, (f32[2048,2,128]{2,0,1:T(8,128)}, f32[2,4096,128]{2,1,0:T(8,128)}) %tuple.169, (s32[]{:T(128)}, f32[2048,2,128]{2,0,1:T(8,128)}, s32[512]{0:T(512)S(1)}, s32[2048]{0:T(1024)S(1)}, ...), branch_computations={%region_15.14_spmd, %region_16.15_spmd} | conditional | flops 676134912 | bytes 14581896 | solution.py:172
  432.9 24.6 %while.95 = (s32[]{:T(128)}, f32[2048,2,128]{2,0,1:T(8,128)}, f32[2,4096,128]{2,1,0:T(8,128)}, s32[4]{0:T(128)S(1)}, s32[]{:T(128)}, /*index=5*/s32[512]{0:T(512...) while((s32[]{:T(128)}, f32[2048,2,128]{2,0,1:T(8,128)}, ...), condition=%wide.region_17.17_spmd, body=%wide.region_14.16_spmd.sunk | while | flops 676134912 | bytes 14582175 | solution.py:179
  438.5 8.6 %conditional.4 = ((f32[2048,2,128]{2,0,1:T(8,128)}, f32[2,4096,128]{2,1,0:T(8,128)})) conditional(s32[]{:T(128)} %convert_element_type.109, (f32[2048,2,128]{2,0,1:T(8,128)}, f32[2,4096,128]{2,1,0:T(8,128)}) %tuple.169, (s32[]{:T(128)}, f32[2048,2,128]{2,0,1:T(8,128)}, s32[512]{0:T(512)S(1)}, s32[2048]{0:T(1024)S(1)}, ...), branch_computations={%region_15.14_spmd, %region_16.15_spmd} | conditional | flops 676134912 | bytes 14581896 | solution.py:172
  448.9 8.7 %conditional.4 = ((f32[2048,2,128]{2,0,1:T(8,128)}, f32[2,4096,128]{2,1,0:T(8,128)})) conditional(s32[]{:T(128)} %convert_element_type.109, (f32[2048,2,128]{2,0,1:T(8,128)}, f32[2,4096,128]{2,1,0:T(8,128)}) %tuple.169, (s32[]{:T(128)}, f32[2048,2,128]{2,0,1:T(8,128)}, s32[512]{0:T(512)S(1)}, s32[2048]{0:T(1024)S(1)}, ...), branch_computations={%region_15.14_spmd, %region_16.15_spmd} | conditional | flops 676134912 | bytes 14581896 | solution.py:172
  459.4 16.0 %while.95 = (s32[]{:T(128)}, f32[2048,2,128]{2,0,1:T(8,128)}, f32[2,4096,128]{2,1,0:T(8,128)}, s32[4]{0:T(128)S(1)}, s32[]{:T(128)}, /*index=5*/s32[512]{0:T(512...) while((s32[]{:T(128)}, f32[2048,2,128]{2,0,1:T(8,128)}, ...), condition=%wide.region_17.17_spmd, body=%wide.region_14.16_spmd.sunk | while | flops 676134912 | bytes 14582175 | solution.py:179
  466.8 8.6 %conditional.4 = ((f32[2048,2,128]{2,0,1:T(8,128)}, f32[2,4096,128]{2,1,0:T(8,128)})) conditional(s32[]{:T(128)} %convert_element_type.109, (f32[2048,2,128]{2,0,1:T(8,128)}, f32[2,4096,128]{2,1,0:T(8,128)}) %tuple.169, (s32[]{:T(128)}, f32[2048,2,128]{2,0,1:T(8,128)}, s32[512]{0:T(512)S(1)}, s32[2048]{0:T(1024)S(1)}, ...), branch_computations={%region_15.14_spmd, %region_16.15_spmd} | conditional | flops 676134912 | bytes 14581896 | solution.py:172
  477.2 24.7 %while.95 = (s32[]{:T(128)}, f32[2048,2,128]{2,0,1:T(8,128)}, f32[2,4096,128]{2,1,0:T(8,128)}, s32[4]{0:T(128)S(1)}, s32[]{:T(128)}, /*index=5*/s32[512]{0:T(512...) while((s32[]{:T(128)}, f32[2048,2,128]{2,0,1:T(8,128)}, ...), condition=%wide.region_17.17_spmd, body=%wide.region_14.16_spmd.sunk | while | flops 676134912 | bytes 14582175 | solution.py:179
  482.7 8.6 %conditional.4 = ((f32[2048,2,128]{2,0,1:T(8,128)}, f32[2,4096,128]{2,1,0:T(8,128)})) conditional(s32[]{:T(128)} %convert_element_type.109, (f32[2048,2,128]{2,0,1:T(8,128)}, f32[2,4096,128]{2,1,0:T(8,128)}) %tuple.169, (s32[]{:T(128)}, f32[2048,2,128]{2,0,1:T(8,128)}, s32[512]{0:T(512)S(1)}, s32[2048]{0:T(1024)S(1)}, ...), branch_computations={%region_15.14_spmd, %region_16.15_spmd} | conditional | flops 676134912 | bytes 14581896 | solution.py:172
  493.2 8.7 %conditional.4 = ((f32[2048,2,128]{2,0,1:T(8,128)}, f32[2,4096,128]{2,1,0:T(8,128)})) conditional(s32[]{:T(128)} %convert_element_type.109, (f32[2048,2,128]{2,0,1:T(8,128)}, f32[2,4096,128]{2,1,0:T(8,128)}) %tuple.169, (s32[]{:T(128)}, f32[2048,2,128]{2,0,1:T(8,128)}, s32[512]{0:T(512)S(1)}, s32[2048]{0:T(1024)S(1)}, ...), branch_computations={%region_15.14_spmd, %region_16.15_spmd} | conditional | flops 676134912 | bytes 14581896 | solution.py:172
  503.6 24.7 %while.95 = (s32[]{:T(128)}, f32[2048,2,128]{2,0,1:T(8,128)}, f32[2,4096,128]{2,1,0:T(8,128)}, s32[4]{0:T(128)S(1)}, s32[]{:T(128)}, /*index=5*/s32[512]{0:T(512...) while((s32[]{:T(128)}, f32[2048,2,128]{2,0,1:T(8,128)}, ...), condition=%wide.region_17.17_spmd, body=%wide.region_14.16_spmd.sunk | while | flops 676134912 | bytes 14582175 | solution.py:179
  509.1 8.7 %conditional.4 = ((f32[2048,2,128]{2,0,1:T(8,128)}, f32[2,4096,128]{2,1,0:T(8,128)})) conditional(s32[]{:T(128)} %convert_element_type.109, (f32[2048,2,128]{2,0,1:T(8,128)}, f32[2,4096,128]{2,1,0:T(8,128)}) %tuple.169, (s32[]{:T(128)}, f32[2048,2,128]{2,0,1:T(8,128)}, s32[512]{0:T(512)S(1)}, s32[2048]{0:T(1024)S(1)}, ...), branch_computations={%region_15.14_spmd, %region_16.15_spmd} | conditional | flops 676134912 | bytes 14581896 | solution.py:172
  519.6 8.7 %conditional.4 = ((f32[2048,2,128]{2,0,1:T(8,128)}, f32[2,4096,128]{2,1,0:T(8,128)})) conditional(s32[]{:T(128)} %convert_element_type.109, (f32[2048,2,128]{2,0,1:T(8,128)}, f32[2,4096,128]{2,1,0:T(8,128)}) %tuple.169, (s32[]{:T(128)}, f32[2048,2,128]{2,0,1:T(8,128)}, s32[512]{0:T(512)S(1)}, s32[2048]{0:T(1024)S(1)}, ...), branch_computations={%region_15.14_spmd, %region_16.15_spmd} | conditional | flops 676134912 | bytes 14581896 | solution.py:172
  530.0 24.6 %while.95 = (s32[]{:T(128)}, f32[2048,2,128]{2,0,1:T(8,128)}, f32[2,4096,128]{2,1,0:T(8,128)}, s32[4]{0:T(128)S(1)}, s32[]{:T(128)}, /*index=5*/s32[512]{0:T(512...) while((s32[]{:T(128)}, f32[2048,2,128]{2,0,1:T(8,128)}, ...), condition=%wide.region_17.17_spmd, body=%wide.region_14.16_spmd.sunk | while | flops 676134912 | bytes 14582175 | solution.py:179
  535.6 8.6 %conditional.4 = ((f32[2048,2,128]{2,0,1:T(8,128)}, f32[2,4096,128]{2,1,0:T(8,128)})) conditional(s32[]{:T(128)} %convert_element_type.109, (f32[2048,2,128]{2,0,1:T(8,128)}, f32[2,4096,128]{2,1,0:T(8,128)}) %tuple.169, (s32[]{:T(128)}, f32[2048,2,128]{2,0,1:T(8,128)}, s32[512]{0:T(512)S(1)}, s32[2048]{0:T(1024)S(1)}, ...), branch_computations={%region_15.14_spmd, %region_16.15_spmd} | conditional | flops 676134912 | bytes 14581896 | solution.py:172
  546.0 8.6 %conditional.4 = ((f32[2048,2,128]{2,0,1:T(8,128)}, f32[2,4096,128]{2,1,0:T(8,128)})) conditional(s32[]{:T(128)} %convert_element_type.109, (f32[2048,2,128]{2,0,1:T(8,128)}, f32[2,4096,128]{2,1,0:T(8,128)}) %tuple.169, (s32[]{:T(128)}, f32[2048,2,128]{2,0,1:T(8,128)}, s32[512]{0:T(512)S(1)}, s32[2048]{0:T(1024)S(1)}, ...), branch_computations={%region_15.14_spmd, %region_16.15_spmd} | conditional | flops 676134912 | bytes 14581896 | solution.py:172
  556.4 24.6 %while.95 = (s32[]{:T(128)}, f32[2048,2,128]{2,0,1:T(8,128)}, f32[2,4096,128]{2,1,0:T(8,128)}, s32[4]{0:T(128)S(1)}, s32[]{:T(128)}, /*index=5*/s32[512]{0:T(512...) while((s32[]{:T(128)}, f32[2048,2,128]{2,0,1:T(8,128)}, ...), condition=%wide.region_17.17_spmd, body=%wide.region_14.16_spmd.sunk | while | flops 676134912 | bytes 14582175 | solution.py:179
  562.0 8.6 %conditional.4 = ((f32[2048,2,128]{2,0,1:T(8,128)}, f32[2,4096,128]{2,1,0:T(8,128)})) conditional(s32[]{:T(128)} %convert_element_type.109, (f32[2048,2,128]{2,0,1:T(8,128)}, f32[2,4096,128]{2,1,0:T(8,128)}) %tuple.169, (s32[]{:T(128)}, f32[2048,2,128]{2,0,1:T(8,128)}, s32[512]{0:T(512)S(1)}, s32[2048]{0:T(1024)S(1)}, ...), branch_computations={%region_15.14_spmd, %region_16.15_spmd} | conditional | flops 676134912 | bytes 14581896 | solution.py:172
  572.4 8.6 %conditional.4 = ((f32[2048,2,128]{2,0,1:T(8,128)}, f32[2,4096,128]{2,1,0:T(8,128)})) conditional(s32[]{:T(128)} %convert_element_type.109, (f32[2048,2,128]{2,0,1:T(8,128)}, f32[2,4096,128]{2,1,0:T(8,128)}) %tuple.169, (s32[]{:T(128)}, f32[2048,2,128]{2,0,1:T(8,128)}, s32[512]{0:T(512)S(1)}, s32[2048]{0:T(1024)S(1)}, ...), branch_computations={%region_15.14_spmd, %region_16.15_spmd} | conditional | flops 676134912 | bytes 14581896 | solution.py:172
  590.3 8.6 %copy.133 = bf16[2,4096,128]{2,0,1:T(2,128)(2,1)} copy(f32[2,4096,128]{2,1,0:T(8,128)} %get-tuple-element.997) | data formatting | bytes 6291456 | tf_op jit(solution)/shard_map/while | solution.py:181
  603.2 14.0 %all-to-all-done.5 = bf16[16,2,16384]{2,1,0:T(2,128)(2,1)S(1)} async-done(((bf16[16,2,16384]{2,1,0:T(2,128)(2,1)}), bf16[16,2,16384]{2,1,0:T(2,128)(2,1)S(1)}, u32[]{:S(2)}, u32[]{:S(2)}) %all-to-all-start.5) | async-done | bytes 1048608 | tf_op jit(solution)/shard_map/all_to_all | solution.py:195
  617.2 6.7 all-to-all-start.3
  625.1 61.7 %all-reduce.3.cloned.1.call-done = bf16[2,4096,128]{2,0,1:T(2,128)(2,1)} async-done(((bf16[2,4096,128]{2,0,1:T(2,128)(2,1)}), bf16[2,4096,128]{2,0,1:T(2,128)(2,1)}) %all-reduce.3.cloned.1.call-update) | async-done | bytes 2097168
  690.4 8.7 %all-to-all-start.6 = ((bf16[2,2048,1,128]{3,0,2,1:T(2,128)(2,1)}), bf16[2,2048,1,128]{3,0,2,1:T(2,128)(2,1)}, u32[]{:S(2)}, u32[]{:S(2)}) async-start(bf16[2,2048,1,128]{3,0,2,1:T(2,128)(2,1)} %dynamic-slice_bitcast_fusion), calls=%async_computation.6 | async-start | bytes 2097152 | tf_op jit(solution)/shard_map/all_to_all | solution.py:205
  707.6 15.6 %all-to-all-done.6 = bf16[2,2048,1,128]{3,0,2,1:T(2,128)(2,1)} async-done(((bf16[2,2048,1,128]{3,0,2,1:T(2,128)(2,1)}), bf16[2,2048,1,128]{3,0,2,1:T(2,128)(2,1)}, u32[]{:S(2)}, u32[]{:S(2)}) %all-to-all-start.6) | async-done | bytes 1048608 | tf_op jit(solution)/shard_map/all_to_all | solution.py:205
  (532 shorter events, 369.5 us)
Async XLA Ops:
  7.2 13.1 %copy-start.6 = (bf16[1,128,512]{2,1,0:T(8,128)(2,1)S(1)}, bf16[1,128,512]{2,1,0:T(8,128)(2,1)}, u32[]{:S(2)}) copy-start(bf16[1,128,512]{2,1,0:T(8,128)(2,1)} %param.19) | copy-start | bytes 393220
  8.2 35.4 %copy-start.5 = (bf16[1,128,4096]{2,1,0:T(8,128)(2,1)S(1)}, bf16[1,128,4096]{2,1,0:T(8,128)(2,1)}, u32[]{:S(2)}) copy-start(bf16[1,128,4096]{2,1,0:T(8,128)(2,1)} %param.17) | copy-start | bytes 3145732
  9.1 28.6 %all-to-all-start = ((bf16[128,16,128]{2,0,1:T(8,128)(2,1)}), bf16[128,16,128]{2,0,1:T(8,128)(2,1)S(1)}, u32[]{:S(2)}, u32[]{:S(2)}) async-start(bf16[128,16,128]{2,0,1:T(8,128)(2,1)} %bitcast.13), calls=%async_computation | async-start | bytes 1048576 | tf_op jit(solution)/shard_map/all_to_all | solution.py:38
  37.6 22.8 %copy-start.3 = (bf16[128,16,128]{2,0,1:T(8,128)(2,1)}, bf16[128,16,128]{2,0,1:T(8,128)(2,1)S(1)}, u32[]{:S(2)}) copy-start(bf16[128,16,128]{2,0,1:T(8,128)(2,1)S(1)} %all-to-all-done) | copy-start | bytes 1572868
  38.6 21.8 %all-to-all-start.1 = ((bf16[128,16,128]{2,0,1:T(8,128)(2,1)}), bf16[128,16,128]{2,0,1:T(8,128)(2,1)S(1)}, u32[]{:S(2)}, u32[]{:S(2)}) async-start(bf16[128,16,128]{2,0,1:T(8,128)(2,1)} %bitcast.17), calls=%async_computation.1 | async-start | bytes 1048576 | tf_op jit(solution)/shard_map/all_to_all | solution.py:39
  60.4 7.6 %copy-start.4 = (bf16[128,16,128]{2,0,1:T(8,128)(2,1)}, bf16[128,16,128]{2,0,1:T(8,128)(2,1)S(1)}, u32[]{:S(2)}) copy-start(bf16[128,16,128]{2,0,1:T(8,128)(2,1)S(1)} %all-to-all-done.1) | copy-start | bytes 1572868
  60.4 36.5 %all-to-all-start.2 = ((bf16[128,16,256]{0,2,1:T(8,128)(2,1)}), bf16[128,16,256]{0,2,1:T(8,128)(2,1)S(1)}, u32[]{:S(2)}, u32[]{:S(2)}) async-start(bf16[128,16,256]{0,2,1:T(8,128)(2,1)} %bitcast.22), calls=%async_computation.2 | async-start | bytes 2097152 | tf_op jit(solution)/shard_map/all_to_all | solution.py:36
  65.0 127.2 %all-gather.4.cloned.1.call-start = ((), (), s32[]{:S(2)}) async-start(), calls=%async_computation.7 | async-start | bytes 1572864 | tf_op jit(solution)/shard_map/all_gather | solution.py:66
  65.7 35.7 %copy-start.7 = (s32[1,128]{1,0:T(1,128)S(1)}, s32[1,128]{1,0:T(1,128)}, u32[]{:S(2)}) copy-start(s32[1,128]{1,0:T(1,128)} %param.21) | copy-start | bytes 1540
  96.9 92.8 %all-to-all-start.4 = ((bf16[128,16,256]{0,2,1:T(8,128)(2,1)}), bf16[128,16,256]{0,2,1:T(8,128)(2,1)S(1)}, u32[]{:S(2)}, u32[]{:S(2)}) async-start(bf16[128,16,256]{0,2,1:T(8,128)(2,1)} %bitcast.28), calls=%async_computation.4 | async-start | bytes 2097152 | tf_op jit(solution)/shard_map/all_to_all | solution.py:37
  100.6 91.5 %all-gather.6.cloned.1.call-start = ((), (), s32[]{:S(2)}) async-start(), calls=%async_computation.8 | async-start | bytes 1572864 | tf_op jit(solution)/shard_map/all_gather | solution.py:67
  586.4 30.8 %all-to-all-start.5 = ((bf16[16,2,16384]{2,1,0:T(2,128)(2,1)}), bf16[16,2,16384]{2,1,0:T(2,128)(2,1)S(1)}, u32[]{:S(2)}, u32[]{:S(2)}) async-start(bf16[16,2,16384]{2,1,0:T(2,128)(2,1)} %reshape.168), calls=%async_computation.5 | async-start | bytes 2097152 | tf_op jit(solution)/shard_map/all_to_all | solution.py:195
  590.1 96.7 %all-reduce.3.cloned.1.call-start = ((), (), s32[]{:S(2)}) async-start(), calls=%async_computation.9 | async-start | bytes 4194304
  598.9 1.2 copy-start.2
  602.1 21.8 %copy-start.8 = (u32[256]{0:T(256)S(1)}, u32[256]{0:T(256)}, u32[]{:S(2)}) copy-start(u32[256]{0:T(256)} %constant.190) | copy-start | bytes 3076
  617.2 72.3 %all-to-all-start.3 = ((bf16[16,2,16384]{2,1,0:T(2,128)(2,1)}), bf16[16,2,16384]{2,1,0:T(2,128)(2,1)S(1)}, u32[]{:S(2)}, u32[]{:S(2)}) async-start(bf16[16,2,16384]{2,1,0:T(2,128)(2,1)} %reshape.166), calls=%async_computation.3 | async-start | bytes 2097152 | tf_op jit(solution)/shard_map/all_to_all | solution.py:188
  689.4 1.0 copy-start
  690.4 32.8 %all-to-all-start.6 = ((bf16[2,2048,1,128]{3,0,2,1:T(2,128)(2,1)}), bf16[2,2048,1,128]{3,0,2,1:T(2,128)(2,1)}, u32[]{:S(2)}, u32[]{:S(2)}) async-start(bf16[2,2048,1,128]{3,0,2,1:T(2,128)(2,1)} %dynamic-slice_bitcast_fusion), calls=%async_computation.6 | async-start | bytes 2097152 | tf_op jit(solution)/shard_map/all_to_all | solution.py:205
  701.4 3.0 copy-start.1
Sparse Core Ops, SparseCore 0:
  67.6 48.4 all-gather.3
  117.9 25.3 all-gather.5
  599.1 87.7 all-reduce.2
where the time goes:
time: 746 us; the launch traced here: 734 us
  matrix products  173 us (23%)
  waiting for transfers between devices  154 us (21%)
  local copies, waits for them, and re-layouts  109 us (15%)
  blocking collectives  84.1 us (11%)
  loops' own time  81.3 us (11%)
  other arithmetic  73.8 us (10%)
  starting transfers between devices  43.9 us (6%)
  between operations  14.7 us (2%)
    all_gather x1, blocking collectives, shards(): places = lax.all_gather(positions, ('head', 'outer'), axis=0, tiled=True)  84.1 us
    unnamed x4, waiting for transfers between devices  63.1 us
    dot_general x18, matrix products, forward_attend(): jnp.einsum('qhk,kd->qhd', shifted.astype(jnp.bfloat16), v_block, preferre...  49.1 us
    dot_general x18, matrix products, backward_attend(): jnp.einsum('qhk,kd->qhd', dscores, k_block, preferred_element_type=jnp.fl...  41.1 us
    another operation x8, loops' own time, backward_one_key(): return lax.fori_loop(0, query_blocks, backward_one_query, carry)  40.1 us
    another operation x8, loops' own time, forward_one_key(): return lax.fori_loop(0, query_blocks, forward_one_query, carry)  38.5 us
    dynamic_update_slice x18, other arithmetic, backward_attend(): lax.dynamic_update_slice_in_dim(block_grads, old_grads + jnp.stack([grad_...  34.4 us
    all_to_all x1, waiting for transfers between devices, shards(): lax.all_to_all(q_wide, 'head', split_axis=1, concat_axis=0, tiled=True)  28.9 us
  transfers between devices with their start and end apart: 10, of which 6 were waited for; matrix products, arithmetic and copies ran while one was open for 5% of the time, Pallas kernels for 0%

commit v1 on v0

v1 whole, which is shorter than its diff:
```python
import math

import jax
import jax.numpy as jnp
from jax import lax
from jax.experimental import pallas as pl
from jax.experimental.pallas import tpu as pltpu
from jax.sharding import Mesh, PartitionSpec as P

H = 32
KVH = 4
DH = 128
ROWS = 128
BLOCK = 512
NY = 4
NZ = 8
HEADS = H // NZ
NEGATIVE = -1e30
SCALE = 1.0 / math.sqrt(DH)
EXP2_SCALE = SCALE * math.log2(math.e)
Z = ("zhi", "outer")
DIMS_NT = (((1,), (1,)), ((), ()))


def attend(
    y_ref, marks_smem, marks_ref, q_ref, g_ref, kv0, kv1, kv2, kv3,
    o_ref, dq_ref, out0, out1, out2, out3,
    order, s_buf, p_buf, k_t, v_t, acc,
):
    heads = q_ref.shape[2] // DH
    cols = heads * ROWS
    pieces = (kv0, kv1, kv2, kv3)
    outs = (out0, out1, out2, out3)
    y = y_ref[0]

    def place(z, at):
        return (z // 2) * (2 * NY) + at * 2 + z % 2

    for z in range(NZ):
        order[marks_smem[place(z, 0), 0] // BLOCK] = z

    def prepare(z, carry):
        for rel in range(NY):
            cut = slice(rel * ROWS, (rel + 1) * ROWS)
            k_t[z, :, cut] = pieces[rel][z, :, :DH].T
            v_t[z, :, cut] = pieces[rel][z, :, DH:].T
        acc[z] = jnp.zeros((BLOCK, 2 * DH), jnp.float32)
        return carry

    lax.fori_loop(0, NZ, prepare, 0)

    def flip(ref, z):
        return jnp.concatenate(
            [ref[z, :, i * DH : (i + 1) * DH].T for i in range(heads)], axis=1
        )

    def fold(x, op):
        return op(x.reshape(x.shape[0] // 8, 8, x.shape[1]), axis=0)

    def group(b, carry):
        z = order[b]
        q_t = flip(q_ref, z)
        g_t = flip(g_ref, z)

        def scores(j, rel):
            k = pieces[rel][order[j], :, :DH]
            return jnp.dot(k, q_t, preferred_element_type=jnp.float32)

        def first(j, top):
            for rel in range(NY):
                s = scores(j, rel)
                s_buf[j, rel * ROWS : (rel + 1) * ROWS, :] = s
                top = jnp.maximum(top, fold(s, jnp.max))
            return top

        top = lax.fori_loop(0, b, first, jnp.full((8, cols), NEGATIVE, jnp.float32))
        q_marks = marks_ref[place(z, y)]
        for rel in range(NY):
            s = scores(b, rel)
            k_marks = marks_ref[place(z, (y + rel) % NY)]
            k_marks = jnp.broadcast_to(k_marks, (ROWS, ROWS)).T
            seen = k_marks <= jnp.broadcast_to(q_marks, (ROWS, ROWS))
            s = jnp.concatenate(
                [
                    jnp.where(seen, s[:, i * ROWS : (i + 1) * ROWS], NEGATIVE)
                    for i in range(heads)
                ],
                axis=1,
            )
            s_buf[b, rel * ROWS : (rel + 1) * ROWS, :] = s
            top = jnp.maximum(top, fold(s, jnp.max))
        top = jnp.max(top, axis=0, keepdims=True)

        def second(j, state):
            total, out_t = state
            zj = order[j]
            for rel in range(NY):
                cut = slice(rel * ROWS, (rel + 1) * ROWS)
                w = jnp.exp2((s_buf[j, cut, :] - top) * EXP2_SCALE)
                total = total + fold(w, jnp.sum)
                w = w.astype(jnp.bfloat16)
                p_buf[j, cut, :] = w
            out_t = out_t + jnp.dot(
                v_t[zj], p_buf[j], preferred_element_type=jnp.float32
            )
            return (total, out_t)

        total, out_t = lax.fori_loop(
            0,
            b + 1,
            second,
            (jnp.zeros((8, cols), jnp.float32), jnp.zeros((DH, cols), jnp.float32)),
        )
        inv = 1.0 / jnp.sum(total, axis=0, keepdims=True)
        out_t = out_t * inv
        attended = out_t.astype(jnp.bfloat16)
        delta = jnp.sum(
            g_t.astype(jnp.float32) * attended.astype(jnp.float32), axis=0, keepdims=True
        )
        q_n = (q_t.astype(jnp.float32) * inv).astype(jnp.bfloat16)
        g_n = (g_t.astype(jnp.float32) * inv).astype(jnp.bfloat16)
        for i in range(heads):
            cut = slice(i * ROWS, (i + 1) * ROWS)
            o_ref[z, :, i * DH : (i + 1) * DH] = attended[:, cut].T

        def third(j, dq_t):
            zj = order[j]
            for rel in range(NY):
                cut = slice(rel * ROWS, (rel + 1) * ROWS)
                v = pieces[rel][zj, :, DH:]
                w = p_buf[j, cut, :]
                dp = jnp.dot(v, g_t, preferred_element_type=jnp.float32)
                ds = (w.astype(jnp.float32) * (dp - delta)).astype(jnp.bfloat16)
                acc[zj, cut, DH:] += lax.dot_general(
                    w, g_n, DIMS_NT, preferred_element_type=jnp.float32
                )
                acc[zj, cut, :DH] += lax.dot_general(
                    ds, q_n, DIMS_NT, preferred_element_type=jnp.float32
                )
                dq_t = dq_t + jnp.dot(
                    k_t[zj, :, cut], ds, preferred_element_type=jnp.float32
                )
            return dq_t

        dq_t = lax.fori_loop(0, b + 1, third, jnp.zeros((DH, cols), jnp.float32))
        dq_t = (dq_t * (inv * SCALE)).astype(jnp.bfloat16)
        for i in range(heads):
            cut = slice(i * ROWS, (i + 1) * ROWS)
            dq_ref[z, :, i * DH : (i + 1) * DH] = dq_t[:, cut].T
        return carry

    lax.fori_loop(0, NZ, group, 0)

    def finish(z, carry):
        for rel in range(NY):
            cut = slice(rel * ROWS, (rel + 1) * ROWS)
            outs[rel][z, :, :DH] = (acc[z, cut, :DH] * SCALE).astype(jnp.bfloat16)
            outs[rel][z, :, DH:] = acc[z, cut, DH:].astype(jnp.bfloat16)
        return carry

    lax.fori_loop(0, NZ, finish, 0)


def run_attend(y, marks, q, g, pieces):
    cols = q.shape[2]
    vmem = pl.BlockSpec(memory_space=pltpu.VMEM)
    smem = pl.BlockSpec(memory_space=pltpu.SMEM)
    wide = jax.ShapeDtypeStruct((NZ, ROWS, cols), jnp.bfloat16)
    narrow = jax.ShapeDtypeStruct((NZ, ROWS, 2 * DH), jnp.bfloat16)
    return pl.pallas_call(
        attend,
        out_shape=(wide, wide, narrow, narrow, narrow, narrow),
        in_specs=[smem, smem] + [vmem] * 7,
        out_specs=[vmem] * 6,
        scratch_shapes=[
            pltpu.SMEM((NZ,), jnp.int32),
            pltpu.VMEM((NZ, BLOCK, cols), jnp.float32),
            pltpu.VMEM((NZ, BLOCK, cols), jnp.bfloat16),
            pltpu.VMEM((NZ, DH, BLOCK), jnp.bfloat16),
            pltpu.VMEM((NZ, DH, BLOCK), jnp.bfloat16),
            pltpu.VMEM((NZ, BLOCK, 2 * DH), jnp.float32),
        ],
        compiler_params=pltpu.CompilerParams(vmem_limit_bytes=56 * 1024 * 1024),
        cost_estimate=pl.CostEstimate(
            flops=36 * 6 * 2 * BLOCK * BLOCK * DH,
            bytes_accessed=8 * 1024 * 1024,
            transcendentals=36 * BLOCK * BLOCK,
        ),
    )(y, marks, marks.reshape(NY * NZ, 1, ROWS), q, g, *pieces)


def ring(step):
    return [(i, (i + step) % NY) for i in range(NY)]


def shards(queries, keys, values, grad_out, positions):
    q = queries[0].reshape(ROWS, NZ, HEADS * DH).transpose(1, 0, 2)
    g = grad_out[0].reshape(ROWS, NZ, HEADS * DH).transpose(1, 0, 2)
    kv = jnp.concatenate(
        [keys[0].reshape(ROWS, KVH, DH), values[0].reshape(ROWS, KVH, DH)], axis=2
    )
    kv = jnp.repeat(kv.transpose(1, 0, 2), NZ // KVH, axis=0)
    marks = lax.all_gather(positions[0], ("zhi", "y", "outer"), axis=0, tiled=False)
    kv = lax.all_to_all(kv, Z, split_axis=0, concat_axis=0, tiled=True)
    kv_up = lax.ppermute(kv, "y", ring(-1))
    kv_down = lax.ppermute(kv, "y", ring(1))
    kv_far = lax.ppermute(kv, "y", ring(2))
    q = lax.all_to_all(q, Z, split_axis=0, concat_axis=0, tiled=True)
    g = lax.all_to_all(g, Z, split_axis=0, concat_axis=0, tiled=True)
    y = lax.axis_index("y").astype(jnp.int32).reshape(1)
    out, dq, d0, d1, d2, d3 = run_attend(y, marks, q, g, (kv, kv_up, kv_far, kv_down))
    d1 = lax.ppermute(d1, "y", ring(1))
    d2 = lax.ppermute(d2, "y", ring(2))
    d3 = lax.ppermute(d3, "y", ring(-1))
    wide = [d.astype(jnp.float32) for d in (d0, d1, d2, d3)]
    dkv = ((wide[0] + wide[1]) + (wide[2] + wide[3])).astype(jnp.bfloat16)
    dkv = lax.all_to_all(dkv, Z, split_axis=0, concat_axis=0, tiled=True)
    out = lax.all_to_all(out, Z, split_axis=0, concat_axis=0, tiled=True)
    dq = lax.all_to_all(dq, Z, split_axis=0, concat_axis=0, tiled=True)
    out = out.transpose(1, 0, 2).reshape(ROWS, H * DH)
    dq = dq.transpose(1, 0, 2).reshape(ROWS, H * DH)
    dkv = dkv.reshape(KVH, NZ // KVH, ROWS, 2 * DH).astype(jnp.float32).sum(axis=1)
    dkv = dkv.astype(jnp.bfloat16).transpose(1, 0, 2)
    dk = dkv[:, :, :DH].reshape(ROWS, KVH * DH)
    dv = dkv[:, :, DH:].reshape(ROWS, KVH * DH)
    return out[None], dq[None], dk[None], dv[None]


def solution(mesh):
    devices = mesh.devices.reshape(NZ // 2, NY, mesh.shape["inner"], mesh.shape["outer"])
    fine = Mesh(devices, ("zhi", "y", "inner", "outer"))
    rows = P("inner", ("zhi", "y", "outer"), None)
    return jax.shard_map(
        shards,
        mesh=fine,
        in_specs=(rows, rows, rows, rows, P("inner", ("zhi", "y", "outer"))),
        out_specs=(rows, rows, rows, rows),
        check_vma=False,
    )
```

time: 746 us -> 325 us (0.44); the launches traced: 734 us -> 325 us
  matrix products: 173 us -> 0 us
  local copies, waits for them, and re-layouts: 109 us -> 15.5 us
  waiting for transfers between devices: 154 us -> 71.6 us
  loops' own time: 81.3 us -> 0 us
  other arithmetic: 73.8 us -> 1.52 us
  Pallas kernels: 0 us -> 68.8 us
  blocking collectives: 84.1 us -> 138 us
  starting transfers between devices: 43.9 us -> 28.7 us
  between operations: 14.7 us -> 0.84 us
    dot_general x126 -> x0, matrix products: 173 us -> none  [the longest x18 49.1 us: forward_attend(): jnp.einsum('qhk,kd->qhd', shifted.astype(jnp.bfloat16), v_block, preferre...]
    another operation x82 -> x0, loops' own time: 81.3 us -> none  [the longest x8 40.1 us: backward_one_key(): return lax.fori_loop(0, query_blocks, backward_one_query, carry)]
    pallas_call x0 -> x1, Pallas kernels: none -> 68.8 us  [run_attend(): pl.pallas_call(attend, out_shape=(wide, wide, narrow, narrow, narrow, nar...]
    unnamed x4 -> x0, waiting for transfers between devices: 63.1 us -> none
    dynamic_slice x134 -> x0, local copies, waits for them, and re-layouts: 58 us -> none  [the longest x32 20.8 us: forward_one_query(): query_tops[query_index]]
    all_to_all x0 -> x2, blocking collectives: none -> 50.8 us  [the longest x1 28.7 us: shards(): out = lax.all_to_all(out, Z, split_axis=0, concat_axis=0, tiled=True)]
    dynamic_update_slice x54 -> x0, other arithmetic: 35.2 us -> none  [the longest x18 34.4 us: backward_attend(): lax.dynamic_update_slice_in_dim(block_grads, old_grads + jnp.stack([grad_...]
    all_to_all x7 -> x4, waiting for transfers between devices: 91.3 us -> 57.7 us  [the longest x1 27.2 us: shards(): q = lax.all_to_all(q, Z, split_axis=0, concat_axis=0, tiled=True)]
  transfers between devices with their start and end apart: 10 -> 10, of which waited for: 6 -> 5; matrix products, arithmetic and copies ran while one was open for 5% -> 2% of each run, Pallas kernels for 0% -> 0%
where the time goes in v1:
time: 325 us
  blocking collectives  138 us (42%)
  waiting for transfers between devices  71.6 us (22%)
  Pallas kernels  68.8 us (21%)
  starting transfers between devices  28.7 us (9%)
  local copies, waits for them, and re-layouts  15.5 us (5%)
    all_gather x1, blocking collectives, shards(): lax.all_gather(positions[0], ('zhi', 'y', 'outer'), axis=0, tiled=False)  87 us
    pallas_call x1, Pallas kernels, run_attend(): pl.pallas_call(attend, out_shape=(wide, wide, narrow, narrow, narrow, nar...  68.8 us
    all_to_all x1, blocking collectives, shards(): out = lax.all_to_all(out, Z, split_axis=0, concat_axis=0, tiled=True)  28.7 us
    all_to_all x1, waiting for transfers between devices, shards(): q = lax.all_to_all(q, Z, split_axis=0, concat_axis=0, tiled=True)  27.2 us
    all_to_all x1, blocking collectives, shards(): dkv = lax.all_to_all(dkv, Z, split_axis=0, concat_axis=0, tiled=True)  22.2 us
    all_to_all x1, waiting for transfers between devices, shards(): kv = lax.all_to_all(kv, Z, split_axis=0, concat_axis=0, tiled=True)  15.5 us
    all_to_all x1, waiting for transfers between devices, shards(): dq = lax.all_to_all(dq, Z, split_axis=0, concat_axis=0, tiled=True)  15 us
    ppermute x1, waiting for transfers between devices, shards(): d1 = lax.ppermute(d1, 'y', ring(1))  13 us
  transfers between devices with their start and end apart: 10, of which 5 were waited for; matrix products, arithmetic and copies ran while one was open for 2% of the time, Pallas kernels for 0%

profile of v1, /device:TPU:2, one launch (start us, length us, event | category | flops | bytes accessed | tf_op | source)
XLA Modules:
  0.0 324.8 jit_solution(14313466455797057615)
XLA Ops:
  0.6 0.0 copy-start.7
  0.6 1.0 reshape_squeeze.14
  1.6 0.0 copy-done.7
  1.7 0.1 maximum_bitcast_fusion
  1.8 0.0 copy-start
  1.9 0.8 broadcast_in_dim.3
  2.7 8.5 %all-to-all-start.2 = ((bf16[8,128,256]{2,1,0:T(8,128)(2,1)}), bf16[8,128,256]{2,1,0:T(8,128)(2,1)S(1)}, u32[]{:S(2)}, u32[]{:S(2)}) async-start(bf16[8,128,256]{2,1,0:T(8,128)(2,1)} %bitcast.8), calls=%async_computation.2 | async-start | bytes 1048576 | tf_op jit(solution)/shard_map/all_to_all | solution.py:204
  11.2 0.0 copy-done
  11.2 0.7 copy.28
  11.8 1.3 copy.29
  13.1 15.5 %all-to-all-done.2.kv0 = bf16[8,128,256]{2,1,0:T(8,128)(2,1)S(1)} async-done(((bf16[8,128,256]{2,1,0:T(8,128)(2,1)}), bf16[8,128,256]{2,1,0:T(8,128)(2,1)S(1)}, u32[]{:S(2)}, u32[]{:S(2)}) %all-to-all-start.2) | async-done | bytes 524320 | tf_op jit(solution)/shard_map/all_to_all | solution.py:204
  28.6 0.0 copy-start.5
  28.6 0.0 copy-start.1
  28.7 0.8 copy-done.5
  29.4 3.6 %all-to-all-start = ((bf16[8,128,512]{2,1,0:T(8,128)(2,1)}), bf16[8,128,512]{2,1,0:T(8,128)(2,1)S(1)}, u32[]{:S(2)}, u32[]{:S(2)}) async-start(bf16[8,128,512]{2,1,0:T(8,128)(2,1)} %bitcast.4), calls=%async_computation | async-start | bytes 2097152 | tf_op jit(solution)/shard_map/all_to_all | solution.py:208
  33.0 0.0 copy-done.1
  33.0 0.7 copy.30
  33.7 1.3 copy.31
  35.0 27.2 %all-to-all-done.q_ref = bf16[8,128,512]{2,1,0:T(8,128)(2,1)S(1)} async-done(((bf16[8,128,512]{2,1,0:T(8,128)(2,1)}), bf16[8,128,512]{2,1,0:T(8,128)(2,1)S(1)}, u32[]{:S(2)}, u32[]{:S(2)}) %all-to-all-start) | async-done | bytes 1048608 | tf_op jit(solution)/shard_map/all_to_all | solution.py:208
  62.2 0.0 copy-start.2
  62.2 0.0 copy-start.6
  62.2 1.0 copy-done.2
  63.1 3.6 %all-to-all-start.1 = ((bf16[8,128,512]{2,1,0:T(8,128)(2,1)}), bf16[8,128,512]{2,1,0:T(8,128)(2,1)S(1)}, u32[]{:S(2)}, u32[]{:S(2)}) async-start(bf16[8,128,512]{2,1,0:T(8,128)(2,1)} %bitcast.6), calls=%async_computation.1 | async-start | bytes 2097152 | tf_op jit(solution)/shard_map/all_to_all | solution.py:209
  66.7 0.0 copy-done.6
  66.7 1.7 collective-permute-start.2
  68.4 2.9 collective-permute-start.1
  71.3 1.3 collective-permute-start
  72.6 0.0 copy-start.8
  72.6 0.7 copy-done.8
  73.3 87.0 %all-gather.marks_ref = s32[32,1,128]{2,1,0:T(1,128)} all-gather(s32[1,1,128]{2,1,0:T(1,128)S(1)} %bitcast.29), channel_id=1, replica_groups=mesh['zhi'=4,'y'=4,'inner'=8,'outer'=2] {'zhi','y','outer'}, dimensions={0}, use_global_device_ids=true | all-gather | bytes 16896 | tf_op jit(solution)/shard_map/all_gather | solution.py:203
  160.3 0.0 collective-permute-done.2.kv3
  160.3 0.0 collective-permute-done.1.kv2
  160.3 0.0 copy-start.10
  160.3 0.0 collective-permute-done.kv1
  160.3 0.0 copy-start.11
  160.3 0.0 all-to-all-done.1.g_ref
  160.3 0.0 copy-start.3
  160.3 0.7 copy-done.9
  161.1 0.2 copy-done.10
  161.2 0.2 copy-done.11
  161.4 0.3 copy-done.3
  161.8 68.8 %shard_map.84 = (bf16[8,128,512]{2,1,0:T(8,128)(2,1)}, bf16[8,128,512]{2,1,0:T(8,128)(2,1)}, bf16[8,128,256]{2,1,0:T(8,128)(2,1)}, bf16[8,128,256]{2,1,0:T(8,128...) custom-call(s32[1]{0:T(128)} %bitcast.y_ref, s32[32,128]{1,0:T(8,128)} %bitcast.28, ...), custom_call_target="tpu_custom_call" | custom-call | flops 14495514624 | bytes 8388608 | tf_op jit(solution)/shard_map/pallas_call | solution.py:170
  230.5 0.0 collective-permute-start.3
  230.5 0.0 collective-permute-start.4
  230.6 3.2 collective-permute-start.5
  233.8 13.0 %collective-permute-done.3 = bf16[8,128,256]{2,1,0:T(8,128)(2,1)S(1)} collective-permute-done((bf16[8,128,256]{2,1,0:T(8,128)(2,1)}, bf16[8,128,256]{2,1,0:T(8,128)(2,1)S(1)}, u32[]{:S(2)}, u32[]{:S(2)}) %collective-permute-start.3) | collective-permute-done | bytes 524320 | tf_op jit(solution)/shard_map/ppermute | solution.py:212
  246.7 0.0 collective-permute-done.4
  246.8 0.9 collective-permute-done.5
  247.6 1.3 add_convert_fusion
  249.0 0.0 copy-start.4
  249.0 22.2 %all_to_all.30 = bf16[8,128,256]{2,1,0:T(8,128)(2,1)S(1)} all-to-all(bf16[8,128,256]{2,1,0:T(8,128)(2,1)S(1)} %add_convert_fusion), channel_id=1, replica_groups=mesh['zhi'=4,'y'=4,'inner'=8,'outer'=2] {'zhi','outer'}, dimensions={0} | all-to-all | bytes 1048576 | tf_op jit(solution)/shard_map/all_to_all | solution.py:217
  271.1 0.0 copy-done.4
  271.1 28.7 %all_to_all.31 = bf16[8,128,512]{2,1,0:T(8,128)(2,1)S(1)} all-to-all(bf16[8,128,512]{2,1,0:T(8,128)(2,1)S(1)} %copy-done.4), channel_id=1, replica_groups=mesh['zhi'=4,'y'=4,'inner'=8,'outer'=2] {'zhi','outer'}, dimensions={0} | all-to-all | bytes 2097152 | tf_op jit(solution)/shard_map/all_to_all | solution.py:218
  299.8 4.0 %all-to-all-start.4 = ((bf16[8,128,512]{2,1,0:T(8,128)(2,1)}), bf16[8,128,512]{2,1,0:T(8,128)(2,1)S(1)}, u32[]{:S(2)}, u32[]{:S(2)}) async-start(bf16[8,128,512]{2,1,0:T(8,128)(2,1)} %get-tuple-element.11), calls=%async_computation.4 | async-start | bytes 2097152 | tf_op jit(solution)/shard_map/all_to_all | solution.py:219
  303.8 0.1 bitcast_reduce_fusion
  304.0 0.1 copy.36
  304.1 0.8 copy.40
  304.9 0.1 copy.35
  305.0 0.8 copy.39
  305.8 0.7 copy.33
  306.5 1.3 copy.37
  307.8 15.0 %all-to-all-done.4 = bf16[8,128,512]{2,1,0:T(8,128)(2,1)S(1)} async-done(((bf16[8,128,512]{2,1,0:T(8,128)(2,1)}), bf16[8,128,512]{2,1,0:T(8,128)(2,1)S(1)}, u32[]{:S(2)}, u32[]{:S(2)}) %all-to-all-start.4) | async-done | bytes 1048608 | tf_op jit(solution)/shard_map/all_to_all | solution.py:219
  322.8 0.7 copy.34
  323.5 1.3 copy.38
  (4 shorter events, 0.1 us)
Async XLA Ops:
  0.6 1.0 copy-start.7
  1.8 9.3 %copy-start = (bf16[1,128,4096]{2,1,0:T(8,128)(2,1)S(1)}, bf16[1,128,4096]{2,1,0:T(8,128)(2,1)}, u32[]{:S(2)}) copy-start(bf16[1,128,4096]{2,1,0:T(8,128)(2,1)} %param.5) | copy-start | bytes 3145732
  2.7 26.0 %all-to-all-start.2 = ((bf16[8,128,256]{2,1,0:T(8,128)(2,1)}), bf16[8,128,256]{2,1,0:T(8,128)(2,1)S(1)}, u32[]{:S(2)}, u32[]{:S(2)}) async-start(bf16[8,128,256]{2,1,0:T(8,128)(2,1)} %bitcast.8), calls=%async_computation.2 | async-start | bytes 1048576 | tf_op jit(solution)/shard_map/all_to_all | solution.py:204
  28.6 0.8 copy-start.5
  28.6 4.4 %copy-start.1 = (bf16[1,128,4096]{2,1,0:T(8,128)(2,1)S(1)}, bf16[1,128,4096]{2,1,0:T(8,128)(2,1)}, u32[]{:S(2)}) copy-start(bf16[1,128,4096]{2,1,0:T(8,128)(2,1)} %param.8) | copy-start | bytes 3145732
  29.4 32.7 %all-to-all-start = ((bf16[8,128,512]{2,1,0:T(8,128)(2,1)}), bf16[8,128,512]{2,1,0:T(8,128)(2,1)S(1)}, u32[]{:S(2)}, u32[]{:S(2)}) async-start(bf16[8,128,512]{2,1,0:T(8,128)(2,1)} %bitcast.4), calls=%async_computation | async-start | bytes 2097152 | tf_op jit(solution)/shard_map/all_to_all | solution.py:208
  62.2 1.0 copy-start.2
  62.2 4.5 %copy-start.6 = (bf16[8,128,256]{2,1,0:T(8,128)(2,1)S(1)}, bf16[8,128,256]{2,1,0:T(8,128)(2,1)}, u32[]{:S(2)}) copy-start(bf16[8,128,256]{2,1,0:T(8,128)(2,1)} %copy-done.5) | copy-start | bytes 1572868
  63.1 97.2 %all-to-all-start.1 = ((bf16[8,128,512]{2,1,0:T(8,128)(2,1)}), bf16[8,128,512]{2,1,0:T(8,128)(2,1)S(1)}, u32[]{:S(2)}, u32[]{:S(2)}) async-start(bf16[8,128,512]{2,1,0:T(8,128)(2,1)} %bitcast.6), calls=%async_computation.1 | async-start | bytes 2097152 | tf_op jit(solution)/shard_map/all_to_all | solution.py:209
  66.7 93.6 %collective-permute-start.2 = (bf16[8,128,256]{2,1,0:T(8,128)(2,1)S(1)}, bf16[8,128,256]{2,1,0:T(8,128)(2,1)S(1)}, u32[]{:S(2)}, u32[]{:S(2)}) collective-permute-start(bf16[8,128,256]{2,1,0:T(8,128)(2,1)S(1)} %copy-done.6), channel_id=1, source_target_pairs={{0,16},{16,32},{32,48},{48,0},{1,17},{17,33},{33,49},{49,1},{2,18}... | collective-permute-start | bytes 1572872 | tf_op jit(solution)/shard_map/ppermute | solution.py:206
  68.4 91.9 %collective-permute-start.1 = (bf16[8,128,256]{2,1,0:T(8,128)(2,1)S(1)}, bf16[8,128,256]{2,1,0:T(8,128)(2,1)S(1)}, u32[]{:S(2)}, u32[]{:S(2)}) collective-permute-start(bf16[8,128,256]{2,1,0:T(8,128)(2,1)S(1)} %copy-done.6), channel_id=1, source_target_pairs={{0,32},{16,48},{32,0},{48,16},{1,33},{17,49},{33,1},{49,17},{2,34}... | collective-permute-start | bytes 1572872 | tf_op jit(solution)/shard_map/ppermute | solution.py:207
  71.3 89.0 %collective-permute-start = (bf16[8,128,256]{2,1,0:T(8,128)(2,1)S(1)}, bf16[8,128,256]{2,1,0:T(8,128)(2,1)S(1)}, u32[]{:S(2)}, u32[]{:S(2)}) collective-permute-start(bf16[8,128,256]{2,1,0:T(8,128)(2,1)S(1)} %copy-done.6), channel_id=1, source_target_pairs={{0,48},{16,0},{32,16},{48,32},{1,49},{17,1},{33,17},{49,33},{2,50}... | collective-permute-start | bytes 1572872 | tf_op jit(solution)/shard_map/ppermute | solution.py:205
  72.6 0.7 copy-start.8
  160.3 0.8 copy-start.9
  160.3 1.0 copy-start.10
  160.3 1.1 copy-start.11
  160.3 1.4 copy-start.3
  230.5 16.2 %collective-permute-start.3 = (bf16[8,128,256]{2,1,0:T(8,128)(2,1)}, bf16[8,128,256]{2,1,0:T(8,128)(2,1)S(1)}, u32[]{:S(2)}, u32[]{:S(2)}) collective-permute-start(bf16[8,128,256]{2,1,0:T(8,128)(2,1)} %get-tuple-element.13), channel_id=1, source_target_pairs={{0,16},{16,32},{32,48},{48,0},{1,17},{17,33},{33,49},{49,1},{2,18}... | collective-permute-start | bytes 1572872 | tf_op jit(solution)/shard_map/ppermute | solution.py:212
  230.5 16.2 %collective-permute-start.4 = (bf16[8,128,256]{2,1,0:T(8,128)(2,1)}, bf16[8,128,256]{2,1,0:T(8,128)(2,1)S(1)}, u32[]{:S(2)}, u32[]{:S(2)}) collective-permute-start(bf16[8,128,256]{2,1,0:T(8,128)(2,1)} %get-tuple-element.14), channel_id=1, source_target_pairs={{0,32},{16,48},{32,0},{48,16},{1,33},{17,49},{33,1},{49,17},{2,34}... | collective-permute-start | bytes 1572872 | tf_op jit(solution)/shard_map/ppermute | solution.py:213
  230.6 17.1 %collective-permute-start.5 = (bf16[8,128,256]{2,1,0:T(8,128)(2,1)}, bf16[8,128,256]{2,1,0:T(8,128)(2,1)S(1)}, u32[]{:S(2)}, u32[]{:S(2)}) collective-permute-start(bf16[8,128,256]{2,1,0:T(8,128)(2,1)} %get-tuple-element.15), channel_id=1, source_target_pairs={{0,48},{16,0},{32,16},{48,32},{1,49},{17,1},{33,17},{49,33},{2,50}... | collective-permute-start | bytes 1572872 | tf_op jit(solution)/shard_map/ppermute | solution.py:214
  249.0 22.2 %copy-start.4 = (bf16[8,128,512]{2,1,0:T(8,128)(2,1)S(1)}, bf16[8,128,512]{2,1,0:T(8,128)(2,1)}, u32[]{:S(2)}) copy-start(bf16[8,128,512]{2,1,0:T(8,128)(2,1)} %get-tuple-element.10) | copy-start | bytes 3145732
  299.8 23.0 %all-to-all-start.4 = ((bf16[8,128,512]{2,1,0:T(8,128)(2,1)}), bf16[8,128,512]{2,1,0:T(8,128)(2,1)S(1)}, u32[]{:S(2)}, u32[]{:S(2)}) async-start(bf16[8,128,512]{2,1,0:T(8,128)(2,1)} %get-tuple-element.11), calls=%async_computation.4 | async-start | bytes 2097152 | tf_op jit(solution)/shard_map/all_to_all | solution.py:219

commit v2 on v1

v2 whole, which is shorter than its diff:
```python
import math

import jax
import jax.numpy as jnp
from jax import lax
from jax.experimental import pallas as pl
from jax.experimental.pallas import tpu as pltpu
from jax.sharding import Mesh, PartitionSpec as P

H = 32
KVH = 4
DH = 128
ROWS = 128
PADDED = 144
BLOCK = 512
NY = 4
NZ = 8
HEADS = H // NZ
COLS = HEADS * ROWS
TILES = NZ * (NZ + 1) // 2
NEGATIVE = -1e30
SCALE = 1.0 / math.sqrt(DH)
EXP2_SCALE = SCALE * math.log2(math.e)
Z = ("zhi", "outer")
DIMS_NT = (((1,), (1,)), ((), ()))
PLACES = (0, 2, 1, 3, 5, 7, 4, 6)
F32 = jnp.float32
BF16 = jnp.bfloat16


def flip(ref, z):
    return jnp.concatenate(
        [ref[z, :, i * DH : (i + 1) * DH].T for i in range(HEADS)], axis=1
    )


def unflip(ref, z, value):
    for i in range(HEADS):
        ref[z, :, i * DH : (i + 1) * DH] = value[:, i * ROWS : (i + 1) * ROWS].T


def fold(x, op):
    return op(x.reshape(x.shape[0] // 8, 8, x.shape[1]), axis=0)


def set_order(turn, order):
    for b in range(NZ):
        order[b] = jnp.bitwise_xor(turn[0], PLACES[b])


def tile_at(b, j):
    return b * (b + 1) // 2 + j


def forward(
    turn, q_ref, kv0, kv1, kv2, kv3, o_ref, stat_ref, p_hbm,
    order, s_buf, p_buf, k_n, v_t, out_acc, top_acc, sems,
):
    pieces = (kv0, kv1, kv2, kv3)
    set_order(turn, order)

    def row_marks(piece, z):
        row = piece[z, ROWS : ROWS + 16, :].astype(F32)[0:1]
        return row[:, :DH] * 64.0 + row[:, DH:]

    def enter(b):
        z = order[b]
        for rel in range(NY):
            cut = slice(rel * ROWS, (rel + 1) * ROWS)
            k_n[b, cut, :] = pieces[rel][z, :ROWS, :DH]
            v_t[b, :, cut] = pieces[rel][z, :ROWS, DH:].T
        q_t = flip(q_ref, z)
        s = jnp.dot(k_n[b], q_t, preferred_element_type=F32)
        q_marks = jnp.broadcast_to(row_marks(kv0, z), (ROWS, ROWS))
        slot = b % 2
        top = jnp.full((8, COLS), NEGATIVE, F32)
        for rel in range(NY):
            cut = slice(rel * ROWS, (rel + 1) * ROWS)
            k_marks = jnp.broadcast_to(row_marks(pieces[rel], z), (ROWS, ROWS)).T
            seen = k_marks <= q_marks
            part = jnp.concatenate(
                [
                    jnp.where(seen, s[cut, i * ROWS : (i + 1) * ROWS], NEGATIVE)
                    for i in range(HEADS)
                ],
                axis=1,
            )
            s_buf[slot, b, cut, :] = part
            top = jnp.maximum(top, fold(part, jnp.max))
        top_acc[...] = top
        return q_t

    def weigh(b, j, top):
        w = jnp.exp2((s_buf[b % 2, j] - top) * EXP2_SCALE)
        part = fold(w, jnp.sum)
        w = w.astype(BF16)
        tile = tile_at(b, j)
        p_buf[tile] = w
        out_acc[...] += jnp.dot(v_t[j], w, preferred_element_type=F32)
        return part

    def send(b, j):
        tile = tile_at(b, j)
        pltpu.make_async_copy(p_buf.at[tile], p_hbm.at[tile], sems.at[tile]).start()

    def leave(b, top, total):
        inv = 1.0 / jnp.sum(total, axis=0, keepdims=True)
        unflip(o_ref, order[b], (out_acc[...] * inv).astype(BF16))
        stat_ref[b] = inv

    enter(0)

    def group(b, carry):
        top = jnp.max(top_acc[...], axis=0, keepdims=True)
        q_next = enter(b + 1)
        out_acc[...] = jnp.zeros((DH, COLS), F32)

        def step(j, total):
            s = jnp.dot(k_n[j], q_next, preferred_element_type=F32)
            s_buf[(b + 1) % 2, j] = s
            top_acc[...] = jnp.maximum(top_acc[...], fold(s, jnp.max))
            total = total + weigh(b, j, top)
            send(b, j)
            return total

        total = lax.fori_loop(0, b + 1, step, jnp.zeros((8, COLS), F32))
        leave(b, top, total)
        return carry

    lax.fori_loop(0, NZ - 1, group, 0)
    last = NZ - 1
    top = jnp.max(top_acc[...], axis=0, keepdims=True)
    out_acc[...] = jnp.zeros((DH, COLS), F32)

    def step(j, total):
        total = total + weigh(last, j, top)
        send(last, j)
        return total

    total = lax.fori_loop(0, NZ, step, jnp.zeros((8, COLS), F32))
    leave(last, top, total)

    def wait(tile, carry):
        pltpu.make_async_copy(p_buf.at[tile], p_hbm.at[tile], sems.at[tile]).wait()
        return carry

    lax.fori_loop(0, TILES, wait, 0)


def backward(
    turn, q_ref, g_ref, o_ref, stat_ref, kv0, kv1, kv2, kv3, p_hbm,
    dq_ref, out0, out1, out2, out3,
    order, p_buf, k_t, v_n, acc, dq_acc, sems,
):
    pieces = (kv0, kv1, kv2, kv3)
    outs = (out0, out1, out2, out3)
    set_order(turn, order)

    def fetch(tile, carry):
        pltpu.make_async_copy(p_hbm.at[tile], p_buf.at[tile], sems.at[tile]).start()
        return carry

    lax.fori_loop(0, TILES, fetch, 0)

    def group(b, carry):
        z = order[b]
        for rel in range(NY):
            cut = slice(rel * ROWS, (rel + 1) * ROWS)
            k_t[b, :, cut] = pieces[rel][z, :ROWS, :DH].T
            v_n[b, cut, :] = pieces[rel][z, :ROWS, DH:]
        acc[b] = jnp.zeros((BLOCK, 2 * DH), F32)
        dq_acc[...] = jnp.zeros((DH, COLS), F32)
        q_t = flip(q_ref, z)
        g_t = flip(g_ref, z)
        o_t = flip(o_ref, z)
        inv = stat_ref[b]
        delta = jnp.sum(g_t.astype(F32) * o_t.astype(F32), axis=0, keepdims=True)
        q_n = (q_t.astype(F32) * inv).astype(BF16)
        g_n = (g_t.astype(F32) * inv).astype(BF16)

        def step(j, carry):
            tile = tile_at(b, j)
            pltpu.make_async_copy(p_hbm.at[tile], p_buf.at[tile], sems.at[tile]).wait()
            w = p_buf[tile]
            dp = jnp.dot(v_n[j], g_t, preferred_element_type=F32)
            ds = (w.astype(F32) * (dp - delta)).astype(BF16)
            acc[j, :, DH:] += lax.dot_general(w, g_n, DIMS_NT, preferred_element_type=F32)
            acc[j, :, :DH] += lax.dot_general(ds, q_n, DIMS_NT, preferred_element_type=F32)
            dq_acc[...] += jnp.dot(k_t[j], ds, preferred_element_type=F32)
            return carry

        lax.fori_loop(0, b + 1, step, 0)
        unflip(dq_ref, z, (dq_acc[...] * (inv * SCALE)).astype(BF16))
        return carry

    lax.fori_loop(0, NZ, group, 0)

    def finish(b, carry):
        z = order[b]
        for rel in range(NY):
            cut = slice(rel * ROWS, (rel + 1) * ROWS)
            outs[rel][z, :, :DH] = (acc[b, cut, :DH] * SCALE).astype(BF16)
            outs[rel][z, :, DH:] = acc[b, cut, DH:].astype(BF16)
        return carry

    lax.fori_loop(0, NZ, finish, 0)


VMEM = pl.BlockSpec(memory_space=pltpu.VMEM)
SMEM = pl.BlockSpec(memory_space=pltpu.SMEM)
ANY = pl.BlockSpec(memory_space=pl.ANY)
WIDE = jax.ShapeDtypeStruct((NZ, ROWS, COLS), BF16)
NARROW = jax.ShapeDtypeStruct((NZ, ROWS, 2 * DH), BF16)
WEIGHTS = jax.ShapeDtypeStruct((TILES, BLOCK, COLS), BF16)
STATS = jax.ShapeDtypeStruct((NZ, 1, COLS), F32)
PARAMS = pltpu.CompilerParams(vmem_limit_bytes=56 * 1024 * 1024)


def cost(matmuls, exps):
    return pl.CostEstimate(
        flops=TILES * matmuls * 2 * BLOCK * COLS * DH * 2,
        bytes_accessed=24 * 1024 * 1024,
        transcendentals=exps * TILES * BLOCK * COLS,
    )


def run_forward(turn, q, pieces):
    return pl.pallas_call(
        forward,
        name="forward",
        out_shape=(WIDE, STATS, WEIGHTS),
        in_specs=[SMEM] + [VMEM] * 5,
        out_specs=[VMEM, VMEM, ANY],
        scratch_shapes=[
            pltpu.SMEM((NZ,), jnp.int32),
            pltpu.VMEM((2, NZ, BLOCK, COLS), F32),
            pltpu.VMEM((TILES, BLOCK, COLS), BF16),
            pltpu.VMEM((NZ, BLOCK, DH), BF16),
            pltpu.VMEM((NZ, DH, BLOCK), BF16),
            pltpu.VMEM((DH, COLS), F32),
            pltpu.VMEM((8, COLS), F32),
            pltpu.SemaphoreType.DMA((TILES,)),
        ],
        compiler_params=PARAMS,
        cost_estimate=cost(2, 1),
    )(turn, q, *pieces)


def run_backward(turn, q, g, o, stat, pieces, weights):
    return pl.pallas_call(
        backward,
        name="backward",
        out_shape=(WIDE, NARROW, NARROW, NARROW, NARROW),
        in_specs=[SMEM] + [VMEM] * 8 + [ANY],
        out_specs=[VMEM] * 5,
        scratch_shapes=[
            pltpu.SMEM((NZ,), jnp.int32),
            pltpu.VMEM((TILES, BLOCK, COLS), BF16),
            pltpu.VMEM((NZ, DH, BLOCK), BF16),
            pltpu.VMEM((NZ, BLOCK, DH), BF16),
            pltpu.VMEM((NZ, BLOCK, 2 * DH), F32),
            pltpu.VMEM((DH, COLS), F32),
            pltpu.SemaphoreType.DMA((TILES,)),
        ],
        compiler_params=PARAMS,
        cost_estimate=cost(4, 0),
    )(turn, q, g, o, stat, *pieces, weights)


def ring(step):
    return [(i, (i + step) % NY) for i in range(NY)]


def exchange(x):
    return lax.all_to_all(x, Z, split_axis=0, concat_axis=0, tiled=True)


def spread(x):
    return exchange(x[0].reshape(ROWS, NZ, COLS).transpose(1, 0, 2))


def collect(x):
    return exchange(x).transpose(1, 0, 2).reshape(1, ROWS, H * DH)


def shards(queries, keys, values, grad_out, positions):
    kv = jnp.concatenate(
        [keys[0].reshape(ROWS, KVH, DH), values[0].reshape(ROWS, KVH, DH)], axis=2
    ).transpose(1, 0, 2)
    marks = jnp.concatenate([positions[0] // 64, positions[0] % 64]).astype(BF16)
    marks = jnp.broadcast_to(marks, (KVH, PADDED - ROWS, 2 * DH))
    kv = jnp.concatenate([kv, marks], axis=1)
    kv = exchange(jnp.repeat(kv, NZ // KVH, axis=0))
    own = positions[0, 0] // (2 * BLOCK)
    own = jnp.where(lax.axis_index("zhi") < NZ // 4, own, NZ // 2 - 1 - own)
    turn = jnp.bitwise_xor(own, lax.axis_index("outer")).astype(jnp.int32).reshape(1)
    pieces = (
        kv,
        lax.ppermute(kv, "y", ring(-1)),
        lax.ppermute(kv, "y", ring(2)),
        lax.ppermute(kv, "y", ring(1)),
    )
    q = spread(queries)
    out, stat, weights = run_forward(turn, q, pieces)
    g = spread(grad_out)
    dq, d0, d1, d2, d3 = run_backward(turn, q, g, out, stat, pieces, weights)
    out = collect(out)
    d1 = lax.ppermute(d1, "y", ring(1))
    d2 = lax.ppermute(d2, "y", ring(2))
    d3 = lax.ppermute(d3, "y", ring(-1))
    dq = collect(dq)
    wide = [d.astype(F32) for d in (d0, d1, d2, d3)]
    dkv = exchange(((wide[0] + wide[1]) + (wide[2] + wide[3])).astype(BF16))
    dkv = dkv.reshape(KVH, NZ // KVH, ROWS, 2 * DH).astype(F32).sum(axis=1)
    dkv = dkv.astype(BF16).transpose(1, 0, 2)
    dk = dkv[:, :, :DH].reshape(1, ROWS, KVH * DH)
    dv = dkv[:, :, DH:].reshape(1, ROWS, KVH * DH)
    return out, dq, dk, dv


def solution(mesh):
    devices = mesh.devices.reshape(NZ // 2, NY, mesh.shape["inner"], mesh.shape["outer"])
    fine = Mesh(devices, ("zhi", "y", "inner", "outer"))
    rows = P("inner", ("zhi", "y", "outer"), None)
    return jax.shard_map(
        shards,
        mesh=fine,
        in_specs=(rows, rows, rows, rows, P("inner", ("zhi", "y", "outer"))),
        out_specs=(rows, rows, rows, rows),
        check_vma=False,
    )
```

time: 325 us -> 273 us (0.84)
  blocking collectives: 138 us -> 53.1 us
  waiting for transfers between devices: 71.6 us -> 107 us
  Pallas kernels: 68.8 us -> 59 us
    all_gather x1 -> x0, blocking collectives: 87 us -> none  [shards(): lax.all_gather(positions[0], ('zhi', 'y', 'outer'), axis=0, tiled=False)]
    ppermute x3, waiting for transfers between devices: 0.01 us -> 22 us  [the longest x1 13.9 us: shards(): lax.ppermute(kv, 'y', ring(2))]
    ppermute x1, waiting for transfers between devices: 0.01 us -> 12.4 us  [shards(): d2 = lax.ppermute(d2, 'y', ring(2))]
    pallas_call x1 -> x2, Pallas kernels: 68.8 us -> 59 us  [the longest x1 31.2 us: run_backward(): pl.pallas_call(backward, name='backward', out_shape=(WIDE, NARROW, NARROW...]
    all_to_all x4, waiting for transfers between devices: 57.7 us -> 63.2 us  [exchange(): return lax.all_to_all(x, Z, split_axis=0, concat_axis=0, tiled=True)]
    ppermute x1, waiting for transfers between devices: 13 us -> 9.26 us  [shards(): d1 = lax.ppermute(d1, 'y', ring(1))]
    unnamed x30 -> x14, local copies, waits for them, and re-layouts: 9.37 us -> 8.38 us
  transfers between devices with their start and end apart: 10 -> 10, of which waited for: 5 -> 7; matrix products, arithmetic and copies ran while one was open for 2% -> 4% of each run, Pallas kernels for 0% -> 10%
where the time goes in v2:
time: 273 us; the launch traced here: 271 us
  waiting for transfers between devices  107 us (39%)
  Pallas kernels  59 us (22%)
  blocking collectives  53.1 us (19%)
  starting transfers between devices  30.3 us (11%)
  local copies, waits for them, and re-layouts  15.4 us (6%)
  between operations  3.42 us (1%)
    all_to_all x4, waiting for transfers between devices, exchange(): return lax.all_to_all(x, Z, split_axis=0, concat_axis=0, tiled=True)  63.2 us
    all_to_all x2, blocking collectives, exchange(): return lax.all_to_all(x, Z, split_axis=0, concat_axis=0, tiled=True)  53.1 us
    pallas_call x1, Pallas kernels, run_backward(): pl.pallas_call(backward, name='backward', out_shape=(WIDE, NARROW, NARROW...  31.2 us
    pallas_call x1, Pallas kernels, run_forward(): pl.pallas_call(forward, name='forward', out_shape=(WIDE, STATS, WEIGHTS),...  27.9 us
    all_to_all x4, starting transfers between devices, exchange(): return lax.all_to_all(x, Z, split_axis=0, concat_axis=0, tiled=True)  19.1 us
    ppermute x1, waiting for transfers between devices, shards(): lax.ppermute(kv, 'y', ring(2))  13.9 us
    ppermute x1, waiting for transfers between devices, shards(): d2 = lax.ppermute(d2, 'y', ring(2))  12.4 us
    ppermute x1, waiting for transfers between devices, shards(): d1 = lax.ppermute(d1, 'y', ring(1))  9.26 us
  transfers between devices with their start and end apart: 10, of which 7 were waited for; matrix products, arithmetic and copies ran while one was open for 4% of the time, Pallas kernels for 10%

profile of v2, /device:TPU:2, one launch (start us, length us, event | category | flops | bytes accessed | tf_op | source)
XLA Modules:
  0.0 270.6 jit_solution(13381121865245343504)
XLA Ops:
  0.6 0.7 fusion.1
  1.3 0.9 reshape_squeeze.13
  2.2 0.9 reshape_squeeze.14
  3.2 0.1 maximum_bitcast_fusion
  3.4 0.2 pad_maximum_fusion
  3.6 0.9 broadcast_in_dim.7
  4.5 8.5 %all-to-all-start.1 = ((bf16[8,144,256]{2,1,0:T(8,128)(2,1)}), bf16[8,144,256]{2,1,0:T(8,128)(2,1)S(1)}, u32[]{:S(2)}, u32[]{:S(2)}) async-start(bf16[8,144,256]{2,1,0:T(8,128)(2,1)} %bitcast.6), calls=%async_computation.1 | async-start | bytes 1179648 | tf_op jit(solution)/shard_map/all_to_all | solution.py:275
  12.9 1.6 copy.28
  14.5 1.3 copy.29
  15.9 16.0 %all-to-all-done.1.kv0 = bf16[8,144,256]{2,1,0:T(8,128)(2,1)S(1)} async-done(((bf16[8,144,256]{2,1,0:T(8,128)(2,1)}), bf16[8,144,256]{2,1,0:T(8,128)(2,1)S(1)}, u32[]{:S(2)}, u32[]{:S(2)}) %all-to-all-start.1) | async-done | bytes 589856 | tf_op jit(solution)/shard_map/all_to_all | solution.py:275
  31.8 0.0 copy-start.2
  31.8 3.6 %all-to-all-start = ((bf16[8,128,512]{2,1,0:T(8,128)(2,1)}), bf16[8,128,512]{2,1,0:T(8,128)(2,1)S(1)}, u32[]{:S(2)}, u32[]{:S(2)}) async-start(bf16[8,128,512]{2,1,0:T(8,128)(2,1)} %bitcast.3), calls=%async_computation | async-start | bytes 2097152 | tf_op jit(solution)/shard_map/all_to_all | solution.py:275
  35.4 1.6 copy.32
  37.0 1.3 copy.33
  38.3 26.2 %all-to-all-done.q_ref = bf16[8,128,512]{2,1,0:T(8,128)(2,1)S(1)} async-done(((bf16[8,128,512]{2,1,0:T(8,128)(2,1)}), bf16[8,128,512]{2,1,0:T(8,128)(2,1)S(1)}, u32[]{:S(2)}, u32[]{:S(2)}) %all-to-all-start) | async-done | bytes 1048608 | tf_op jit(solution)/shard_map/all_to_all | solution.py:275
  64.5 0.0 copy-start
  64.5 3.6 %all-to-all-start.3 = ((bf16[8,128,512]{2,1,0:T(8,128)(2,1)}), bf16[8,128,512]{2,1,0:T(8,128)(2,1)S(1)}, u32[]{:S(2)}, u32[]{:S(2)}) async-start(bf16[8,128,512]{2,1,0:T(8,128)(2,1)} %bitcast.10), calls=%async_computation.3 | async-start | bytes 2097152 | tf_op jit(solution)/shard_map/all_to_all | solution.py:275
  68.1 1.7 collective-permute-start.2
  69.8 2.9 %collective-permute-start.1 = (bf16[8,144,256]{2,1,0:T(8,128)(2,1)S(1)}, bf16[8,144,256]{2,1,0:T(8,128)(2,1)}, u32[]{:S(2)}, u32[]{:S(2)}) collective-permute-start(bf16[8,144,256]{2,1,0:T(8,128)(2,1)S(1)} %all-to-all-done.1.kv0), channel_id=1, source_target_pairs={{0,32},{16,48},{32,0},{48,16},{1,33},{17,49},{33,1},{49,17},{2,34}... | collective-permute-start | bytes 1769480 | tf_op jit(solution)/shard_map/ppermute | solution.py:300
  72.7 1.3 collective-permute-start
  76.6 8.1 %collective-permute-done.2.kv3 = bf16[8,144,256]{2,1,0:T(8,128)(2,1)S(1)} collective-permute-done((bf16[8,144,256]{2,1,0:T(8,128)(2,1)S(1)}, bf16[8,144,256]{2,1,0:T(8,128)(2,1)S(1)}, u32[]{:S(2)}, u32[]{:S(2)}) %collective-permute-start.2) | collective-permute-done | bytes 589856 | tf_op jit(solution)/shard_map/ppermute | solution.py:301
  84.7 0.0 copy-start.3
  84.7 13.9 %collective-permute-done.1.kv2 = bf16[8,144,256]{2,1,0:T(8,128)(2,1)} collective-permute-done((bf16[8,144,256]{2,1,0:T(8,128)(2,1)S(1)}, bf16[8,144,256]{2,1,0:T(8,128)(2,1)}, u32[]{:S(2)}, u32[]{:S(2)}) %collective-permute-start.1) | collective-permute-done | bytes 589856 | tf_op jit(solution)/shard_map/ppermute | solution.py:300
  98.6 0.0 collective-permute-done.kv1
  98.6 0.0 copy-done.2
  98.6 0.0 copy-done
  98.7 0.0 copy-done.3
  98.7 27.9 %forward.1 = (bf16[8,128,512]{2,1,0:T(8,128)(2,1)}, f32[8,1,512]{2,1,0:T(1,128)}, bf16[36,512,512]{2,1,0:T(8,128)(2,1)}) custom-call(s32[1]{0:T(128)} %bitcast.1.turn, bf16[8,128,512]{2,1,0:T(8,128)(2,1)} %copy-done, bf16[8,144,256]{2,1,0:T(8,128)(2,1)} %copy-done.2, bf16[8,144,256]{2,1,0:T(8,128)(2,1)} %collective-permute-done.kv1, ...), custom_call_target="tpu_custom_call" | custom-call | flops 9663676416 | bytes 25165824 | tf_op jit(solution)/shard_map/forward/pallas_call | solution.py:228
  126.6 0.0 all-to-all-done.3.g_ref
  126.6 0.0 copy-start.1
  126.6 1.0 copy-done.1
  127.5 31.2 %backward.1 = (bf16[8,128,512]{2,1,0:T(8,128)(2,1)}, bf16[8,128,256]{2,1,0:T(8,128)(2,1)}, bf16[8,128,256]{2,1,0:T(8,128)(2,1)}, bf16[8,128,256]{2,1,0:T(8,128)(2,1)}, bf16[8,128,256]{2,1,0:T(8,128)(2,1)}) custom-call(s32[1]{0:T(128)} %bitcast.1.turn, bf16[8,128,512]{2,1,0:T(8,128)(2,1)} %copy-done, bf16[8,128,512]{2,1,0:T(8,128)(2,1)} %copy-done.1, ...), custom_call_target="tpu_custom_call" | custom-call | flops 19327352832 | bytes 25165824 | tf_op jit(solution)/shard_map/backward/pallas_call | solution.py:250
  158.7 1.3 collective-permute-start.3
  160.0 2.4 collective-permute-start.4
  162.4 1.6 collective-permute-start.5
  164.0 9.3 %collective-permute-done.3 = bf16[8,128,256]{2,1,0:T(8,128)(2,1)S(1)} collective-permute-done((bf16[8,128,256]{2,1,0:T(8,128)(2,1)}, bf16[8,128,256]{2,1,0:T(8,128)(2,1)S(1)}, u32[]{:S(2)}, u32[]{:S(2)}) %collective-permute-start.3) | collective-permute-done | bytes 524320 | tf_op jit(solution)/shard_map/ppermute | solution.py:308
  173.2 12.4 %collective-permute-done.4 = bf16[8,128,256]{2,1,0:T(8,128)(2,1)S(1)} collective-permute-done((bf16[8,128,256]{2,1,0:T(8,128)(2,1)}, bf16[8,128,256]{2,1,0:T(8,128)(2,1)S(1)}, u32[]{:S(2)}, u32[]{:S(2)}) %collective-permute-start.4) | collective-permute-done | bytes 524320 | tf_op jit(solution)/shard_map/ppermute | solution.py:309
  185.7 0.0 collective-permute-done.5
  185.7 1.3 add_convert_fusion
  187.0 23.3 %all_to_all.30 = bf16[8,128,256]{2,1,0:T(8,128)(2,1)S(1)} all-to-all(bf16[8,128,256]{2,1,0:T(8,128)(2,1)S(1)} %add_convert_fusion), channel_id=1, replica_groups=mesh['zhi'=4,'y'=4,'inner'=8,'outer'=2] {'zhi','outer'}, dimensions={0} | all-to-all | bytes 1048576 | tf_op jit(solution)/shard_map/all_to_all | solution.py:275
  210.3 29.8 %all_to_all.31 = bf16[8,128,512]{2,1,0:T(8,128)(2,1)S(1)} all-to-all(bf16[8,128,512]{2,1,0:T(8,128)(2,1)} %get-tuple-element.15), channel_id=1, replica_groups=mesh['zhi'=4,'y'=4,'inner'=8,'outer'=2] {'zhi','outer'}, dimensions={0} | all-to-all | bytes 2097152 | tf_op jit(solution)/shard_map/all_to_all | solution.py:275
  240.1 3.6 %all-to-all-start.2 = ((bf16[8,128,512]{2,1,0:T(8,128)(2,1)}), bf16[8,128,512]{2,1,0:T(8,128)(2,1)S(1)}, u32[]{:S(2)}, u32[]{:S(2)}) async-start(bf16[8,128,512]{2,1,0:T(8,128)(2,1)} %get-tuple-element.12.o_ref), calls=%async_computation.2 | async-start | bytes 2097152 | tf_op jit(solution)/shard_map/all_to_all | solution.py:275
  243.7 0.1 bitcast_reduce_fusion
  243.8 0.1 copy.36
  244.0 0.8 copy.40
  244.7 0.1 copy.35
  244.9 0.8 copy.39
  245.6 0.7 copy.34
  246.3 1.3 copy.38
  247.6 21.0 %all-to-all-done.2 = bf16[8,128,512]{2,1,0:T(8,128)(2,1)S(1)} async-done(((bf16[8,128,512]{2,1,0:T(8,128)(2,1)}), bf16[8,128,512]{2,1,0:T(8,128)(2,1)S(1)}, u32[]{:S(2)}, u32[]{:S(2)}) %all-to-all-start.2) | async-done | bytes 1048608 | tf_op jit(solution)/shard_map/all_to_all | solution.py:275
  268.6 0.7 copy.31
  269.3 1.3 copy.37
  (4 shorter events, 0.1 us)
Async XLA Ops:
  4.5 27.4 %all-to-all-start.1 = ((bf16[8,144,256]{2,1,0:T(8,128)(2,1)}), bf16[8,144,256]{2,1,0:T(8,128)(2,1)S(1)}, u32[]{:S(2)}, u32[]{:S(2)}) async-start(bf16[8,144,256]{2,1,0:T(8,128)(2,1)} %bitcast.6), calls=%async_computation.1 | async-start | bytes 1179648 | tf_op jit(solution)/shard_map/all_to_all | solution.py:275
  31.8 66.8 %copy-start.2 = (bf16[8,144,256]{2,1,0:T(8,128)(2,1)}, bf16[8,144,256]{2,1,0:T(8,128)(2,1)S(1)}, u32[]{:S(2)}) copy-start(bf16[8,144,256]{2,1,0:T(8,128)(2,1)S(1)} %all-to-all-done.1.kv0) | copy-start | bytes 1769476
  31.8 32.7 %all-to-all-start = ((bf16[8,128,512]{2,1,0:T(8,128)(2,1)}), bf16[8,128,512]{2,1,0:T(8,128)(2,1)S(1)}, u32[]{:S(2)}, u32[]{:S(2)}) async-start(bf16[8,128,512]{2,1,0:T(8,128)(2,1)} %bitcast.3), calls=%async_computation | async-start | bytes 2097152 | tf_op jit(solution)/shard_map/all_to_all | solution.py:275
  64.5 34.1 %copy-start = (bf16[8,128,512]{2,1,0:T(8,128)(2,1)}, bf16[8,128,512]{2,1,0:T(8,128)(2,1)S(1)}, u32[]{:S(2)}) copy-start(bf16[8,128,512]{2,1,0:T(8,128)(2,1)S(1)} %all-to-all-done.q_ref) | copy-start | bytes 3145732
  64.5 62.0 %all-to-all-start.3 = ((bf16[8,128,512]{2,1,0:T(8,128)(2,1)}), bf16[8,128,512]{2,1,0:T(8,128)(2,1)S(1)}, u32[]{:S(2)}, u32[]{:S(2)}) async-start(bf16[8,128,512]{2,1,0:T(8,128)(2,1)} %bitcast.10), calls=%async_computation.3 | async-start | bytes 2097152 | tf_op jit(solution)/shard_map/all_to_all | solution.py:275
  68.1 16.6 %collective-permute-start.2 = (bf16[8,144,256]{2,1,0:T(8,128)(2,1)S(1)}, bf16[8,144,256]{2,1,0:T(8,128)(2,1)S(1)}, u32[]{:S(2)}, u32[]{:S(2)}) collective-permute-start(bf16[8,144,256]{2,1,0:T(8,128)(2,1)S(1)} %all-to-all-done.1.kv0), channel_id=1, source_target_pairs={{0,16},{16,32},{32,48},{48,0},{1,17},{17,33},{33,49},{49,1},{2,18}... | collective-permute-start | bytes 1769480 | tf_op jit(solution)/shard_map/ppermute | solution.py:301
  69.8 28.9 %collective-permute-start.1 = (bf16[8,144,256]{2,1,0:T(8,128)(2,1)S(1)}, bf16[8,144,256]{2,1,0:T(8,128)(2,1)}, u32[]{:S(2)}, u32[]{:S(2)}) collective-permute-start(bf16[8,144,256]{2,1,0:T(8,128)(2,1)S(1)} %all-to-all-done.1.kv0), channel_id=1, source_target_pairs={{0,32},{16,48},{32,0},{48,16},{1,33},{17,49},{33,1},{49,17},{2,34}... | collective-permute-start | bytes 1769480 | tf_op jit(solution)/shard_map/ppermute | solution.py:300
  72.7 26.0 %collective-permute-start = (bf16[8,144,256]{2,1,0:T(8,128)(2,1)S(1)}, bf16[8,144,256]{2,1,0:T(8,128)(2,1)}, u32[]{:S(2)}, u32[]{:S(2)}) collective-permute-start(bf16[8,144,256]{2,1,0:T(8,128)(2,1)S(1)} %all-to-all-done.1.kv0), channel_id=1, source_target_pairs={{0,48},{16,0},{32,16},{48,32},{1,49},{17,1},{33,17},{49,33},{2,50}... | collective-permute-start | bytes 1769480 | tf_op jit(solution)/shard_map/ppermute | solution.py:299
  84.7 13.9 %copy-start.3 = (bf16[8,144,256]{2,1,0:T(8,128)(2,1)}, bf16[8,144,256]{2,1,0:T(8,128)(2,1)S(1)}, u32[]{:S(2)}) copy-start(bf16[8,144,256]{2,1,0:T(8,128)(2,1)S(1)} %collective-permute-done.2.kv3) | copy-start | bytes 1769476
  126.6 1.0 copy-start.1
  158.7 14.5 %collective-permute-start.3 = (bf16[8,128,256]{2,1,0:T(8,128)(2,1)}, bf16[8,128,256]{2,1,0:T(8,128)(2,1)S(1)}, u32[]{:S(2)}, u32[]{:S(2)}) collective-permute-start(bf16[8,128,256]{2,1,0:T(8,128)(2,1)} %get-tuple-element.17), channel_id=1, source_target_pairs={{0,16},{16,32},{32,48},{48,0},{1,17},{17,33},{33,49},{49,1},{2,18}... | collective-permute-start | bytes 1572872 | tf_op jit(solution)/shard_map/ppermute | solution.py:308
  160.0 25.6 %collective-permute-start.4 = (bf16[8,128,256]{2,1,0:T(8,128)(2,1)}, bf16[8,128,256]{2,1,0:T(8,128)(2,1)S(1)}, u32[]{:S(2)}, u32[]{:S(2)}) collective-permute-start(bf16[8,128,256]{2,1,0:T(8,128)(2,1)} %get-tuple-element.18), channel_id=1, source_target_pairs={{0,32},{16,48},{32,0},{48,16},{1,33},{17,49},{33,1},{49,17},{2,34}... | collective-permute-start | bytes 1572872 | tf_op jit(solution)/shard_map/ppermute | solution.py:309
  162.4 23.3 %collective-permute-start.5 = (bf16[8,128,256]{2,1,0:T(8,128)(2,1)}, bf16[8,128,256]{2,1,0:T(8,128)(2,1)S(1)}, u32[]{:S(2)}, u32[]{:S(2)}) collective-permute-start(bf16[8,128,256]{2,1,0:T(8,128)(2,1)} %get-tuple-element.19), channel_id=1, source_target_pairs={{0,48},{16,0},{32,16},{48,32},{1,49},{17,1},{33,17},{49,33},{2,50}... | collective-permute-start | bytes 1572872 | tf_op jit(solution)/shard_map/ppermute | solution.py:310
  240.1 28.5 %all-to-all-start.2 = ((bf16[8,128,512]{2,1,0:T(8,128)(2,1)}), bf16[8,128,512]{2,1,0:T(8,128)(2,1)S(1)}, u32[]{:S(2)}, u32[]{:S(2)}) async-start(bf16[8,128,512]{2,1,0:T(8,128)(2,1)} %get-tuple-element.12.o_ref), calls=%async_computation.2 | async-start | bytes 2097152 | tf_op jit(solution)/shard_map/all_to_all | solution.py:275

commit v3 on v2

--- a/solution.py
+++ b/solution.py
@@ -275,12 +275,37 @@
     return lax.all_to_all(x, Z, split_axis=0, concat_axis=0, tiled=True)
 
 
-def spread(x):
-    return exchange(x[0].reshape(ROWS, NZ, COLS).transpose(1, 0, 2))
-
-
-def collect(x):
-    return exchange(x).transpose(1, 0, 2).reshape(1, ROWS, H * DH)
+def after(x, *earlier):
+    return lax.optimization_barrier((x, *earlier))[0]
+
+
+def gather_y(kv):
+    half = kv.shape[0] // 2
+    up = lax.ppermute(kv, "y", ring(-1))
+    down = lax.ppermute(kv, "y", ring(1))
+    far = jnp.concatenate(
+        [lax.ppermute(down[:half], "y", ring(1)), lax.ppermute(up[half:], "y", ring(-1))]
+    )
+    return kv, up, far, down
+
+
+def add(x, y):
+    return (x.astype(F32) + y.astype(F32)).astype(BF16)
+
+
+def scatter_y(own, up, far, down):
+    half = own.shape[0] // 2
+    from_down = lax.ppermute(far[:half], "y", ring(1))
+    from_up = lax.ppermute(far[half:], "y", ring(-1))
+    up = jnp.concatenate([add(up[:half], from_down), up[half:]])
+    down = jnp.concatenate([down[:half], add(down[half:], from_up)])
+    up = lax.ppermute(up, "y", ring(1))
+    down = lax.ppermute(down, "y", ring(-1))
+    return (own.astype(F32) + (up.astype(F32) + down.astype(F32))).astype(BF16)
+
+
+def chunks(x):
+    return x[0].reshape(ROWS, NZ, COLS).transpose(1, 0, 2)
 
 
 def shards(queries, keys, values, grad_out, positions):
@@ -294,27 +319,20 @@
     own = positions[0, 0] // (2 * BLOCK)
     own = jnp.where(lax.axis_index("zhi") < NZ // 4, own, NZ // 2 - 1 - own)
     turn = jnp.bitwise_xor(own, lax.axis_index("outer")).astype(jnp.int32).reshape(1)
-    pieces = (
-        kv,
-        lax.ppermute(kv, "y", ring(-1)),
-        lax.ppermute(kv, "y", ring(2)),
-        lax.ppermute(kv, "y", ring(1)),
-    )
-    q = spread(queries)
+    pieces = gather_y(kv)
+    q = exchange(after(chunks(queries), kv))
+    g = exchange(after(chunks(grad_out), q, *pieces))
     out, stat, weights = run_forward(turn, q, pieces)
-    g = spread(grad_out)
     dq, d0, d1, d2, d3 = run_backward(turn, q, g, out, stat, pieces, weights)
-    out = collect(out)
-    d1 = lax.ppermute(d1, "y", ring(1))
-    d2 = lax.ppermute(d2, "y", ring(2))
-    d3 = lax.ppermute(d3, "y", ring(-1))
-    dq = collect(dq)
-    wide = [d.astype(F32) for d in (d0, d1, d2, d3)]
-    dkv = exchange(((wide[0] + wide[1]) + (wide[2] + wide[3])).astype(BF16))
+    out = exchange(out)
+    dq = exchange(after(dq, out))
+    dkv = exchange(after(scatter_y(d0, d1, d2, d3), dq))
     dkv = dkv.reshape(KVH, NZ // KVH, ROWS, 2 * DH).astype(F32).sum(axis=1)
     dkv = dkv.astype(BF16).transpose(1, 0, 2)
     dk = dkv[:, :, :DH].reshape(1, ROWS, KVH * DH)
     dv = dkv[:, :, DH:].reshape(1, ROWS, KVH * DH)
+    out = out.transpose(1, 0, 2).reshape(1, ROWS, H * DH)
+    dq = dq.transpose(1, 0, 2).reshape(1, ROWS, H * DH)
     return out, dq, dk, dv
 
 

time: 273 us -> 197 us (0.72)
  blocking collectives: 53.1 us -> 0 us
  waiting for transfers between devices: 107 us -> 56.1 us
  starting transfers between devices: 30.3 us -> 53.9 us
  local copies, waits for them, and re-layouts: 15.4 us -> 19.4 us
  other arithmetic: 2.4 us -> 6.35 us
    all_to_all x2 -> x0, blocking collectives: 53.1 us -> none  [exchange(): return lax.all_to_all(x, Z, split_axis=0, concat_axis=0, tiled=True)]
    all_to_all x4 -> x6, waiting for transfers between devices: 63.2 us -> 27 us  [exchange(): return lax.all_to_all(x, Z, split_axis=0, concat_axis=0, tiled=True)]
    all_to_all x4 -> x6, starting transfers between devices: 19.1 us -> 39.6 us  [exchange(): return lax.all_to_all(x, Z, split_axis=0, concat_axis=0, tiled=True)]
    ppermute x6 -> x8, waiting for transfers between devices: 43.7 us -> 29.1 us  [the longest x1 13.3 us: gather_y(): down = lax.ppermute(kv, 'y', ring(1))]
    slice x0 -> x5, local copies, waits for them, and re-layouts: none -> 3.79 us  [the longest x1 1.06 us: scatter_y(): from_down = lax.ppermute(far[:half], 'y', ring(1))]
    ppermute x6 -> x8, starting transfers between devices: 11.2 us -> 14.3 us  [the longest x1 3.77 us: scatter_y(): down = lax.ppermute(down, 'y', ring(-1))]
    convert_element_type x1 -> x3, other arithmetic: 1.32 us -> 4.07 us  [the longest x1 2.05 us: scatter_y(): return (own.astype(F32) + (up.astype(F32) + down.astype(F32))).astype(BF16)]
    unnamed x14 -> x21, local copies, waits for them, and re-layouts: 8.38 us -> 7.65 us
  transfers between devices with their start and end apart: 10 -> 14, of which waited for: 7 -> 10; matrix products, arithmetic and copies ran while one was open for 4% -> 10% of each run, Pallas kernels for 10% -> 30%
where the time goes in v3:
time: 197 us; the launch traced here: 196 us
  Pallas kernels  59.1 us (30%)
  waiting for transfers between devices  56.1 us (28%)
  starting transfers between devices  53.9 us (27%)
  local copies, waits for them, and re-layouts  19.4 us (10%)
  other arithmetic  6.35 us (3%)
    all_to_all x6, starting transfers between devices, exchange(): return lax.all_to_all(x, Z, split_axis=0, concat_axis=0, tiled=True)  39.6 us
    pallas_call x1, Pallas kernels, run_backward(): pl.pallas_call(backward, name='backward', out_shape=(WIDE, NARROW, NARROW...  31.2 us
    pallas_call x1, Pallas kernels, run_forward(): pl.pallas_call(forward, name='forward', out_shape=(WIDE, STATS, WEIGHTS),...  27.9 us
    all_to_all x6, waiting for transfers between devices, exchange(): return lax.all_to_all(x, Z, split_axis=0, concat_axis=0, tiled=True)  27 us
    ppermute x1, waiting for transfers between devices, gather_y(): down = lax.ppermute(kv, 'y', ring(1))  13.3 us
    unnamed x21, local copies, waits for them, and re-layouts  7.65 us
    ppermute x1, waiting for transfers between devices, scatter_y(): up = lax.ppermute(up, 'y', ring(1))  5.71 us
    ppermute x1, waiting for transfers between devices, scatter_y(): down = lax.ppermute(down, 'y', ring(-1))  4.67 us
  transfers between devices with their start and end apart: 14, of which 10 were waited for; matrix products, arithmetic and copies ran while one was open for 10% of the time, Pallas kernels for 30%

profile of v3, /device:TPU:2, one launch (start us, length us, event | category | flops | bytes accessed | tf_op | source)
XLA Modules:
  0.0 196.0 jit_solution(9382073407980366945)
XLA Ops:
  0.6 0.0 copy-start.6
  0.6 0.7 fusion.1
  1.4 0.9 reshape_squeeze.13
  2.3 0.9 reshape_squeeze.14
  3.3 0.1 maximum_bitcast_fusion
  3.4 0.2 pad_maximum_fusion.2
  3.7 0.9 broadcast_in_dim.7
  4.5 8.5 %all-to-all-start = ((bf16[8,144,256]{2,1,0:T(8,128)(2,1)}), bf16[8,144,256]{2,1,0:T(8,128)(2,1)S(1)}, u32[]{:S(2)}, u32[]{:S(2)}) async-start(bf16[8,144,256]{2,1,0:T(8,128)(2,1)} %bitcast.6), calls=%async_computation | async-start | bytes 1179648 | tf_op jit(solution)/shard_map/all_to_all | solution.py:275
  13.0 1.6 copy.28
  14.6 1.3 copy.29
  15.9 16.0 %all-to-all-done.kv0 = bf16[8,144,256]{2,1,0:T(8,128)(2,1)S(1)} async-done(((bf16[8,144,256]{2,1,0:T(8,128)(2,1)}), bf16[8,144,256]{2,1,0:T(8,128)(2,1)S(1)}, u32[]{:S(2)}, u32[]{:S(2)}) %all-to-all-start) | async-done | bytes 589856 | tf_op jit(solution)/shard_map/all_to_all | solution.py:275
  31.9 3.6 %all-to-all-start.1 = ((bf16[8,128,512]{2,1,0:T(8,128)(2,1)}), bf16[8,128,512]{2,1,0:T(8,128)(2,1)S(1)}, u32[]{:S(2)}, u32[]{:S(2)}) async-start(bf16[8,128,512]{2,1,0:T(8,128)(2,1)} %bitcast.3), calls=%async_computation.1 | async-start | bytes 2097152 | tf_op jit(solution)/shard_map/all_to_all | solution.py:275
  35.5 1.7 collective-permute-start.1
  37.1 1.7 collective-permute-start
  38.8 13.3 %collective-permute-done.1.kv3 = bf16[8,144,256]{2,1,0:T(8,128)(2,1)S(1)} collective-permute-done((bf16[8,144,256]{2,1,0:T(8,128)(2,1)S(1)}, bf16[8,144,256]{2,1,0:T(8,128)(2,1)S(1)}, u32[]{:S(2)}, u32[]{:S(2)}) %collective-permute-start.1) | collective-permute-done | bytes 589856 | tf_op jit(solution)/shard_map/ppermute | solution.py:285
  52.1 0.4 collective-permute-start.2
  52.5 0.0 collective-permute-done.kv1
  52.5 0.8 slice.45
  53.2 0.0 copy-done.3
  53.2 0.2 copy-done.4
  53.5 2.9 %collective-permute-start.3 = (bf16[4,144,256]{2,1,0:T(8,128)(2,1)}, bf16[4,144,256]{2,1,0:T(8,128)(2,1)}, u32[]{:S(2)}, u32[]{:S(2)}) collective-permute-start(bf16[4,144,256]{2,1,0:T(8,128)(2,1)} %slice.45), channel_id=1, source_target_pairs={{0,48},{16,0},{32,16},{48,32},{1,49},{17,1},{33,17},{49,33},{2,50}... | collective-permute-start | bytes 884744 | tf_op jit(solution)/shard_map/ppermute | solution.py:287
  56.4 1.6 copy.32
  58.0 1.3 copy.33
  59.3 2.2 %collective-permute-done.2 = bf16[4,144,256]{2,1,0:T(8,128)(2,1)S(1)} collective-permute-done((bf16[4,144,256]{2,1,0:T(8,128)(2,1)S(1)}, bf16[4,144,256]{2,1,0:T(8,128)(2,1)S(1)}, u32[]{:S(2)}, u32[]{:S(2)}) %collective-permute-start.2) | collective-permute-done | bytes 294944 | tf_op jit(solution)/shard_map/ppermute | solution.py:287
  61.6 0.5 collective-permute-done.3
  62.1 1.0 constant_dynamic-update-slice_fusion.kv2
  63.1 0.0 copy-start.5
  63.1 1.5 all-to-all-done.1.q_ref
  64.6 0.0 copy-done.5
  64.6 5.7 %all-to-all-start.3 = ((bf16[8,128,512]{2,1,0:T(8,128)(2,1)}), bf16[8,128,512]{2,1,0:T(8,128)(2,1)S(1)}, u32[]{:S(2)}, u32[]{:S(2)}) async-start(bf16[8,128,512]{2,1,0:T(8,128)(2,1)} %bitcast.10), calls=%async_computation.3 | async-start | bytes 2097152 | tf_op jit(solution)/shard_map/all_to_all | solution.py:275
  70.3 0.0 copy-done.6
  70.5 0.0 copy-done.2
  70.5 27.9 %forward.1 = (bf16[8,128,512]{2,1,0:T(8,128)(2,1)}, f32[8,1,512]{2,1,0:T(1,128)}, bf16[36,512,512]{2,1,0:T(8,128)(2,1)}) custom-call(s32[1]{0:T(128)} %bitcast.1.turn, bf16[8,128,512]{2,1,0:T(8,128)(2,1)} %copy-done, bf16[8,144,256]{2,1,0:T(8,128)(2,1)} %copy-done.2, bf16[8,144,256]{2,1,0:T(8,128)(2,1)} %copy-done.4, bf16[8,144,256]{2,1,0:T(8,128)(2,1)} %copy-done.5, ...), custom_call_target="tpu_custom_call" | custom-call | flops 9663676416 | bytes 25165824 | tf_op jit(solution)/shard_map/forward/pallas_call | solution.py:228
  98.4 0.0 all-to-all-done.3.g_ref
  98.4 7.2 %all-to-all-start.2 = ((bf16[8,128,512]{2,1,0:T(8,128)(2,1)}), bf16[8,128,512]{2,1,0:T(8,128)(2,1)S(1)}, u32[]{:S(2)}, u32[]{:S(2)}) async-start(bf16[8,128,512]{2,1,0:T(8,128)(2,1)} %get-tuple-element.17.o_ref), calls=%async_computation.2 | async-start | bytes 2097152 | tf_op jit(solution)/shard_map/all_to_all | solution.py:275
  105.7 31.2 %backward.1 = (bf16[8,128,512]{2,1,0:T(8,128)(2,1)}, bf16[8,128,256]{2,1,0:T(8,128)(2,1)}, bf16[8,128,256]{2,1,0:T(8,128)(2,1)}, bf16[8,128,256]{2,1,0:T(8,128)(2,1)}, bf16[8,128,256]{2,1,0:T(8,128)(2,1)}) custom-call(s32[1]{0:T(128)} %bitcast.1.turn, bf16[8,128,512]{2,1,0:T(8,128)(2,1)} %copy-done, bf16[8,128,512]{2,1,0:T(8,128)(2,1)} %copy-done.1, ...), custom_call_target="tpu_custom_call" | custom-call | flops 19327352832 | bytes 25165824 | tf_op jit(solution)/shard_map/backward/pallas_call | solution.py:250
  136.9 0.0 all-to-all-done.2
  136.9 7.2 %all-to-all-start.4 = ((bf16[8,128,512]{2,1,0:T(8,128)(2,1)}), bf16[8,128,512]{2,1,0:T(8,128)(2,1)S(1)}, u32[]{:S(2)}, u32[]{:S(2)}) async-start(bf16[8,128,512]{2,1,0:T(8,128)(2,1)} %get-tuple-element.22), calls=%async_computation.4 | async-start | bytes 2097152 | tf_op jit(solution)/shard_map/all_to_all | solution.py:275
  144.1 1.1 fusion.2
  145.2 3.8 %collective-permute-start.6 = (bf16[4,128,256]{2,1,0:T(8,128)(2,1)S(1)}, bf16[4,128,256]{2,1,0:T(8,128)(2,1)S(1)}, u32[]{:S(2)}, u32[]{:S(2)}) collective-permute-start(bf16[4,128,256]{2,1,0:T(8,128)(2,1)S(1)} %get-tuple-element.41), channel_id=1, source_target_pairs={{0,48},{16,0},{32,16},{48,32},{1,49},{17,1},{33,17},{49,33},{2,50}... | collective-permute-start | bytes 786440 | tf_op jit(solution)/shard_map/ppermute | solution.py:299
  149.0 1.0 slice.38
  149.9 1.0 slice.39
  150.9 0.1 collective-permute-start.4
  151.0 1.9 collective-permute-done.6
  152.9 1.0 add_convert_fusion.1
  153.9 3.8 %collective-permute-start.7 = (bf16[8,128,256]{2,1,0:T(8,128)(2,1)S(1)}, bf16[8,128,256]{2,1,0:T(8,128)(2,1)S(1)}, u32[]{:S(2)}, u32[]{:S(2)}) collective-permute-start(bf16[8,128,256]{2,1,0:T(8,128)(2,1)S(1)} %pad_maximum_fusion.1), channel_id=1, source_target_pairs={{0,48},{16,0},{32,16},{48,32},{1,49},{17,1},{33,17},{49,33},{2,50}... | collective-permute-start | bytes 1572872 | tf_op jit(solution)/shard_map/ppermute | solution.py:303
  157.7 0.9 collective-permute-done.4
  158.6 1.0 add_convert_fusion.2
  159.6 0.1 collective-permute-start.5
  159.7 4.7 %collective-permute-done.7 = bf16[8,128,256]{2,1,0:T(8,128)(2,1)S(1)} collective-permute-done((bf16[8,128,256]{2,1,0:T(8,128)(2,1)S(1)}, bf16[8,128,256]{2,1,0:T(8,128)(2,1)S(1)}, u32[]{:S(2)}, u32[]{:S(2)}) %collective-permute-start.7) | collective-permute-done | bytes 524320 | tf_op jit(solution)/shard_map/ppermute | solution.py:303
  164.4 5.7 %collective-permute-done.5 = bf16[8,128,256]{2,1,0:T(8,128)(2,1)S(1)} collective-permute-done((bf16[8,128,256]{2,1,0:T(8,128)(2,1)S(1)}, bf16[8,128,256]{2,1,0:T(8,128)(2,1)S(1)}, u32[]{:S(2)}, u32[]{:S(2)}) %collective-permute-start.5) | collective-permute-done | bytes 524320 | tf_op jit(solution)/shard_map/ppermute | solution.py:302
  170.1 2.0 %add_convert_fusion = bf16[8,128,256]{2,1,0:T(8,128)(2,1)} fusion(bf16[8,128,256]{2,1,0:T(8,128)(2,1)S(1)} %collective-permute-done.7, bf16[8,128,256]{2,1,0:T(8,128)(2,1)S(1)} %collective-permute-done.5, bf16[8,128,256]{2,1,0:T(8,128)(2,1)} %get-tuple-element.23), kind=kLoop, calls=%fused_computation | loop fusion | flops 1572864 | bytes 2097152 | tf_op jit(solution)/shard_map/convert_element_type | solution.py:304
  172.2 0.0 all-to-all-done.4
  172.2 7.4 %all-to-all-start.5 = ((bf16[8,128,256]{2,1,0:T(8,128)(2,1)}), bf16[8,128,256]{2,1,0:T(8,128)(2,1)}, u32[]{:S(2)}, u32[]{:S(2)}) async-start(bf16[8,128,256]{2,1,0:T(8,128)(2,1)} %add_convert_fusion), calls=%async_computation.5 | async-start | bytes 1048576 | tf_op jit(solution)/shard_map/all_to_all | solution.py:275
  179.6 0.7 copy.31
  180.3 1.3 copy.37
  181.6 0.7 copy.34
  182.2 1.3 copy.38
  183.6 9.5 %all-to-all-done.5 = bf16[8,128,256]{2,1,0:T(8,128)(2,1)} async-done(((bf16[8,128,256]{2,1,0:T(8,128)(2,1)}), bf16[8,128,256]{2,1,0:T(8,128)(2,1)}, u32[]{:S(2)}, u32[]{:S(2)}) %all-to-all-start.5) | async-done | bytes 524320 | tf_op jit(solution)/shard_map/all_to_all | solution.py:275
  193.0 1.1 bitcast_reduce_fusion
  194.2 0.1 copy.36
  194.3 0.8 copy.40
  195.1 0.1 copy.35
  195.2 0.8 copy.39
  (15 shorter events, 0.3 us)
Async XLA Ops:
  0.6 69.7 %copy-start.6 = (s32[1,128]{1,0:T(1,128)S(1)}, s32[1,128]{1,0:T(1,128)}, u32[]{:S(2)}) copy-start(s32[1,128]{1,0:T(1,128)} %param.9) | copy-start | bytes 1540
  4.5 27.4 %all-to-all-start = ((bf16[8,144,256]{2,1,0:T(8,128)(2,1)}), bf16[8,144,256]{2,1,0:T(8,128)(2,1)S(1)}, u32[]{:S(2)}, u32[]{:S(2)}) async-start(bf16[8,144,256]{2,1,0:T(8,128)(2,1)} %bitcast.6), calls=%async_computation | async-start | bytes 1179648 | tf_op jit(solution)/shard_map/all_to_all | solution.py:275
  31.9 38.6 %copy-start.2 = (bf16[8,144,256]{2,1,0:T(8,128)(2,1)}, bf16[8,144,256]{2,1,0:T(8,128)(2,1)S(1)}, u32[]{:S(2)}) copy-start(bf16[8,144,256]{2,1,0:T(8,128)(2,1)S(1)} %all-to-all-done.kv0) | copy-start | bytes 1769476
  31.9 32.7 %all-to-all-start.1 = ((bf16[8,128,512]{2,1,0:T(8,128)(2,1)}), bf16[8,128,512]{2,1,0:T(8,128)(2,1)S(1)}, u32[]{:S(2)}, u32[]{:S(2)}) async-start(bf16[8,128,512]{2,1,0:T(8,128)(2,1)} %bitcast.3), calls=%async_computation.1 | async-start | bytes 2097152 | tf_op jit(solution)/shard_map/all_to_all | solution.py:275
  35.5 16.6 %collective-permute-start.1 = (bf16[8,144,256]{2,1,0:T(8,128)(2,1)S(1)}, bf16[8,144,256]{2,1,0:T(8,128)(2,1)S(1)}, u32[]{:S(2)}, u32[]{:S(2)}) collective-permute-start(bf16[8,144,256]{2,1,0:T(8,128)(2,1)S(1)} %all-to-all-done.kv0), channel_id=1, source_target_pairs={{0,16},{16,32},{32,48},{48,0},{1,17},{17,33},{33,49},{49,1},{2,18}... | collective-permute-start | bytes 1769480 | tf_op jit(solution)/shard_map/ppermute | solution.py:285
  37.1 15.4 %collective-permute-start = (bf16[8,144,256]{2,1,0:T(8,128)(2,1)S(1)}, bf16[8,144,256]{2,1,0:T(8,128)(2,1)S(1)}, u32[]{:S(2)}, u32[]{:S(2)}) collective-permute-start(bf16[8,144,256]{2,1,0:T(8,128)(2,1)S(1)} %all-to-all-done.kv0), channel_id=1, source_target_pairs={{0,48},{16,0},{32,16},{48,32},{1,49},{17,1},{33,17},{49,33},{2,50}... | collective-permute-start | bytes 1769480 | tf_op jit(solution)/shard_map/ppermute | solution.py:284
  52.1 1.2 copy-start.3
  52.1 9.4 %collective-permute-start.2 = (bf16[4,144,256]{2,1,0:T(8,128)(2,1)S(1)}, bf16[4,144,256]{2,1,0:T(8,128)(2,1)S(1)}, u32[]{:S(2)}, u32[]{:S(2)}) collective-permute-start(bf16[4,144,256]{2,1,0:T(8,128)(2,1)S(1)} %slice.44), channel_id=1, source_target_pairs={{0,16},{16,32},{32,48},{48,0},{1,17},{17,33},{33,49},{49,1},{2,18}... | collective-permute-start | bytes 884744 | tf_op jit(solution)/shard_map/ppermute | solution.py:287
  52.5 1.0 copy-start.4
  53.5 8.6 %collective-permute-start.3 = (bf16[4,144,256]{2,1,0:T(8,128)(2,1)}, bf16[4,144,256]{2,1,0:T(8,128)(2,1)}, u32[]{:S(2)}, u32[]{:S(2)}) collective-permute-start(bf16[4,144,256]{2,1,0:T(8,128)(2,1)} %slice.45), channel_id=1, source_target_pairs={{0,48},{16,0},{32,16},{48,32},{1,49},{17,1},{33,17},{49,33},{2,50}... | collective-permute-start | bytes 884744 | tf_op jit(solution)/shard_map/ppermute | solution.py:287
  63.1 1.5 copy-start.5
  64.6 5.9 %copy-start = (bf16[8,128,512]{2,1,0:T(8,128)(2,1)}, bf16[8,128,512]{2,1,0:T(8,128)(2,1)S(1)}, u32[]{:S(2)}) copy-start(bf16[8,128,512]{2,1,0:T(8,128)(2,1)S(1)} %all-to-all-done.1.q_ref) | copy-start | bytes 3145732
  64.6 33.8 %all-to-all-start.3 = ((bf16[8,128,512]{2,1,0:T(8,128)(2,1)}), bf16[8,128,512]{2,1,0:T(8,128)(2,1)S(1)}, u32[]{:S(2)}, u32[]{:S(2)}) async-start(bf16[8,128,512]{2,1,0:T(8,128)(2,1)} %bitcast.10), calls=%async_computation.3 | async-start | bytes 2097152 | tf_op jit(solution)/shard_map/all_to_all | solution.py:275
  98.4 7.2 %copy-start.1 = (bf16[8,128,512]{2,1,0:T(8,128)(2,1)}, bf16[8,128,512]{2,1,0:T(8,128)(2,1)S(1)}, u32[]{:S(2)}) copy-start(bf16[8,128,512]{2,1,0:T(8,128)(2,1)S(1)} %all-to-all-done.3.g_ref) | copy-start | bytes 3145732
  98.4 38.5 %all-to-all-start.2 = ((bf16[8,128,512]{2,1,0:T(8,128)(2,1)}), bf16[8,128,512]{2,1,0:T(8,128)(2,1)S(1)}, u32[]{:S(2)}, u32[]{:S(2)}) async-start(bf16[8,128,512]{2,1,0:T(8,128)(2,1)} %get-tuple-element.17.o_ref), calls=%async_computation.2 | async-start | bytes 2097152 | tf_op jit(solution)/shard_map/all_to_all | solution.py:275
  136.9 35.2 %all-to-all-start.4 = ((bf16[8,128,512]{2,1,0:T(8,128)(2,1)}), bf16[8,128,512]{2,1,0:T(8,128)(2,1)S(1)}, u32[]{:S(2)}, u32[]{:S(2)}) async-start(bf16[8,128,512]{2,1,0:T(8,128)(2,1)} %get-tuple-element.22), calls=%async_computation.4 | async-start | bytes 2097152 | tf_op jit(solution)/shard_map/all_to_all | solution.py:275
  145.2 7.7 %collective-permute-start.6 = (bf16[4,128,256]{2,1,0:T(8,128)(2,1)S(1)}, bf16[4,128,256]{2,1,0:T(8,128)(2,1)S(1)}, u32[]{:S(2)}, u32[]{:S(2)}) collective-permute-start(bf16[4,128,256]{2,1,0:T(8,128)(2,1)S(1)} %get-tuple-element.41), channel_id=1, source_target_pairs={{0,48},{16,0},{32,16},{48,32},{1,49},{17,1},{33,17},{49,33},{2,50}... | collective-permute-start | bytes 786440 | tf_op jit(solution)/shard_map/ppermute | solution.py:299
  150.9 7.7 %collective-permute-start.4 = (bf16[4,128,256]{2,1,0:T(8,128)(2,1)S(1)}, bf16[4,128,256]{2,1,0:T(8,128)(2,1)S(1)}, u32[]{:S(2)}, u32[]{:S(2)}) collective-permute-start(bf16[4,128,256]{2,1,0:T(8,128)(2,1)S(1)} %get-tuple-element.40), channel_id=1, source_target_pairs={{0,16},{16,32},{32,48},{48,0},{1,17},{17,33},{33,49},{49,1},{2,18}... | collective-permute-start | bytes 786440 | tf_op jit(solution)/shard_map/ppermute | solution.py:298
  153.9 10.5 %collective-permute-start.7 = (bf16[8,128,256]{2,1,0:T(8,128)(2,1)S(1)}, bf16[8,128,256]{2,1,0:T(8,128)(2,1)S(1)}, u32[]{:S(2)}, u32[]{:S(2)}) collective-permute-start(bf16[8,128,256]{2,1,0:T(8,128)(2,1)S(1)} %pad_maximum_fusion.1), channel_id=1, source_target_pairs={{0,48},{16,0},{32,16},{48,32},{1,49},{17,1},{33,17},{49,33},{2,50}... | collective-permute-start | bytes 1572872 | tf_op jit(solution)/shard_map/ppermute | solution.py:303
  159.6 10.5 %collective-permute-start.5 = (bf16[8,128,256]{2,1,0:T(8,128)(2,1)S(1)}, bf16[8,128,256]{2,1,0:T(8,128)(2,1)S(1)}, u32[]{:S(2)}, u32[]{:S(2)}) collective-permute-start(bf16[8,128,256]{2,1,0:T(8,128)(2,1)S(1)} %pad_maximum_fusion), channel_id=1, source_target_pairs={{0,16},{16,32},{32,48},{48,0},{1,17},{17,33},{33,49},{49,1},{2,18}... | collective-permute-start | bytes 1572872 | tf_op jit(solution)/shard_map/ppermute | solution.py:302
  172.2 20.8 %all-to-all-start.5 = ((bf16[8,128,256]{2,1,0:T(8,128)(2,1)}), bf16[8,128,256]{2,1,0:T(8,128)(2,1)}, u32[]{:S(2)}, u32[]{:S(2)}) async-start(bf16[8,128,256]{2,1,0:T(8,128)(2,1)} %add_convert_fusion), calls=%async_computation.5 | async-start | bytes 1048576 | tf_op jit(solution)/shard_map/all_to_all | solution.py:275

commit v4 on v3

v4 whole, which is shorter than its diff:
```python
import math

import jax
import jax.numpy as jnp
from jax import lax
from jax.experimental import pallas as pl
from jax.experimental.pallas import tpu as pltpu
from jax.sharding import Mesh, PartitionSpec as P

H = 32
KVH = 4
DH = 128
ROWS = 128
PADDED = 144
BLOCK = 512
NY = 4
NH = 4
NZ = 2 * NH
PACK = H // NH
COLS = PACK * ROWS
TILES = NZ * (NZ + 1) // 4
NEGATIVE = -1e30
SCALE = 1.0 / math.sqrt(DH)
EXP2_SCALE = SCALE * math.log2(math.e)
DIMS_NT = (((1,), (1,)), ((), ()))
SLOTS = (0, 1, 4, 5, 6, 7, 2, 3)
F32 = jnp.float32
BF16 = jnp.bfloat16


def flip(ref, i):
    return jnp.concatenate([ref[i, :, k * DH : (k + 1) * DH].T for k in range(PACK)], axis=1)


def unflip(ref, i, value):
    for k in range(PACK):
        ref[i, :, k * DH : (k + 1) * DH] = value[:, k * ROWS : (k + 1) * ROWS].T


def fold(x, op):
    return op(x.reshape(x.shape[0] // 8, 8, x.shape[1]), axis=0)


def own_block(turn, n):
    return jnp.where(n < NH // 2, n + 2 * turn[0], n + NH - 2 * turn[0])


def turned(turn, slot):
    return (slot // NH) * NH + jnp.bitwise_and(slot - turn[1], NH - 1)


def key_slot(turn, slots, b):
    return turned(turn, jnp.bitwise_xor(slots[b], NH * turn[0]))


def set_slots(slots):
    for b in range(NZ):
        slots[b] = SLOTS[b]


def forward(
    turn, q_ref, kv0, kv1, kv2, kv3, o_ref, stat_ref, p_hbm,
    slots, s_buf, p_buf, k_n, v_t, out_acc, sems,
):
    pieces = (kv0, kv1, kv2, kv3)
    set_slots(slots)

    def row_marks(piece, z):
        row = piece[z, ROWS : ROWS + 16, :].astype(F32)[0:1]
        return row[:, :DH] * 64.0 + row[:, DH:]

    def prepare(b, carry):
        z = key_slot(turn, slots, b)
        for rel in range(NY):
            cut = slice(rel * ROWS, (rel + 1) * ROWS)
            k_n[b, cut, :] = pieces[rel][z, :ROWS, :DH]
            v_t[b, :, cut] = pieces[rel][z, :ROWS, DH:].T
        return carry

    lax.fori_loop(0, NZ, prepare, 0)

    def group(i, base):
        b = own_block(turn, i)
        z = turned(turn, i)
        q_t = flip(q_ref, i)
        out_acc[...] = jnp.zeros((DH, COLS), F32)

        def first(j, top):
            s = jnp.dot(k_n[j], q_t, preferred_element_type=F32)
            s_buf[j] = s
            return jnp.maximum(top, fold(s, jnp.max))

        top = lax.fori_loop(0, b, first, jnp.full((8, COLS), NEGATIVE, F32))
        s = jnp.dot(k_n[b], q_t, preferred_element_type=F32)
        q_marks = jnp.broadcast_to(row_marks(kv0, z), (ROWS, ROWS))
        for rel in range(NY):
            cut = slice(rel * ROWS, (rel + 1) * ROWS)
            k_marks = jnp.broadcast_to(row_marks(pieces[rel], z), (ROWS, ROWS)).T
            seen = k_marks <= q_marks
            part = jnp.concatenate(
                [
                    jnp.where(seen, s[cut, k * ROWS : (k + 1) * ROWS], NEGATIVE)
                    for k in range(PACK)
                ],
                axis=1,
            )
            s_buf[b, cut, :] = part
            top = jnp.maximum(top, fold(part, jnp.max))
        top = jnp.max(top, axis=0, keepdims=True)

        def second(j, total):
            w = jnp.exp2((s_buf[j] - top) * EXP2_SCALE)
            total = total + fold(w, jnp.sum)
            w = w.astype(BF16)
            tile = base + j
            p_buf[tile] = w
            out_acc[...] += jnp.dot(v_t[j], w, preferred_element_type=F32)
            pltpu.make_async_copy(p_buf.at[tile], p_hbm.at[tile], sems.at[tile]).start()
            return total

        total = lax.fori_loop(0, b + 1, second, jnp.zeros((8, COLS), F32))
        inv = 1.0 / jnp.sum(total, axis=0, keepdims=True)
        unflip(o_ref, i, (out_acc[...] * inv).astype(BF16))
        stat_ref[i] = inv
        return base + b + 1

    lax.fori_loop(0, NH, group, 0)

    def wait(tile, carry):
        pltpu.make_async_copy(p_buf.at[tile], p_hbm.at[tile], sems.at[tile]).wait()
        return carry

    lax.fori_loop(0, TILES, wait, 0)


def backward(
    turn, q_ref, g_ref, o_ref, stat_ref, kv0, kv1, kv2, kv3, p_hbm,
    dq_ref, out0, out1, out2, out3,
    slots, p_buf, k_t, v_n, acc, dq_acc, sems,
):
    pieces = (kv0, kv1, kv2, kv3)
    outs = (out0, out1, out2, out3)
    set_slots(slots)

    def fetch(tile, carry):
        pltpu.make_async_copy(p_hbm.at[tile], p_buf.at[tile], sems.at[tile]).start()
        return carry

    lax.fori_loop(0, TILES, fetch, 0)

    def prepare(b, carry):
        z = key_slot(turn, slots, b)
        for rel in range(NY):
            cut = slice(rel * ROWS, (rel + 1) * ROWS)
            k_t[b, :, cut] = pieces[rel][z, :ROWS, :DH].T
            v_n[b, cut, :] = pieces[rel][z, :ROWS, DH:]
        acc[b] = jnp.zeros((BLOCK, 2 * DH), F32)
        return carry

    lax.fori_loop(0, NZ, prepare, 0)

    def group(i, base):
        b = own_block(turn, i)
        dq_acc[...] = jnp.zeros((DH, COLS), F32)
        q_t = flip(q_ref, i)
        g_t = flip(g_ref, i)
        o_t = flip(o_ref, i)
        inv = stat_ref[i]
        delta = jnp.sum(g_t.astype(F32) * o_t.astype(F32), axis=0, keepdims=True)
        q_n = (q_t.astype(F32) * inv).astype(BF16)
        g_n = (g_t.astype(F32) * inv).astype(BF16)

        def step(j, carry):
            tile = base + j
            pltpu.make_async_copy(p_hbm.at[tile], p_buf.at[tile], sems.at[tile]).wait()
            w = p_buf[tile]
            dp = jnp.dot(v_n[j], g_t, preferred_element_type=F32)
            ds = (w.astype(F32) * (dp - delta)).astype(BF16)
            acc[j, :, DH:] += lax.dot_general(w, g_n, DIMS_NT, preferred_element_type=F32)
            acc[j, :, :DH] += lax.dot_general(ds, q_n, DIMS_NT, preferred_element_type=F32)
            dq_acc[...] += jnp.dot(k_t[j], ds, preferred_element_type=F32)
            return carry

        lax.fori_loop(0, b + 1, step, 0)
        unflip(dq_ref, i, (dq_acc[...] * (inv * SCALE)).astype(BF16))
        return base + b + 1

    lax.fori_loop(0, NH, group, 0)

    def finish(b, carry):
        slot = jnp.bitwise_xor(slots[b], NH * turn[0])
        z = (slot % NH) * 2 + jnp.bitwise_xor(slot // NH, turn[2])
        for rel in range(NY):
            cut = slice(rel * ROWS, (rel + 1) * ROWS)
            outs[rel][z, :, :DH] = (acc[b, cut, :DH] * SCALE).astype(BF16)
            outs[rel][z, :, DH:] = acc[b, cut, DH:].astype(BF16)
        return carry

    lax.fori_loop(0, NZ, finish, 0)


VMEM = pl.BlockSpec(memory_space=pltpu.VMEM)
SMEM = pl.BlockSpec(memory_space=pltpu.SMEM)
ANY = pl.BlockSpec(memory_space=pl.ANY)
WIDE = jax.ShapeDtypeStruct((NH, ROWS, COLS), BF16)
NARROW = jax.ShapeDtypeStruct((NZ, ROWS, 2 * DH), BF16)
WEIGHTS = jax.ShapeDtypeStruct((TILES, BLOCK, COLS), BF16)
STATS = jax.ShapeDtypeStruct((NH, 1, COLS), F32)
PARAMS = pltpu.CompilerParams(vmem_limit_bytes=56 * 1024 * 1024)


def cost(matmuls, exps):
    return pl.CostEstimate(
        flops=TILES * matmuls * 2 * BLOCK * COLS * DH * 2,
        bytes_accessed=24 * 1024 * 1024,
        transcendentals=exps * TILES * BLOCK * COLS,
    )


def run_forward(turn, q, pieces):
    return pl.pallas_call(
        forward,
        name="forward",
        out_shape=(WIDE, STATS, WEIGHTS),
        in_specs=[SMEM] + [VMEM] * 5,
        out_specs=[VMEM, VMEM, ANY],
        scratch_shapes=[
            pltpu.SMEM((NZ,), jnp.int32),
            pltpu.VMEM((NZ, BLOCK, COLS), F32),
            pltpu.VMEM((TILES, BLOCK, COLS), BF16),
            pltpu.VMEM((NZ, BLOCK, DH), BF16),
            pltpu.VMEM((NZ, DH, BLOCK), BF16),
            pltpu.VMEM((DH, COLS), F32),
            pltpu.SemaphoreType.DMA((TILES,)),
        ],
        compiler_params=PARAMS,
        cost_estimate=cost(2, 1),
    )(turn, q, *pieces)


def run_backward(turn, q, g, o, stat, pieces, weights):
    return pl.pallas_call(
        backward,
        name="backward",
        out_shape=(WIDE, NARROW, NARROW, NARROW, NARROW),
        in_specs=[SMEM] + [VMEM] * 8 + [ANY],
        out_specs=[VMEM] * 5,
        scratch_shapes=[
            pltpu.SMEM((NZ,), jnp.int32),
            pltpu.VMEM((TILES, BLOCK, COLS), BF16),
            pltpu.VMEM((NZ, DH, BLOCK), BF16),
            pltpu.VMEM((NZ, BLOCK, DH), BF16),
            pltpu.VMEM((NZ, BLOCK, 2 * DH), F32),
            pltpu.VMEM((DH, COLS), F32),
            pltpu.SemaphoreType.DMA((TILES,)),
        ],
        compiler_params=PARAMS,
        cost_estimate=cost(4, 0),
    )(turn, q, g, o, stat, *pieces, weights)


def ring(step):
    return [(i, (i + step) % NY) for i in range(NY)]


def hop(x, step):
    return lax.ppermute(x, "zhi", [(i, (i + step) % NH) for i in range(NH)])


def swap(x):
    return lax.ppermute(x, "outer", [(0, 1), (1, 0)])


def exchange(x):
    return lax.all_to_all(x, "zhi", split_axis=0, concat_axis=0, tiled=True)


def after(x, *earlier):
    return lax.optimization_barrier((x, *earlier))[0]


def gather_y(kv):
    half = kv.shape[0] // 2
    up = lax.ppermute(kv, "y", ring(-1))
    down = lax.ppermute(kv, "y", ring(1))
    far = jnp.concatenate(
        [lax.ppermute(down[:half], "y", ring(1)), lax.ppermute(up[half:], "y", ring(-1))]
    )
    return kv, up, far, down


def add(x, y):
    return (x.astype(F32) + y.astype(F32)).astype(BF16)


def scatter_y(own, up, far, down):
    half = own.shape[0] // 2
    from_down = lax.ppermute(far[:half], "y", ring(1))
    from_up = lax.ppermute(far[half:], "y", ring(-1))
    up = jnp.concatenate([add(up[:half], from_down), up[half:]])
    down = jnp.concatenate([down[:half], add(down[half:], from_up)])
    up = lax.ppermute(up, "y", ring(1))
    down = lax.ppermute(down, "y", ring(-1))
    return (own.astype(F32) + (up.astype(F32) + down.astype(F32))).astype(BF16)


def chunks(x):
    return x[0].reshape(ROWS, NH, COLS).transpose(1, 0, 2)


def rows(x):
    return x.transpose(1, 0, 2).reshape(1, ROWS, H * DH)


def shards(queries, keys, values, grad_out, positions):
    here = lax.axis_index("zhi").astype(jnp.int32)
    kv = jnp.concatenate(
        [keys[0].reshape(ROWS, KVH, DH), values[0].reshape(ROWS, KVH, DH)], axis=2
    ).transpose(1, 0, 2)
    marks = jnp.concatenate([positions[0] // 64, positions[0] % 64]).astype(BF16)
    marks = jnp.broadcast_to(marks, (KVH, PADDED - ROWS, 2 * DH))
    kv = jnp.concatenate([kv, marks], axis=1)
    own = positions[0, 0] // (2 * BLOCK)
    own = jnp.where(here < NH // 2, own, NH - 1 - own).astype(jnp.int32)
    parts = []
    for step in range(NH):
        part = lax.dynamic_index_in_dim(
            kv, jnp.bitwise_and(here - step, NH - 1), 0, keepdims=False
        )
        parts.append(hop(part, -step) if step else part)
    kv = jnp.stack(parts)
    turn = jnp.stack([own, here, lax.axis_index("outer").astype(jnp.int32)])
    kv = jnp.concatenate([kv, swap(kv)])
    pieces = gather_y(kv)
    q = exchange(after(chunks(queries), kv))
    g = exchange(after(chunks(grad_out), q, *pieces))
    out, stat, weights = run_forward(turn, q, pieces)
    dq, d0, d1, d2, d3 = run_backward(turn, q, g, out, stat, pieces, weights)
    out = exchange(out)
    dq = exchange(after(dq, out))
    dkv = after(scatter_y(d0, d1, d2, d3), dq)
    dkv = lax.all_to_all(dkv, ("zhi", "outer"), split_axis=0, concat_axis=0, tiled=True)
    dkv = dkv.reshape(NH, 2, ROWS, 2 * DH)
    dkv = add(dkv[:, 0], dkv[:, 1])
    dkv = dkv.transpose(1, 0, 2)
    dk = dkv[:, :, :DH].reshape(1, ROWS, KVH * DH)
    dv = dkv[:, :, DH:].reshape(1, ROWS, KVH * DH)
    return rows(out), rows(dq), dk, dv


def solution(mesh):
    devices = mesh.devices.reshape(NH, NY, mesh.shape["inner"], mesh.shape["outer"])
    fine = Mesh(devices, ("zhi", "y", "inner", "outer"))
    wide = P("inner", ("zhi", "y", "outer"), None)
    return jax.shard_map(
        shards,
        mesh=fine,
        in_specs=(wide, wide, wide, wide, P("inner", ("zhi", "y", "outer"))),
        out_specs=(wide, wide, wide, wide),
        check_vma=False,
    )
```

time: 197 us -> 185 us (0.939)
  Pallas kernels: 59.1 us -> 51.2 us
  waiting for transfers between devices: 56.1 us -> 48.9 us
  starting transfers between devices: 53.9 us -> 58.2 us
    all_to_all x6 -> x5, waiting for transfers between devices: 27 us -> 10.6 us  [the longest x1 9.45 us: shards(): lax.all_to_all(dkv, ('zhi', 'outer'), split_axis=0, concat_axis=0, tiled=...]
    ppermute x0 -> x4, starting transfers between devices: none -> 11.5 us  [the longest x3 11.4 us: hop(): return lax.ppermute(x, 'zhi', [(i, (i + step) % NH) for i in range(NH)])]
    ppermute x0 -> x4, waiting for transfers between devices: none -> 10.8 us  [the longest x1 8.87 us: swap(): return lax.ppermute(x, 'outer', [(0, 1), (1, 0)])]
    all_to_all x6 -> x5, starting transfers between devices: 39.6 us -> 32.8 us  [the longest x4 25.6 us: exchange(): return lax.all_to_all(x, 'zhi', split_axis=0, concat_axis=0, tiled=True)]
    pallas_call x1, Pallas kernels: 27.9 us -> 23.5 us  [run_forward(): pl.pallas_call(forward, name='forward', out_shape=(WIDE, STATS, WEIGHTS),...]
    pallas_call x1, Pallas kernels: 31.2 us -> 27.7 us  [run_backward(): pl.pallas_call(backward, name='backward', out_shape=(WIDE, NARROW, NARROW...]
    ppermute x1, waiting for transfers between devices: 0.87 us -> 3.61 us  [scatter_y(): from_down = lax.ppermute(far[:half], 'y', ring(1))]
    ppermute x1, waiting for transfers between devices: 4.67 us -> 1.99 us  [scatter_y(): down = lax.ppermute(down, 'y', ring(-1))]
  transfers between devices with their start and end apart: 14 -> 17, of which waited for: 10 -> 10; matrix products, arithmetic and copies ran while one was open for 10% -> 10% of each run, Pallas kernels for 30% -> 28%
where the time goes in v4:
time: 185 us; the launch traced here: 184 us
  starting transfers between devices  58.2 us (31%)
  Pallas kernels  51.2 us (28%)
  waiting for transfers between devices  48.9 us (26%)
  local copies, waits for them, and re-layouts  17.8 us (10%)
  other arithmetic  6.76 us (4%)
    pallas_call x1, Pallas kernels, run_backward(): pl.pallas_call(backward, name='backward', out_shape=(WIDE, NARROW, NARROW...  27.7 us
    all_to_all x4, starting transfers between devices, exchange(): return lax.all_to_all(x, 'zhi', split_axis=0, concat_axis=0, tiled=True)  25.6 us
    pallas_call x1, Pallas kernels, run_forward(): pl.pallas_call(forward, name='forward', out_shape=(WIDE, STATS, WEIGHTS),...  23.5 us
    ppermute x1, waiting for transfers between devices, gather_y(): down = lax.ppermute(kv, 'y', ring(1))  12.2 us
    ppermute x3, starting transfers between devices, hop(): return lax.ppermute(x, 'zhi', [(i, (i + step) % NH) for i in range(NH)])  11.4 us
    all_to_all x1, waiting for transfers between devices, shards(): lax.all_to_all(dkv, ('zhi', 'outer'), split_axis=0, concat_axis=0, tiled=...  9.45 us
    ppermute x1, waiting for transfers between devices, swap(): return lax.ppermute(x, 'outer', [(0, 1), (1, 0)])  8.87 us
    unnamed x24, local copies, waits for them, and re-layouts  8.78 us
  transfers between devices with their start and end apart: 17, of which 10 were waited for; matrix products, arithmetic and copies ran while one was open for 10% of the time, Pallas kernels for 28%

profile of v4, /device:TPU:2, one launch (start us, length us, event | category | flops | bytes accessed | tf_op | source)
XLA Modules:
  0.0 184.0 jit_solution(7372093879401704727)
XLA Ops:
  0.7 0.7 fusion.9
  1.4 1.0 copy.13
  2.4 0.1 copy.15
  2.5 1.0 copy.14
  3.6 0.1 copy.16
  3.8 3.3 %collective-permute-start.2 = (bf16[144,256]{1,0:T(8,128)(2,1)S(1)}, bf16[144,256]{1,0:T(8,128)(2,1)S(1)}, u32[]{:S(2)}, u32[]{:S(2)}) collective-permute-start(bf16[144,256]{1,0:T(8,128)(2,1)S(1)} %get-tuple-element.36), channel_id=1, source_target_pairs={{0,64},{64,128},{128,192},{192,0},{1,65},{65,129},{129,193},{193,1... | collective-permute-start | bytes 221192 | tf_op jit(solution)/shard_map/ppermute | solution.py:267
  7.2 5.4 %collective-permute-start.1 = (bf16[144,256]{1,0:T(8,128)(2,1)S(1)}, bf16[144,256]{1,0:T(8,128)(2,1)S(1)}, u32[]{:S(2)}, u32[]{:S(2)}) collective-permute-start(bf16[144,256]{1,0:T(8,128)(2,1)S(1)} %get-tuple-element.37), channel_id=1, source_target_pairs={{0,128},{64,192},{128,0},{192,64},{1,129},{65,193},{129,1},{193,65... | collective-permute-start | bytes 221192 | tf_op jit(solution)/shard_map/ppermute | solution.py:267
  12.6 2.7 %collective-permute-start = (bf16[144,256]{1,0:T(8,128)(2,1)S(1)}, bf16[144,256]{1,0:T(8,128)(2,1)S(1)}, u32[]{:S(2)}, u32[]{:S(2)}) collective-permute-start(bf16[144,256]{1,0:T(8,128)(2,1)S(1)} %get-tuple-element.38), channel_id=1, source_target_pairs={{0,192},{64,0},{128,64},{192,128},{1,193},{65,1},{129,65},{193,129... | collective-permute-start | bytes 221192 | tf_op jit(solution)/shard_map/ppermute | solution.py:267
  15.2 1.6 copy.11
  16.8 1.3 copy.12
  18.2 0.0 collective-permute-done.2
  18.2 0.0 collective-permute-done.1
  18.2 1.9 %collective-permute-done = bf16[144,256]{1,0:T(8,128)(2,1)S(1)} collective-permute-done((bf16[144,256]{1,0:T(8,128)(2,1)S(1)}, bf16[144,256]{1,0:T(8,128)(2,1)S(1)}, u32[]{:S(2)}, u32[]{:S(2)}) %collective-permute-start) | collective-permute-done | bytes 73760 | tf_op jit(solution)/shard_map/ppermute | solution.py:267
  20.2 0.1 collective-permute-start.3
  20.3 8.9 %collective-permute-done.3 = bf16[4,144,256]{2,1,0:T(8,128)(2,1)S(1)} collective-permute-done((bf16[4,144,256]{2,1,0:T(8,128)(2,1)S(1)}, bf16[4,144,256]{2,1,0:T(8,128)(2,1)S(1)}, u32[]{:S(2)}, u32[]{:S(2)}) %collective-permute-start.3) | collective-permute-done | bytes 294944 | tf_op jit(solution)/shard_map/ppermute | solution.py:271
  29.2 4.6 %all-to-all-start = ((bf16[4,128,1024]{2,1,0:T(8,128)(2,1)}), bf16[4,128,1024]{2,1,0:T(8,128)(2,1)S(1)}, u32[]{:S(2)}, u32[]{:S(2)}) async-start(bf16[4,128,1024]{2,1,0:T(8,128)(2,1)} %bitcast.5), calls=%async_computation | async-start | bytes 2097152 | tf_op jit(solution)/shard_map/all_to_all | solution.py:275
  33.8 1.6 collective-permute-start.5
  35.4 1.7 collective-permute-start.4
  37.1 12.2 %collective-permute-done.5.kv3 = bf16[8,144,256]{2,1,0:T(8,128)(2,1)S(1)} collective-permute-done((bf16[8,144,256]{2,1,0:T(8,128)(2,1)S(1)}, bf16[8,144,256]{2,1,0:T(8,128)(2,1)S(1)}, u32[]{:S(2)}, u32[]{:S(2)}) %collective-permute-start.5) | collective-permute-done | bytes 589856 | tf_op jit(solution)/shard_map/ppermute | solution.py:285
  49.2 0.4 collective-permute-start.6
  49.6 0.0 collective-permute-done.4.kv1
  49.7 0.4 copy-done.2
  50.0 0.4 copy-done.3
  50.5 2.9 %collective-permute-start.7 = (bf16[4,144,256]{2,1,0:T(8,128)(2,1)S(1)}, bf16[4,144,256]{2,1,0:T(8,128)(2,1)S(1)}, u32[]{:S(2)}, u32[]{:S(2)}) collective-permute-start(bf16[4,144,256]{2,1,0:T(8,128)(2,1)S(1)} %slice.53), channel_id=1, source_target_pairs={{0,48},{16,0},{32,16},{48,32},{1,49},{17,1},{33,17},{49,33},{2,50}... | collective-permute-start | bytes 884744 | tf_op jit(solution)/shard_map/ppermute | solution.py:287
  53.4 1.6 copy.18
  55.0 1.3 copy.19
  56.3 1.1 collective-permute-done.6
  57.5 0.2 collective-permute-done.7
  57.7 0.0 copy-start.4
  57.7 1.2 all-to-all-done.q_ref
  58.9 6.5 %all-to-all-start.2 = ((bf16[4,128,1024]{2,1,0:T(8,128)(2,1)}), bf16[4,128,1024]{2,1,0:T(8,128)(2,1)S(1)}, u32[]{:S(2)}, u32[]{:S(2)}) async-start(bf16[4,128,1024]{2,1,0:T(8,128)(2,1)} %bitcast.19), calls=%async_computation.2 | async-start | bytes 2097152 | tf_op jit(solution)/shard_map/all_to_all | solution.py:275
  65.6 0.7 pad_add_fusion.turn
  66.3 23.5 %forward.1 = (bf16[4,128,1024]{2,1,0:T(8,128)(2,1)}, f32[4,1,1024]{2,1,0:T(1,128)}, bf16[18,512,1024]{2,1,0:T(8,128)(2,1)}) custom-call(s32[3]{0:T(128)} %pad_add_fusion.turn, bf16[4,128,1024]{2,1,0:T(8,128)(2,1)} %copy-done, bf16[8,144,256]{2,1,0:T(8,128)(2,1)} %copy-done.5, bf16[8,144,256]{2,1,0:T(8,128)(2,1)} %copy-done.3, ...), custom_call_target="tpu_custom_call" | custom-call | flops 9663676416 | bytes 25165824 | tf_op jit(solution)/shard_map/forward/pallas_call | solution.py:221
  89.8 0.0 all-to-all-done.2.g_ref
  89.8 7.2 %all-to-all-start.1 = ((bf16[4,128,1024]{2,1,0:T(8,128)(2,1)}), bf16[4,128,1024]{2,1,0:T(8,128)(2,1)S(1)}, u32[]{:S(2)}, u32[]{:S(2)}) async-start(bf16[4,128,1024]{2,1,0:T(8,128)(2,1)} %get-tuple-element.17.o_ref), calls=%async_computation.1 | async-start | bytes 2097152 | tf_op jit(solution)/shard_map/all_to_all | solution.py:275
  97.0 27.7 %backward.1 = (bf16[4,128,1024]{2,1,0:T(8,128)(2,1)}, bf16[8,128,256]{2,1,0:T(8,128)(2,1)}, bf16[8,128,256]{2,1,0:T(8,128)(2,1)}, bf16[8,128,256]{2,1,0:T(8,128)(2,1)}, bf16[8,128,256]{2,1,0:T(8,128)(2,1)}) custom-call(s32[3]{0:T(128)} %pad_add_fusion.turn, bf16[4,128,1024]{2,1,0:T(8,128)(2,1)} %copy-done, bf16[4,128,1024]{2,1,0:T(8,128)(2,1)} %copy-done.1, ...), custom_call_target="tpu_custom_call" | custom-call | flops 19327352832 | bytes 25165824 | tf_op jit(solution)/shard_map/backward/pallas_call | solution.py:242
  124.7 1.1 fusion.11
  125.8 3.8 %collective-permute-start.10 = (bf16[4,128,256]{2,1,0:T(8,128)(2,1)S(1)}, bf16[4,128,256]{2,1,0:T(8,128)(2,1)S(1)}, u32[]{:S(2)}, u32[]{:S(2)}) collective-permute-start(bf16[4,128,256]{2,1,0:T(8,128)(2,1)S(1)} %get-tuple-element.35), channel_id=1, source_target_pairs={{0,48},{16,0},{32,16},{48,32},{1,49},{17,1},{33,17},{49,33},{2,50}... | collective-permute-start | bytes 786440 | tf_op jit(solution)/shard_map/ppermute | solution.py:299
  129.6 0.0 all-to-all-done.1
  129.6 7.2 %all-to-all-start.3 = ((bf16[4,128,1024]{2,1,0:T(8,128)(2,1)}), bf16[4,128,1024]{2,1,0:T(8,128)(2,1)S(1)}, u32[]{:S(2)}, u32[]{:S(2)}) async-start(bf16[4,128,1024]{2,1,0:T(8,128)(2,1)} %get-tuple-element.22), calls=%async_computation.3 | async-start | bytes 2097152 | tf_op jit(solution)/shard_map/all_to_all | solution.py:275
  136.8 1.0 slice.44
  137.8 1.0 slice.45
  138.7 0.3 collective-permute-start.8
  139.0 0.0 collective-permute-done.10
  139.0 1.0 add_convert_fusion.2
  140.1 3.3 %collective-permute-start.11 = (bf16[8,128,256]{2,1,0:T(8,128)(2,1)S(1)}, bf16[8,128,256]{2,1,0:T(8,128)(2,1)S(1)}, u32[]{:S(2)}, u32[]{:S(2)}) collective-permute-start(bf16[8,128,256]{2,1,0:T(8,128)(2,1)S(1)} %pad_maximum_fusion.1), channel_id=1, source_target_pairs={{0,48},{16,0},{32,16},{48,32},{1,49},{17,1},{33,17},{49,33},{2,50}... | collective-permute-start | bytes 1572872 | tf_op jit(solution)/shard_map/ppermute | solution.py:303
  143.4 3.6 %collective-permute-done.8 = bf16[4,128,256]{2,1,0:T(8,128)(2,1)S(1)} collective-permute-done((bf16[4,128,256]{2,1,0:T(8,128)(2,1)S(1)}, bf16[4,128,256]{2,1,0:T(8,128)(2,1)S(1)}, u32[]{:S(2)}, u32[]{:S(2)}) %collective-permute-start.8) | collective-permute-done | bytes 262176 | tf_op jit(solution)/shard_map/ppermute | solution.py:298
  147.0 1.0 add_convert_fusion.3
  148.1 0.1 collective-permute-start.9
  148.2 2.0 %collective-permute-done.11 = bf16[8,128,256]{2,1,0:T(8,128)(2,1)S(1)} collective-permute-done((bf16[8,128,256]{2,1,0:T(8,128)(2,1)S(1)}, bf16[8,128,256]{2,1,0:T(8,128)(2,1)S(1)}, u32[]{:S(2)}, u32[]{:S(2)}) %collective-permute-start.11) | collective-permute-done | bytes 524320 | tf_op jit(solution)/shard_map/ppermute | solution.py:303
  150.1 8.4 %collective-permute-done.9 = bf16[8,128,256]{2,1,0:T(8,128)(2,1)S(1)} collective-permute-done((bf16[8,128,256]{2,1,0:T(8,128)(2,1)S(1)}, bf16[8,128,256]{2,1,0:T(8,128)(2,1)S(1)}, u32[]{:S(2)}, u32[]{:S(2)}) %collective-permute-start.9) | collective-permute-done | bytes 524320 | tf_op jit(solution)/shard_map/ppermute | solution.py:302
  158.5 2.0 %add_convert_fusion = bf16[8,128,256]{2,1,0:T(8,128)(2,1)} fusion(bf16[8,128,256]{2,1,0:T(8,128)(2,1)S(1)} %collective-permute-done.11, bf16[8,128,256]{2,1,0:T(8,128)(2,1)S(1)} %collective-permute-done.9, bf16[8,128,256]{2,1,0:T(8,128)(2,1)} %get-tuple-element.23), kind=kLoop, calls=%fused_computation | loop fusion | flops 1572864 | bytes 2097152 | tf_op jit(solution)/shard_map/convert_element_type | solution.py:304
  160.6 0.0 all-to-all-done.3
  160.6 7.2 %all-to-all-start.4 = ((bf16[8,128,256]{2,1,0:T(8,128)(2,1)}), bf16[8,128,256]{2,1,0:T(8,128)(2,1)}, u32[]{:S(2)}, u32[]{:S(2)}) async-start(bf16[8,128,256]{2,1,0:T(8,128)(2,1)} %add_convert_fusion), calls=%async_computation.4 | async-start | bytes 1048576 | tf_op jit(solution)/shard_map/all_to_all | solution.py:342
  167.8 0.7 copy.17
  168.4 1.3 copy.23
  169.7 0.7 copy.20
  170.4 1.3 copy.24
  171.7 9.5 %all-to-all-done.4 = bf16[8,128,256]{2,1,0:T(8,128)(2,1)} async-done(((bf16[8,128,256]{2,1,0:T(8,128)(2,1)}), bf16[8,128,256]{2,1,0:T(8,128)(2,1)}, u32[]{:S(2)}, u32[]{:S(2)}) %all-to-all-start.4) | async-done | bytes 524320 | tf_op jit(solution)/shard_map/all_to_all | solution.py:342
  181.2 1.1 fusion
  182.3 0.1 copy.22
  182.4 0.7 reshape.31
  183.1 0.1 copy.21
  183.2 0.7 reshape.30
  (27 shorter events, 0.4 us)
Async XLA Ops:
  0.6 64.8 %copy-start.6 = (s32[1,128]{1,0:T(1,128)S(1)}, s32[1,128]{1,0:T(1,128)}, u32[]{:S(2)}) copy-start(s32[1,128]{1,0:T(1,128)} %param.9) | copy-start | bytes 1540
  3.8 14.3 %collective-permute-start.2 = (bf16[144,256]{1,0:T(8,128)(2,1)S(1)}, bf16[144,256]{1,0:T(8,128)(2,1)S(1)}, u32[]{:S(2)}, u32[]{:S(2)}) collective-permute-start(bf16[144,256]{1,0:T(8,128)(2,1)S(1)} %get-tuple-element.36), channel_id=1, source_target_pairs={{0,64},{64,128},{128,192},{192,0},{1,65},{65,129},{129,193},{193,1... | collective-permute-start | bytes 221192 | tf_op jit(solution)/shard_map/ppermute | solution.py:267
  7.2 11.0 %collective-permute-start.1 = (bf16[144,256]{1,0:T(8,128)(2,1)S(1)}, bf16[144,256]{1,0:T(8,128)(2,1)S(1)}, u32[]{:S(2)}, u32[]{:S(2)}) collective-permute-start(bf16[144,256]{1,0:T(8,128)(2,1)S(1)} %get-tuple-element.37), channel_id=1, source_target_pairs={{0,128},{64,192},{128,0},{192,64},{1,129},{65,193},{129,1},{193,65... | collective-permute-start | bytes 221192 | tf_op jit(solution)/shard_map/ppermute | solution.py:267
  12.6 7.5 %collective-permute-start = (bf16[144,256]{1,0:T(8,128)(2,1)S(1)}, bf16[144,256]{1,0:T(8,128)(2,1)S(1)}, u32[]{:S(2)}, u32[]{:S(2)}) collective-permute-start(bf16[144,256]{1,0:T(8,128)(2,1)S(1)} %get-tuple-element.38), channel_id=1, source_target_pairs={{0,192},{64,0},{128,64},{192,128},{1,193},{65,1},{129,65},{193,129... | collective-permute-start | bytes 221192 | tf_op jit(solution)/shard_map/ppermute | solution.py:267
  20.2 9.0 %collective-permute-start.3 = (bf16[4,144,256]{2,1,0:T(8,128)(2,1)S(1)}, bf16[4,144,256]{2,1,0:T(8,128)(2,1)S(1)}, u32[]{:S(2)}, u32[]{:S(2)}) collective-permute-start(bf16[4,144,256]{2,1,0:T(8,128)(2,1)S(1)} %pad_maximum_fusion.2), channel_id=1, source_target_pairs={{0,1},{1,0},{2,3},{3,2},{4,5},{5,4},{6,7},{7,6},{8,9},{9,8},{10,11... | collective-permute-start | bytes 884744 | tf_op jit(solution)/shard_map/ppermute | solution.py:271
  29.2 20.4 %copy-start.5 = (bf16[8,144,256]{2,1,0:T(8,128)(2,1)}, bf16[8,144,256]{2,1,0:T(8,128)(2,1)S(1)}, u32[]{:S(2)}) copy-start(bf16[8,144,256]{2,1,0:T(8,128)(2,1)S(1)} %constant_dynamic-update-slice_fusion.kv0) | copy-start | bytes 1769476
  29.2 29.7 %all-to-all-start = ((bf16[4,128,1024]{2,1,0:T(8,128)(2,1)}), bf16[4,128,1024]{2,1,0:T(8,128)(2,1)S(1)}, u32[]{:S(2)}, u32[]{:S(2)}) async-start(bf16[4,128,1024]{2,1,0:T(8,128)(2,1)} %bitcast.5), calls=%async_computation | async-start | bytes 2097152 | tf_op jit(solution)/shard_map/all_to_all | solution.py:275
  33.8 15.4 %collective-permute-start.5 = (bf16[8,144,256]{2,1,0:T(8,128)(2,1)S(1)}, bf16[8,144,256]{2,1,0:T(8,128)(2,1)S(1)}, u32[]{:S(2)}, u32[]{:S(2)}) collective-permute-start(bf16[8,144,256]{2,1,0:T(8,128)(2,1)S(1)} %constant_dynamic-update-slice_fusion.kv0), channel_id=1, source_target_pairs={{0,16},{16,32},{32,48},{48,0},{1,17},{17,33},{33,49},{49,1},{2,18}... | collective-permute-start | bytes 1769480 | tf_op jit(solution)/shard_map/ppermute | solution.py:285
  35.4 14.2 %collective-permute-start.4 = (bf16[8,144,256]{2,1,0:T(8,128)(2,1)S(1)}, bf16[8,144,256]{2,1,0:T(8,128)(2,1)S(1)}, u32[]{:S(2)}, u32[]{:S(2)}) collective-permute-start(bf16[8,144,256]{2,1,0:T(8,128)(2,1)S(1)} %constant_dynamic-update-slice_fusion.kv0), channel_id=1, source_target_pairs={{0,48},{16,0},{32,16},{48,32},{1,49},{17,1},{33,17},{49,33},{2,50}... | collective-permute-start | bytes 1769480 | tf_op jit(solution)/shard_map/ppermute | solution.py:284
  49.2 0.8 copy-start.2
  49.2 8.2 %collective-permute-start.6 = (bf16[4,144,256]{2,1,0:T(8,128)(2,1)S(1)}, bf16[4,144,256]{2,1,0:T(8,128)(2,1)S(1)}, u32[]{:S(2)}, u32[]{:S(2)}) collective-permute-start(bf16[4,144,256]{2,1,0:T(8,128)(2,1)S(1)} %slice.52), channel_id=1, source_target_pairs={{0,16},{16,32},{32,48},{48,0},{1,17},{17,33},{33,49},{49,1},{2,18}... | collective-permute-start | bytes 884744 | tf_op jit(solution)/shard_map/ppermute | solution.py:287
  49.6 0.9 copy-start.3
  50.5 7.2 %collective-permute-start.7 = (bf16[4,144,256]{2,1,0:T(8,128)(2,1)S(1)}, bf16[4,144,256]{2,1,0:T(8,128)(2,1)S(1)}, u32[]{:S(2)}, u32[]{:S(2)}) collective-permute-start(bf16[4,144,256]{2,1,0:T(8,128)(2,1)S(1)} %slice.53), channel_id=1, source_target_pairs={{0,48},{16,0},{32,16},{48,32},{1,49},{17,1},{33,17},{49,33},{2,50}... | collective-permute-start | bytes 884744 | tf_op jit(solution)/shard_map/ppermute | solution.py:287
  57.7 1.2 copy-start.4
  58.9 7.4 %copy-start = (bf16[4,128,1024]{2,1,0:T(8,128)(2,1)}, bf16[4,128,1024]{2,1,0:T(8,128)(2,1)S(1)}, u32[]{:S(2)}) copy-start(bf16[4,128,1024]{2,1,0:T(8,128)(2,1)S(1)} %all-to-all-done.q_ref) | copy-start | bytes 3145732
  58.9 30.9 %all-to-all-start.2 = ((bf16[4,128,1024]{2,1,0:T(8,128)(2,1)}), bf16[4,128,1024]{2,1,0:T(8,128)(2,1)S(1)}, u32[]{:S(2)}, u32[]{:S(2)}) async-start(bf16[4,128,1024]{2,1,0:T(8,128)(2,1)} %bitcast.19), calls=%async_computation.2 | async-start | bytes 2097152 | tf_op jit(solution)/shard_map/all_to_all | solution.py:275
  89.8 7.2 %copy-start.1 = (bf16[4,128,1024]{2,1,0:T(8,128)(2,1)}, bf16[4,128,1024]{2,1,0:T(8,128)(2,1)S(1)}, u32[]{:S(2)}) copy-start(bf16[4,128,1024]{2,1,0:T(8,128)(2,1)S(1)} %all-to-all-done.2.g_ref) | copy-start | bytes 3145732
  89.8 39.8 %all-to-all-start.1 = ((bf16[4,128,1024]{2,1,0:T(8,128)(2,1)}), bf16[4,128,1024]{2,1,0:T(8,128)(2,1)S(1)}, u32[]{:S(2)}, u32[]{:S(2)}) async-start(bf16[4,128,1024]{2,1,0:T(8,128)(2,1)} %get-tuple-element.17.o_ref), calls=%async_computation.1 | async-start | bytes 2097152 | tf_op jit(solution)/shard_map/all_to_all | solution.py:275
  125.8 13.2 %collective-permute-start.10 = (bf16[4,128,256]{2,1,0:T(8,128)(2,1)S(1)}, bf16[4,128,256]{2,1,0:T(8,128)(2,1)S(1)}, u32[]{:S(2)}, u32[]{:S(2)}) collective-permute-start(bf16[4,128,256]{2,1,0:T(8,128)(2,1)S(1)} %get-tuple-element.35), channel_id=1, source_target_pairs={{0,48},{16,0},{32,16},{48,32},{1,49},{17,1},{33,17},{49,33},{2,50}... | collective-permute-start | bytes 786440 | tf_op jit(solution)/shard_map/ppermute | solution.py:299
  129.6 31.0 %all-to-all-start.3 = ((bf16[4,128,1024]{2,1,0:T(8,128)(2,1)}), bf16[4,128,1024]{2,1,0:T(8,128)(2,1)S(1)}, u32[]{:S(2)}, u32[]{:S(2)}) async-start(bf16[4,128,1024]{2,1,0:T(8,128)(2,1)} %get-tuple-element.22), calls=%async_computation.3 | async-start | bytes 2097152 | tf_op jit(solution)/shard_map/all_to_all | solution.py:275
  138.7 8.3 %collective-permute-start.8 = (bf16[4,128,256]{2,1,0:T(8,128)(2,1)S(1)}, bf16[4,128,256]{2,1,0:T(8,128)(2,1)S(1)}, u32[]{:S(2)}, u32[]{:S(2)}) collective-permute-start(bf16[4,128,256]{2,1,0:T(8,128)(2,1)S(1)} %get-tuple-element.34), channel_id=1, source_target_pairs={{0,16},{16,32},{32,48},{48,0},{1,17},{17,33},{33,49},{49,1},{2,18}... | collective-permute-start | bytes 786440 | tf_op jit(solution)/shard_map/ppermute | solution.py:298
  140.1 10.1 %collective-permute-start.11 = (bf16[8,128,256]{2,1,0:T(8,128)(2,1)S(1)}, bf16[8,128,256]{2,1,0:T(8,128)(2,1)S(1)}, u32[]{:S(2)}, u32[]{:S(2)}) collective-permute-start(bf16[8,128,256]{2,1,0:T(8,128)(2,1)S(1)} %pad_maximum_fusion.1), channel_id=1, source_target_pairs={{0,48},{16,0},{32,16},{48,32},{1,49},{17,1},{33,17},{49,33},{2,50}... | collective-permute-start | bytes 1572872 | tf_op jit(solution)/shard_map/ppermute | solution.py:303
  148.1 10.5 %collective-permute-start.9 = (bf16[8,128,256]{2,1,0:T(8,128)(2,1)S(1)}, bf16[8,128,256]{2,1,0:T(8,128)(2,1)S(1)}, u32[]{:S(2)}, u32[]{:S(2)}) collective-permute-start(bf16[8,128,256]{2,1,0:T(8,128)(2,1)S(1)} %pad_maximum_fusion), channel_id=1, source_target_pairs={{0,16},{16,32},{32,48},{48,0},{1,17},{17,33},{33,49},{49,1},{2,18}... | collective-permute-start | bytes 1572872 | tf_op jit(solution)/shard_map/ppermute | solution.py:302
  160.6 20.6 %all-to-all-start.4 = ((bf16[8,128,256]{2,1,0:T(8,128)(2,1)}), bf16[8,128,256]{2,1,0:T(8,128)(2,1)}, u32[]{:S(2)}, u32[]{:S(2)}) async-start(bf16[8,128,256]{2,1,0:T(8,128)(2,1)} %add_convert_fusion), calls=%async_computation.4 | async-start | bytes 1048576 | tf_op jit(solution)/shard_map/all_to_all | solution.py:342

commit v5 on v4

--- a/solution.py
+++ b/solution.py
@@ -37,6 +37,13 @@
         ref[i, :, k * DH : (k + 1) * DH] = value[:, k * ROWS : (k + 1) * ROWS].T
 
 
+def twice(count, step, carry):
+    carry = lax.fori_loop(
+        0, count // 2, lambda j, c: step(2 * j + 1, step(2 * j, c)), carry
+    )
+    return lax.fori_loop(count // 2 * 2, count, step, carry)
+
+
 def fold(x, op):
     return op(x.reshape(x.shape[0] // 8, 8, x.shape[1]), axis=0)
 
@@ -90,7 +97,7 @@
             s_buf[j] = s
             return jnp.maximum(top, fold(s, jnp.max))
 
-        top = lax.fori_loop(0, b, first, jnp.full((8, COLS), NEGATIVE, F32))
+        top = twice(b, first, jnp.full((8, COLS), NEGATIVE, F32))
         s = jnp.dot(k_n[b], q_t, preferred_element_type=F32)
         q_marks = jnp.broadcast_to(row_marks(kv0, z), (ROWS, ROWS))
         for rel in range(NY):
@@ -118,7 +125,7 @@
             pltpu.make_async_copy(p_buf.at[tile], p_hbm.at[tile], sems.at[tile]).start()
             return total
 
-        total = lax.fori_loop(0, b + 1, second, jnp.zeros((8, COLS), F32))
+        total = twice(b + 1, second, jnp.zeros((8, COLS), F32))
         inv = 1.0 / jnp.sum(total, axis=0, keepdims=True)
         unflip(o_ref, i, (out_acc[...] * inv).astype(BF16))
         stat_ref[i] = inv
@@ -135,11 +142,12 @@
 
 def backward(
     turn, q_ref, g_ref, o_ref, stat_ref, kv0, kv1, kv2, kv3, p_hbm,
-    dq_ref, out0, out1, out2, out3,
+    dq_ref, low0, low1, low2, low3, high0, high1, high2, high3,
     slots, p_buf, k_t, v_n, acc, dq_acc, sems,
 ):
     pieces = (kv0, kv1, kv2, kv3)
-    outs = (out0, out1, out2, out3)
+    lows = (low0, low1, low2, low3)
+    highs = (high0, high1, high2, high3)
     set_slots(slots)
 
     def fetch(tile, carry):
@@ -181,7 +189,7 @@
             dq_acc[...] += jnp.dot(k_t[j], ds, preferred_element_type=F32)
             return carry
 
-        lax.fori_loop(0, b + 1, step, 0)
+        twice(b + 1, step, 0)
         unflip(dq_ref, i, (dq_acc[...] * (inv * SCALE)).astype(BF16))
         return base + b + 1
 
@@ -190,10 +198,15 @@
     def finish(b, carry):
         slot = jnp.bitwise_xor(slots[b], NH * turn[0])
         z = (slot % NH) * 2 + jnp.bitwise_xor(slot // NH, turn[2])
-        for rel in range(NY):
-            cut = slice(rel * ROWS, (rel + 1) * ROWS)
-            outs[rel][z, :, :DH] = (acc[b, cut, :DH] * SCALE).astype(BF16)
-            outs[rel][z, :, DH:] = acc[b, cut, DH:].astype(BF16)
+
+        def store(outs, z):
+            for rel in range(NY):
+                cut = slice(rel * ROWS, (rel + 1) * ROWS)
+                outs[rel][z, :, :DH] = (acc[b, cut, :DH] * SCALE).astype(BF16)
+                outs[rel][z, :, DH:] = acc[b, cut, DH:].astype(BF16)
+
+        pl.when(z < NH)(lambda: store(lows, z))
+        pl.when(z >= NH)(lambda: store(highs, z - NH))
         return carry
 
     lax.fori_loop(0, NZ, finish, 0)
@@ -203,7 +216,7 @@
 SMEM = pl.BlockSpec(memory_space=pltpu.SMEM)
 ANY = pl.BlockSpec(memory_space=pl.ANY)
 WIDE = jax.ShapeDtypeStruct((NH, ROWS, COLS), BF16)
-NARROW = jax.ShapeDtypeStruct((NZ, ROWS, 2 * DH), BF16)
+NARROW = jax.ShapeDtypeStruct((NH, ROWS, 2 * DH), BF16)
 WEIGHTS = jax.ShapeDtypeStruct((TILES, BLOCK, COLS), BF16)
 STATS = jax.ShapeDtypeStruct((NH, 1, COLS), F32)
 PARAMS = pltpu.CompilerParams(vmem_limit_bytes=56 * 1024 * 1024)
@@ -242,9 +255,9 @@
     return pl.pallas_call(
         backward,
         name="backward",
-        out_shape=(WIDE, NARROW, NARROW, NARROW, NARROW),
+        out_shape=(WIDE,) + (NARROW,) * (2 * NY),
         in_specs=[SMEM] + [VMEM] * 8 + [ANY],
-        out_specs=[VMEM] * 5,
+        out_specs=[VMEM] * (1 + 2 * NY),
         scratch_shapes=[
             pltpu.SMEM((NZ,), jnp.int32),
             pltpu.VMEM((TILES, BLOCK, COLS), BF16),
@@ -294,14 +307,19 @@
 
 
 def scatter_y(own, up, far, down):
-    half = own.shape[0] // 2
-    from_down = lax.ppermute(far[:half], "y", ring(1))
-    from_up = lax.ppermute(far[half:], "y", ring(-1))
-    up = jnp.concatenate([add(up[:half], from_down), up[half:]])
-    down = jnp.concatenate([down[:half], add(down[half:], from_up)])
-    up = lax.ppermute(up, "y", ring(1))
-    down = lax.ppermute(down, "y", ring(-1))
-    return (own.astype(F32) + (up.astype(F32) + down.astype(F32))).astype(BF16)
+    from_down = lax.ppermute(far[0], "y", ring(1))
+    from_up = lax.ppermute(far[1], "y", ring(-1))
+    up = (lax.ppermute(add(up[0], from_down), "y", ring(1)), lax.ppermute(up[1], "y", ring(1)))
+    down = (
+        lax.ppermute(down[0], "y", ring(-1)),
+        lax.ppermute(add(down[1], from_up), "y", ring(-1)),
+    )
+    return jnp.concatenate(
+        [
+            (o.astype(F32) + (u.astype(F32) + d.astype(F32))).astype(BF16)
+            for o, u, d in zip(own, up, down)
+        ]
+    )
 
 
 def chunks(x):
@@ -335,10 +353,10 @@
     q = exchange(after(chunks(queries), kv))
     g = exchange(after(chunks(grad_out), q, *pieces))
     out, stat, weights = run_forward(turn, q, pieces)
-    dq, d0, d1, d2, d3 = run_backward(turn, q, g, out, stat, pieces, weights)
+    dq, *halves = run_backward(turn, q, g, out, stat, pieces, weights)
     out = exchange(out)
     dq = exchange(after(dq, out))
-    dkv = after(scatter_y(d0, d1, d2, d3), dq)
+    dkv = after(scatter_y(*zip(halves[:NY], halves[NY:])), dq)
     dkv = lax.all_to_all(dkv, ("zhi", "outer"), split_axis=0, concat_axis=0, tiled=True)
     dkv = dkv.reshape(NH, 2, ROWS, 2 * DH)
     dkv = add(dkv[:, 0], dkv[:, 1])

time: 185 us -> 177 us (0.957)
  waiting for transfers between devices: 48.9 us -> 45 us
  Pallas kernels: 51.2 us -> 48.1 us
  local copies, waits for them, and re-layouts: 17.8 us -> 14.7 us
    ppermute x4 -> x6, waiting for transfers between devices: 14 us -> 7.76 us  [the longest x1 2.92 us: scatter_y(): lax.ppermute(add(up[0], from_down), 'y', ring(1))]
    slice x3 -> x0, local copies, waits for them, and re-layouts: 3 us -> none  [the longest x1 1.07 us: scatter_y(): from_down = lax.ppermute(far[:half], 'y', ring(1))]
    ppermute x4 -> x6, starting transfers between devices: 7.41 us -> 9.87 us  [the longest x1 2.85 us: scatter_y(): lax.ppermute(add(down[1], from_up), 'y', ring(-1))]
    pallas_call x1, Pallas kernels: 23.5 us -> 21.5 us  [run_forward(): pl.pallas_call(forward, name='forward', out_shape=(WIDE, STATS, WEIGHTS),...]
  transfers between devices with their start and end apart: 17 -> 19, of which waited for: 10 -> 13; matrix products, arithmetic and copies ran while one was open for 10% -> 9% of each run, Pallas kernels for 28% -> 27%
where the time goes in v5:
time: 177 us; the launch traced here: 176 us
  starting transfers between devices  59.5 us (34%)
  Pallas kernels  48.1 us (27%)
  waiting for transfers between devices  45 us (25%)
  local copies, waits for them, and re-layouts  14.7 us (8%)
  other arithmetic  7.52 us (4%)
    pallas_call x1, Pallas kernels, run_backward(): pl.pallas_call(backward, name='backward', out_shape=(WIDE,) + (NARROW,) *...  26.7 us
    all_to_all x4, starting transfers between devices, exchange(): return lax.all_to_all(x, 'zhi', split_axis=0, concat_axis=0, tiled=True)  24.5 us
    pallas_call x1, Pallas kernels, run_forward(): pl.pallas_call(forward, name='forward', out_shape=(WIDE, STATS, WEIGHTS),...  21.5 us
    ppermute x1, waiting for transfers between devices, gather_y(): down = lax.ppermute(kv, 'y', ring(1))  12.2 us
    ppermute x3, starting transfers between devices, hop(): return lax.ppermute(x, 'zhi', [(i, (i + step) % NH) for i in range(NH)])  11.4 us
    all_to_all x1, waiting for transfers between devices, shards(): lax.all_to_all(dkv, ('zhi', 'outer'), split_axis=0, concat_axis=0, tiled=...  10.5 us
    ppermute x1, waiting for transfers between devices, swap(): return lax.ppermute(x, 'outer', [(0, 1), (1, 0)])  8.87 us
    unnamed x24, local copies, waits for them, and re-layouts  8.78 us
  transfers between devices with their start and end apart: 19, of which 13 were waited for; matrix products, arithmetic and copies ran while one was open for 9% of the time, Pallas kernels for 27%

profile of v5, /device:TPU:2, one launch (start us, length us, event | category | flops | bytes accessed | tf_op | source)
XLA Modules:
  0.0 176.0 jit_solution(14363013214415630160)
XLA Ops:
  0.7 0.7 fusion.9
  1.4 1.0 copy.13
  2.4 0.1 copy.15
  2.5 1.0 copy.14
  3.6 0.1 copy.16
  3.8 3.3 %collective-permute-start.2 = (bf16[144,256]{1,0:T(8,128)(2,1)S(1)}, bf16[144,256]{1,0:T(8,128)(2,1)S(1)}, u32[]{:S(2)}, u32[]{:S(2)}) collective-permute-start(bf16[144,256]{1,0:T(8,128)(2,1)S(1)} %get-tuple-element.42), channel_id=1, source_target_pairs={{0,64},{64,128},{128,192},{192,0},{1,65},{65,129},{129,193},{193,1... | collective-permute-start | bytes 221192 | tf_op jit(solution)/shard_map/ppermute | solution.py:280
  7.2 5.4 %collective-permute-start.1 = (bf16[144,256]{1,0:T(8,128)(2,1)S(1)}, bf16[144,256]{1,0:T(8,128)(2,1)S(1)}, u32[]{:S(2)}, u32[]{:S(2)}) collective-permute-start(bf16[144,256]{1,0:T(8,128)(2,1)S(1)} %get-tuple-element.43), channel_id=1, source_target_pairs={{0,128},{64,192},{128,0},{192,64},{1,129},{65,193},{129,1},{193,65... | collective-permute-start | bytes 221192 | tf_op jit(solution)/shard_map/ppermute | solution.py:280
  12.6 2.7 %collective-permute-start = (bf16[144,256]{1,0:T(8,128)(2,1)S(1)}, bf16[144,256]{1,0:T(8,128)(2,1)S(1)}, u32[]{:S(2)}, u32[]{:S(2)}) collective-permute-start(bf16[144,256]{1,0:T(8,128)(2,1)S(1)} %get-tuple-element.44), channel_id=1, source_target_pairs={{0,192},{64,0},{128,64},{192,128},{1,193},{65,1},{129,65},{193,129... | collective-permute-start | bytes 221192 | tf_op jit(solution)/shard_map/ppermute | solution.py:280
  15.2 1.6 copy.11
  16.8 1.3 copy.12
  18.2 0.0 collective-permute-done.2
  18.2 1.9 %collective-permute-done = bf16[144,256]{1,0:T(8,128)(2,1)S(1)} collective-permute-done((bf16[144,256]{1,0:T(8,128)(2,1)S(1)}, bf16[144,256]{1,0:T(8,128)(2,1)S(1)}, u32[]{:S(2)}, u32[]{:S(2)}) %collective-permute-start) | collective-permute-done | bytes 73760 | tf_op jit(solution)/shard_map/ppermute | solution.py:280
  20.2 0.1 collective-permute-start.3
  20.3 8.9 %collective-permute-done.3 = bf16[4,144,256]{2,1,0:T(8,128)(2,1)S(1)} collective-permute-done((bf16[4,144,256]{2,1,0:T(8,128)(2,1)S(1)}, bf16[4,144,256]{2,1,0:T(8,128)(2,1)S(1)}, u32[]{:S(2)}, u32[]{:S(2)}) %collective-permute-start.3) | collective-permute-done | bytes 294944 | tf_op jit(solution)/shard_map/ppermute | solution.py:284
  29.2 4.6 %all-to-all-start = ((bf16[4,128,1024]{2,1,0:T(8,128)(2,1)}), bf16[4,128,1024]{2,1,0:T(8,128)(2,1)S(1)}, u32[]{:S(2)}, u32[]{:S(2)}) async-start(bf16[4,128,1024]{2,1,0:T(8,128)(2,1)} %bitcast.5), calls=%async_computation | async-start | bytes 2097152 | tf_op jit(solution)/shard_map/all_to_all | solution.py:288
  33.8 1.6 collective-permute-start.5
  35.4 1.7 collective-permute-start.4
  37.1 12.2 %collective-permute-done.5.kv3 = bf16[8,144,256]{2,1,0:T(8,128)(2,1)S(1)} collective-permute-done((bf16[8,144,256]{2,1,0:T(8,128)(2,1)S(1)}, bf16[8,144,256]{2,1,0:T(8,128)(2,1)S(1)}, u32[]{:S(2)}, u32[]{:S(2)}) %collective-permute-start.5) | collective-permute-done | bytes 589856 | tf_op jit(solution)/shard_map/ppermute | solution.py:298
  49.2 0.4 collective-permute-start.6
  49.6 0.0 collective-permute-done.4.kv1
  49.7 0.4 copy-done.2
  50.0 0.4 copy-done.3
  50.5 2.9 %collective-permute-start.7 = (bf16[4,144,256]{2,1,0:T(8,128)(2,1)S(1)}, bf16[4,144,256]{2,1,0:T(8,128)(2,1)S(1)}, u32[]{:S(2)}, u32[]{:S(2)}) collective-permute-start(bf16[4,144,256]{2,1,0:T(8,128)(2,1)S(1)} %slice.29), channel_id=1, source_target_pairs={{0,48},{16,0},{32,16},{48,32},{1,49},{17,1},{33,17},{49,33},{2,50}... | collective-permute-start | bytes 884744 | tf_op jit(solution)/shard_map/ppermute | solution.py:300
  53.4 1.6 copy.18
  55.0 1.3 copy.19
  56.3 1.1 collective-permute-done.6
  57.5 0.2 collective-permute-done.7
  57.7 1.2 all-to-all-done.q_ref
  58.9 6.5 %all-to-all-start.2 = ((bf16[4,128,1024]{2,1,0:T(8,128)(2,1)}), bf16[4,128,1024]{2,1,0:T(8,128)(2,1)S(1)}, u32[]{:S(2)}, u32[]{:S(2)}) async-start(bf16[4,128,1024]{2,1,0:T(8,128)(2,1)} %bitcast.19), calls=%async_computation.2 | async-start | bytes 2097152 | tf_op jit(solution)/shard_map/all_to_all | solution.py:288
  65.6 0.6 pad_add_fusion.turn
  66.2 21.5 %forward.1 = (bf16[4,128,1024]{2,1,0:T(8,128)(2,1)}, f32[4,1,1024]{2,1,0:T(1,128)}, bf16[18,512,1024]{2,1,0:T(8,128)(2,1)}) custom-call(s32[3]{0:T(128)} %pad_add_fusion.turn, bf16[4,128,1024]{2,1,0:T(8,128)(2,1)} %copy-done, bf16[8,144,256]{2,1,0:T(8,128)(2,1)} %copy-done.5, bf16[8,144,256]{2,1,0:T(8,128)(2,1)} %copy-done.3, ...), custom_call_target="tpu_custom_call" | custom-call | flops 9663676416 | bytes 25165824 | tf_op jit(solution)/shard_map/forward/pallas_call | solution.py:234
  87.7 1.1 all-to-all-done.2.g_ref
  88.8 6.1 %all-to-all-start.1 = ((bf16[4,128,1024]{2,1,0:T(8,128)(2,1)}), bf16[4,128,1024]{2,1,0:T(8,128)(2,1)S(1)}, u32[]{:S(2)}, u32[]{:S(2)}) async-start(bf16[4,128,1024]{2,1,0:T(8,128)(2,1)} %get-tuple-element.21.o_ref), calls=%async_computation.1 | async-start | bytes 2097152 | tf_op jit(solution)/shard_map/all_to_all | solution.py:288
  94.9 26.7 %backward.1 = (bf16[4,128,1024]{2,1,0:T(8,128)(2,1)}, bf16[4,128,256]{2,1,0:T(8,128)(2,1)}, bf16[4,128,256]{2,1,0:T(8,128)(2,1)}, bf16[4,128,256]{2,1,0:T(8,128)...) custom-call(s32[3]{0:T(128)} %pad_add_fusion.turn, ...), custom_call_target="tpu_custom_call" | custom-call | flops 19327352832 | bytes 25165824 | tf_op jit(solution)/shard_map/backward/pallas_call | solution.py:255
  121.6 0.0 all-to-all-done.1
  121.6 7.2 %all-to-all-start.3 = ((bf16[4,128,1024]{2,1,0:T(8,128)(2,1)}), bf16[4,128,1024]{2,1,0:T(8,128)(2,1)S(1)}, u32[]{:S(2)}, u32[]{:S(2)}) async-start(bf16[4,128,1024]{2,1,0:T(8,128)(2,1)} %get-tuple-element.26), calls=%async_computation.3 | async-start | bytes 2097152 | tf_op jit(solution)/shard_map/all_to_all | solution.py:288
  128.8 1.1 collective-permute-start.8
  129.9 2.6 %collective-permute-start.12 = (bf16[4,128,256]{2,1,0:T(8,128)(2,1)}, bf16[4,128,256]{2,1,0:T(8,128)(2,1)S(1)}, u32[]{:S(2)}, u32[]{:S(2)}) collective-permute-start(bf16[4,128,256]{2,1,0:T(8,128)(2,1)} %get-tuple-element.34), channel_id=1, source_target_pairs={{0,48},{16,0},{32,16},{48,32},{1,49},{17,1},{33,17},{49,33},{2,50}... | collective-permute-start | bytes 786440 | tf_op jit(solution)/shard_map/ppermute | solution.py:311
  132.5 2.0 %collective-permute-start.10 = (bf16[4,128,256]{2,1,0:T(8,128)(2,1)}, bf16[4,128,256]{2,1,0:T(8,128)(2,1)S(1)}, u32[]{:S(2)}, u32[]{:S(2)}) collective-permute-start(bf16[4,128,256]{2,1,0:T(8,128)(2,1)} %get-tuple-element.30), channel_id=1, source_target_pairs={{0,48},{16,0},{32,16},{48,32},{1,49},{17,1},{33,17},{49,33},{2,50}... | collective-permute-start | bytes 786440 | tf_op jit(solution)/shard_map/ppermute | solution.py:314
  134.5 2.5 %collective-permute-done.8 = bf16[4,128,256]{2,1,0:T(8,128)(2,1)S(1)} collective-permute-done((bf16[4,128,256]{2,1,0:T(8,128)(2,1)}, bf16[4,128,256]{2,1,0:T(8,128)(2,1)S(1)}, u32[]{:S(2)}, u32[]{:S(2)}) %collective-permute-start.8) | collective-permute-done | bytes 262176 | tf_op jit(solution)/shard_map/ppermute | solution.py:310
  137.0 1.0 add_convert_fusion.4
  138.1 0.1 collective-permute-start.9
  138.2 1.2 collective-permute-start.11
  139.4 1.0 add_convert_fusion.2
  140.4 2.8 %collective-permute-start.13 = (bf16[4,128,256]{2,1,0:T(8,128)(2,1)S(1)}, bf16[4,128,256]{2,1,0:T(8,128)(2,1)S(1)}, u32[]{:S(2)}, u32[]{:S(2)}) collective-permute-start(bf16[4,128,256]{2,1,0:T(8,128)(2,1)S(1)} %add_convert_fusion.2), channel_id=1, source_target_pairs={{0,48},{16,0},{32,16},{48,32},{1,49},{17,1},{33,17},{49,33},{2,50}... | collective-permute-start | bytes 786440 | tf_op jit(solution)/shard_map/ppermute | solution.py:315
  143.3 0.6 collective-permute-done.10
  143.8 2.9 %collective-permute-done.9 = bf16[4,128,256]{2,1,0:T(8,128)(2,1)S(1)} collective-permute-done((bf16[4,128,256]{2,1,0:T(8,128)(2,1)S(1)}, bf16[4,128,256]{2,1,0:T(8,128)(2,1)S(1)}, u32[]{:S(2)}, u32[]{:S(2)}) %collective-permute-start.9) | collective-permute-done | bytes 262176 | tf_op jit(solution)/shard_map/ppermute | solution.py:312
  146.7 1.1 add_convert_fusion.3
  147.8 1.7 collective-permute-done.11
  149.5 0.0 collective-permute-done.13
  149.5 1.1 add_convert_fusion.1
  150.6 0.8 pad_maximum_fusion
  151.4 0.1 all-to-all-done.3
  151.5 7.1 %all-to-all-start.4 = ((bf16[8,128,256]{2,1,0:T(8,128)(2,1)}), bf16[8,128,256]{2,1,0:T(8,128)(2,1)}, u32[]{:S(2)}, u32[]{:S(2)}) async-start(bf16[8,128,256]{2,1,0:T(8,128)(2,1)} %pad_maximum_fusion), calls=%async_computation.4 | async-start | bytes 1048576 | tf_op jit(solution)/shard_map/all_to_all | solution.py:360
  158.7 0.7 copy.17
  159.3 1.3 copy.23
  160.6 0.7 copy.20
  161.3 1.3 copy.24
  162.6 10.5 %all-to-all-done.4 = bf16[8,128,256]{2,1,0:T(8,128)(2,1)} async-done(((bf16[8,128,256]{2,1,0:T(8,128)(2,1)}), bf16[8,128,256]{2,1,0:T(8,128)(2,1)}, u32[]{:S(2)}, u32[]{:S(2)}) %all-to-all-start.4) | async-done | bytes 524320 | tf_op jit(solution)/shard_map/all_to_all | solution.py:360
  173.2 1.1 fusion
  174.3 0.1 copy.22
  174.4 0.7 reshape.31
  175.1 0.1 copy.21
  175.2 0.7 reshape.30
  (28 shorter events, 0.3 us)
Async XLA Ops:
  0.6 64.8 %copy-start.6 = (s32[1,128]{1,0:T(1,128)S(1)}, s32[1,128]{1,0:T(1,128)}, u32[]{:S(2)}) copy-start(s32[1,128]{1,0:T(1,128)} %param.9) | copy-start | bytes 1540
  3.8 14.3 %collective-permute-start.2 = (bf16[144,256]{1,0:T(8,128)(2,1)S(1)}, bf16[144,256]{1,0:T(8,128)(2,1)S(1)}, u32[]{:S(2)}, u32[]{:S(2)}) collective-permute-start(bf16[144,256]{1,0:T(8,128)(2,1)S(1)} %get-tuple-element.42), channel_id=1, source_target_pairs={{0,64},{64,128},{128,192},{192,0},{1,65},{65,129},{129,193},{193,1... | collective-permute-start | bytes 221192 | tf_op jit(solution)/shard_map/ppermute | solution.py:280
  7.2 11.0 %collective-permute-start.1 = (bf16[144,256]{1,0:T(8,128)(2,1)S(1)}, bf16[144,256]{1,0:T(8,128)(2,1)S(1)}, u32[]{:S(2)}, u32[]{:S(2)}) collective-permute-start(bf16[144,256]{1,0:T(8,128)(2,1)S(1)} %get-tuple-element.43), channel_id=1, source_target_pairs={{0,128},{64,192},{128,0},{192,64},{1,129},{65,193},{129,1},{193,65... | collective-permute-start | bytes 221192 | tf_op jit(solution)/shard_map/ppermute | solution.py:280
  12.6 7.5 %collective-permute-start = (bf16[144,256]{1,0:T(8,128)(2,1)S(1)}, bf16[144,256]{1,0:T(8,128)(2,1)S(1)}, u32[]{:S(2)}, u32[]{:S(2)}) collective-permute-start(bf16[144,256]{1,0:T(8,128)(2,1)S(1)} %get-tuple-element.44), channel_id=1, source_target_pairs={{0,192},{64,0},{128,64},{192,128},{1,193},{65,1},{129,65},{193,129... | collective-permute-start | bytes 221192 | tf_op jit(solution)/shard_map/ppermute | solution.py:280
  20.2 9.0 %collective-permute-start.3 = (bf16[4,144,256]{2,1,0:T(8,128)(2,1)S(1)}, bf16[4,144,256]{2,1,0:T(8,128)(2,1)S(1)}, u32[]{:S(2)}, u32[]{:S(2)}) collective-permute-start(bf16[4,144,256]{2,1,0:T(8,128)(2,1)S(1)} %pad_maximum_fusion.1), channel_id=1, source_target_pairs={{0,1},{1,0},{2,3},{3,2},{4,5},{5,4},{6,7},{7,6},{8,9},{9,8},{10,11... | collective-permute-start | bytes 884744 | tf_op jit(solution)/shard_map/ppermute | solution.py:284
  29.2 20.4 %copy-start.5 = (bf16[8,144,256]{2,1,0:T(8,128)(2,1)}, bf16[8,144,256]{2,1,0:T(8,128)(2,1)S(1)}, u32[]{:S(2)}) copy-start(bf16[8,144,256]{2,1,0:T(8,128)(2,1)S(1)} %constant_dynamic-update-slice_fusion.kv0) | copy-start | bytes 1769476
  29.2 29.7 %all-to-all-start = ((bf16[4,128,1024]{2,1,0:T(8,128)(2,1)}), bf16[4,128,1024]{2,1,0:T(8,128)(2,1)S(1)}, u32[]{:S(2)}, u32[]{:S(2)}) async-start(bf16[4,128,1024]{2,1,0:T(8,128)(2,1)} %bitcast.5), calls=%async_computation | async-start | bytes 2097152 | tf_op jit(solution)/shard_map/all_to_all | solution.py:288
  33.8 15.4 %collective-permute-start.5 = (bf16[8,144,256]{2,1,0:T(8,128)(2,1)S(1)}, bf16[8,144,256]{2,1,0:T(8,128)(2,1)S(1)}, u32[]{:S(2)}, u32[]{:S(2)}) collective-permute-start(bf16[8,144,256]{2,1,0:T(8,128)(2,1)S(1)} %constant_dynamic-update-slice_fusion.kv0), channel_id=1, source_target_pairs={{0,16},{16,32},{32,48},{48,0},{1,17},{17,33},{33,49},{49,1},{2,18}... | collective-permute-start | bytes 1769480 | tf_op jit(solution)/shard_map/ppermute | solution.py:298
  35.4 14.2 %collective-permute-start.4 = (bf16[8,144,256]{2,1,0:T(8,128)(2,1)S(1)}, bf16[8,144,256]{2,1,0:T(8,128)(2,1)S(1)}, u32[]{:S(2)}, u32[]{:S(2)}) collective-permute-start(bf16[8,144,256]{2,1,0:T(8,128)(2,1)S(1)} %constant_dynamic-update-slice_fusion.kv0), channel_id=1, source_target_pairs={{0,48},{16,0},{32,16},{48,32},{1,49},{17,1},{33,17},{49,33},{2,50}... | collective-permute-start | bytes 1769480 | tf_op jit(solution)/shard_map/ppermute | solution.py:297
  49.2 0.8 copy-start.2
  49.2 8.2 %collective-permute-start.6 = (bf16[4,144,256]{2,1,0:T(8,128)(2,1)S(1)}, bf16[4,144,256]{2,1,0:T(8,128)(2,1)S(1)}, u32[]{:S(2)}, u32[]{:S(2)}) collective-permute-start(bf16[4,144,256]{2,1,0:T(8,128)(2,1)S(1)} %slice.28), channel_id=1, source_target_pairs={{0,16},{16,32},{32,48},{48,0},{1,17},{17,33},{33,49},{49,1},{2,18}... | collective-permute-start | bytes 884744 | tf_op jit(solution)/shard_map/ppermute | solution.py:300
  49.6 0.8 copy-start.3
  50.5 7.2 %collective-permute-start.7 = (bf16[4,144,256]{2,1,0:T(8,128)(2,1)S(1)}, bf16[4,144,256]{2,1,0:T(8,128)(2,1)S(1)}, u32[]{:S(2)}, u32[]{:S(2)}) collective-permute-start(bf16[4,144,256]{2,1,0:T(8,128)(2,1)S(1)} %slice.29), channel_id=1, source_target_pairs={{0,48},{16,0},{32,16},{48,32},{1,49},{17,1},{33,17},{49,33},{2,50}... | collective-permute-start | bytes 884744 | tf_op jit(solution)/shard_map/ppermute | solution.py:300
  57.7 1.2 copy-start.4
  58.9 7.3 %copy-start = (bf16[4,128,1024]{2,1,0:T(8,128)(2,1)}, bf16[4,128,1024]{2,1,0:T(8,128)(2,1)S(1)}, u32[]{:S(2)}) copy-start(bf16[4,128,1024]{2,1,0:T(8,128)(2,1)S(1)} %all-to-all-done.q_ref) | copy-start | bytes 3145732
  58.9 29.9 %all-to-all-start.2 = ((bf16[4,128,1024]{2,1,0:T(8,128)(2,1)}), bf16[4,128,1024]{2,1,0:T(8,128)(2,1)S(1)}, u32[]{:S(2)}, u32[]{:S(2)}) async-start(bf16[4,128,1024]{2,1,0:T(8,128)(2,1)} %bitcast.19), calls=%async_computation.2 | async-start | bytes 2097152 | tf_op jit(solution)/shard_map/all_to_all | solution.py:288
  88.8 6.1 %copy-start.1 = (bf16[4,128,1024]{2,1,0:T(8,128)(2,1)}, bf16[4,128,1024]{2,1,0:T(8,128)(2,1)S(1)}, u32[]{:S(2)}) copy-start(bf16[4,128,1024]{2,1,0:T(8,128)(2,1)S(1)} %all-to-all-done.2.g_ref) | copy-start | bytes 3145732
  88.8 32.8 %all-to-all-start.1 = ((bf16[4,128,1024]{2,1,0:T(8,128)(2,1)}), bf16[4,128,1024]{2,1,0:T(8,128)(2,1)S(1)}, u32[]{:S(2)}, u32[]{:S(2)}) async-start(bf16[4,128,1024]{2,1,0:T(8,128)(2,1)} %get-tuple-element.21.o_ref), calls=%async_computation.1 | async-start | bytes 2097152 | tf_op jit(solution)/shard_map/all_to_all | solution.py:288
  121.6 29.9 %all-to-all-start.3 = ((bf16[4,128,1024]{2,1,0:T(8,128)(2,1)}), bf16[4,128,1024]{2,1,0:T(8,128)(2,1)S(1)}, u32[]{:S(2)}, u32[]{:S(2)}) async-start(bf16[4,128,1024]{2,1,0:T(8,128)(2,1)} %get-tuple-element.26), calls=%async_computation.3 | async-start | bytes 2097152 | tf_op jit(solution)/shard_map/all_to_all | solution.py:288
  128.8 8.2 %collective-permute-start.8 = (bf16[4,128,256]{2,1,0:T(8,128)(2,1)}, bf16[4,128,256]{2,1,0:T(8,128)(2,1)S(1)}, u32[]{:S(2)}, u32[]{:S(2)}) collective-permute-start(bf16[4,128,256]{2,1,0:T(8,128)(2,1)} %get-tuple-element.29), channel_id=1, source_target_pairs={{0,16},{16,32},{32,48},{48,0},{1,17},{17,33},{33,49},{49,1},{2,18}... | collective-permute-start | bytes 786440 | tf_op jit(solution)/shard_map/ppermute | solution.py:310
  129.9 9.5 %collective-permute-start.12 = (bf16[4,128,256]{2,1,0:T(8,128)(2,1)}, bf16[4,128,256]{2,1,0:T(8,128)(2,1)S(1)}, u32[]{:S(2)}, u32[]{:S(2)}) collective-permute-start(bf16[4,128,256]{2,1,0:T(8,128)(2,1)} %get-tuple-element.34), channel_id=1, source_target_pairs={{0,48},{16,0},{32,16},{48,32},{1,49},{17,1},{33,17},{49,33},{2,50}... | collective-permute-start | bytes 786440 | tf_op jit(solution)/shard_map/ppermute | solution.py:311
  132.5 11.3 %collective-permute-start.10 = (bf16[4,128,256]{2,1,0:T(8,128)(2,1)}, bf16[4,128,256]{2,1,0:T(8,128)(2,1)S(1)}, u32[]{:S(2)}, u32[]{:S(2)}) collective-permute-start(bf16[4,128,256]{2,1,0:T(8,128)(2,1)} %get-tuple-element.30), channel_id=1, source_target_pairs={{0,48},{16,0},{32,16},{48,32},{1,49},{17,1},{33,17},{49,33},{2,50}... | collective-permute-start | bytes 786440 | tf_op jit(solution)/shard_map/ppermute | solution.py:314
  138.1 8.7 %collective-permute-start.9 = (bf16[4,128,256]{2,1,0:T(8,128)(2,1)S(1)}, bf16[4,128,256]{2,1,0:T(8,128)(2,1)S(1)}, u32[]{:S(2)}, u32[]{:S(2)}) collective-permute-start(bf16[4,128,256]{2,1,0:T(8,128)(2,1)S(1)} %add_convert_fusion.4), channel_id=1, source_target_pairs={{0,16},{16,32},{32,48},{48,0},{1,17},{17,33},{33,49},{49,1},{2,18}... | collective-permute-start | bytes 786440 | tf_op jit(solution)/shard_map/ppermute | solution.py:312
  138.2 11.4 %collective-permute-start.11 = (bf16[4,128,256]{2,1,0:T(8,128)(2,1)}, bf16[4,128,256]{2,1,0:T(8,128)(2,1)S(1)}, u32[]{:S(2)}, u32[]{:S(2)}) collective-permute-start(bf16[4,128,256]{2,1,0:T(8,128)(2,1)} %get-tuple-element.32), channel_id=1, source_target_pairs={{0,16},{16,32},{32,48},{48,0},{1,17},{17,33},{33,49},{49,1},{2,18}... | collective-permute-start | bytes 786440 | tf_op jit(solution)/shard_map/ppermute | solution.py:312
  140.4 9.1 %collective-permute-start.13 = (bf16[4,128,256]{2,1,0:T(8,128)(2,1)S(1)}, bf16[4,128,256]{2,1,0:T(8,128)(2,1)S(1)}, u32[]{:S(2)}, u32[]{:S(2)}) collective-permute-start(bf16[4,128,256]{2,1,0:T(8,128)(2,1)S(1)} %add_convert_fusion.2), channel_id=1, source_target_pairs={{0,48},{16,0},{32,16},{48,32},{1,49},{17,1},{33,17},{49,33},{2,50}... | collective-permute-start | bytes 786440 | tf_op jit(solution)/shard_map/ppermute | solution.py:315
  151.5 21.6 %all-to-all-start.4 = ((bf16[8,128,256]{2,1,0:T(8,128)(2,1)}), bf16[8,128,256]{2,1,0:T(8,128)(2,1)}, u32[]{:S(2)}, u32[]{:S(2)}) async-start(bf16[8,128,256]{2,1,0:T(8,128)(2,1)} %pad_maximum_fusion), calls=%async_computation.4 | async-start | bytes 1048576 | tf_op jit(solution)/shard_map/all_to_all | solution.py:360

commit v6 on v5

--- a/solution.py
+++ b/solution.py
@@ -332,25 +332,22 @@
 
 def shards(queries, keys, values, grad_out, positions):
     here = lax.axis_index("zhi").astype(jnp.int32)
-    kv = jnp.concatenate(
-        [keys[0].reshape(ROWS, KVH, DH), values[0].reshape(ROWS, KVH, DH)], axis=2
-    ).transpose(1, 0, 2)
     marks = jnp.concatenate([positions[0] // 64, positions[0] % 64]).astype(BF16)
-    marks = jnp.broadcast_to(marks, (KVH, PADDED - ROWS, 2 * DH))
-    kv = jnp.concatenate([kv, marks], axis=1)
-    own = positions[0, 0] // (2 * BLOCK)
+    marks = jnp.broadcast_to(marks, (PADDED - ROWS, 2 * DH))
+    own = lax.shift_right_logical(positions[0, 0], int(math.log2(2 * BLOCK)))
     own = jnp.where(here < NH // 2, own, NH - 1 - own).astype(jnp.int32)
     parts = []
     for step in range(NH):
-        part = lax.dynamic_index_in_dim(
-            kv, jnp.bitwise_and(here - step, NH - 1), 0, keepdims=False
-        )
+        start = jnp.bitwise_and(here - step, NH - 1) * DH
+        heads = [lax.dynamic_slice(x[0], (0, start), (ROWS, DH)) for x in (keys, values)]
+        part = jnp.concatenate([jnp.concatenate(heads, axis=1), marks])
         parts.append(hop(part, -step) if step else part)
     kv = jnp.stack(parts)
     turn = jnp.stack([own, here, lax.axis_index("outer").astype(jnp.int32)])
     kv = jnp.concatenate([kv, swap(kv)])
     pieces = gather_y(kv)
-    q = exchange(after(chunks(queries), kv))
+    q, turn, _ = lax.optimization_barrier((chunks(queries), turn, kv))
+    q = exchange(q)
     g = exchange(after(chunks(grad_out), q, *pieces))
     out, stat, weights = run_forward(turn, q, pieces)
     dq, *halves = run_backward(turn, q, g, out, stat, pieces, weights)
@@ -360,9 +357,8 @@
     dkv = lax.all_to_all(dkv, ("zhi", "outer"), split_axis=0, concat_axis=0, tiled=True)
     dkv = dkv.reshape(NH, 2, ROWS, 2 * DH)
     dkv = add(dkv[:, 0], dkv[:, 1])
-    dkv = dkv.transpose(1, 0, 2)
-    dk = dkv[:, :, :DH].reshape(1, ROWS, KVH * DH)
-    dv = dkv[:, :, DH:].reshape(1, ROWS, KVH * DH)
+    dk = jnp.concatenate([dkv[n, :, :DH] for n in range(KVH)], axis=1)[None]
+    dv = jnp.concatenate([dkv[n, :, DH:] for n in range(KVH)], axis=1)[None]
     return rows(out), rows(dq), dk, dv
 
 

time: 177 us -> 173 us (0.977)
  waiting for transfers between devices: 45 us -> 40 us
  local copies, waits for them, and re-layouts: 14.7 us -> 12.5 us
  starting transfers between devices: 59.5 us -> 61.5 us
    ppermute x1, waiting for transfers between devices: 8.87 us -> 5.33 us  [swap(): return lax.ppermute(x, 'outer', [(0, 1), (1, 0)])]
    ppermute x1, waiting for transfers between devices: 2.53 us -> 4.41 us  [scatter_y(): from_down = lax.ppermute(far[0], 'y', ring(1))]
    unnamed x24 -> x20, local copies, waits for them, and re-layouts: 8.78 us -> 7.51 us
  transfers between devices with their start and end apart: 19 -> 19, of which waited for: 13 -> 10; matrix products, arithmetic and copies ran while one was open for 9% -> 9% of each run, Pallas kernels for 27% -> 28%
where the time goes in v6:
time: 173 us; the launch traced here: 172 us
  starting transfers between devices  61.5 us (36%)
  Pallas kernels  48.1 us (28%)
  waiting for transfers between devices  40 us (23%)
  local copies, waits for them, and re-layouts  12.5 us (7%)
  other arithmetic  8.79 us (5%)
    pallas_call x1, Pallas kernels, run_backward(): pl.pallas_call(backward, name='backward', out_shape=(WIDE,) + (NARROW,) *...  26.7 us
    all_to_all x4, starting transfers between devices, exchange(): return lax.all_to_all(x, 'zhi', split_axis=0, concat_axis=0, tiled=True)  25.6 us
    pallas_call x1, Pallas kernels, run_forward(): pl.pallas_call(forward, name='forward', out_shape=(WIDE, STATS, WEIGHTS),...  21.5 us
    ppermute x1, waiting for transfers between devices, gather_y(): down = lax.ppermute(kv, 'y', ring(1))  11.2 us
    ppermute x3, starting transfers between devices, hop(): return lax.ppermute(x, 'zhi', [(i, (i + step) % NH) for i in range(NH)])  10.2 us
    all_to_all x1, waiting for transfers between devices, shards(): lax.all_to_all(dkv, ('zhi', 'outer'), split_axis=0, concat_axis=0, tiled=...  9.45 us
    all_to_all x1, starting transfers between devices, shards(): lax.all_to_all(dkv, ('zhi', 'outer'), split_axis=0, concat_axis=0, tiled=...  7.53 us
    unnamed x20, local copies, waits for them, and re-layouts  7.51 us
  transfers between devices with their start and end apart: 19, of which 10 were waited for; matrix products, arithmetic and copies ran while one was open for 9% of the time, Pallas kernels for 28%

profile of v6, /device:TPU:2, one launch (start us, length us, event | category | flops | bytes accessed | tf_op | source)
XLA Modules:
  0.0 172.4 jit_solution(9434804831793290877)
XLA Ops:
  0.6 0.7 fusion.3
  1.3 0.9 dynamic-slice_bitcast_fusion
  2.3 6.4 %collective-permute-start = (bf16[144,256]{1,0:T(8,128)(2,1)S(1)}, bf16[144,256]{1,0:T(8,128)(2,1)S(1)}, u32[]{:S(2)}, u32[]{:S(2)}) collective-permute-start(bf16[144,256]{1,0:T(8,128)(2,1)S(1)} %get-tuple-element.59), channel_id=1, source_target_pairs={{0,192},{64,0},{128,64},{192,128},{1,193},{65,1},{129,65},{193,129... | collective-permute-start | bytes 221192 | tf_op jit(solution)/shard_map/ppermute | solution.py:280
  8.7 1.0 collective-permute-start.1
  9.7 2.8 %collective-permute-start.2 = (bf16[144,256]{1,0:T(8,128)(2,1)S(1)}, bf16[144,256]{1,0:T(8,128)(2,1)S(1)}, u32[]{:S(2)}, u32[]{:S(2)}) collective-permute-start(bf16[144,256]{1,0:T(8,128)(2,1)S(1)} %get-tuple-element.61), channel_id=1, source_target_pairs={{0,64},{64,128},{128,192},{192,0},{1,65},{65,129},{129,193},{193,1... | collective-permute-start | bytes 221192 | tf_op jit(solution)/shard_map/ppermute | solution.py:280
  13.1 1.6 copy.11
  14.8 1.3 copy.12
  16.1 0.6 pad_add_fusion.turn
  16.7 0.0 collective-permute-done
  16.7 1.7 collective-permute-done.1
  18.4 0.0 collective-permute-done.2
  18.4 1.7 collective-permute-start.3
  20.1 5.3 %collective-permute-done.3 = bf16[4,144,256]{2,1,0:T(8,128)(2,1)S(1)} collective-permute-done((bf16[4,144,256]{2,1,0:T(8,128)(2,1)S(1)}, bf16[4,144,256]{2,1,0:T(8,128)(2,1)S(1)}, u32[]{:S(2)}, u32[]{:S(2)}) %collective-permute-start.3) | collective-permute-done | bytes 294944 | tf_op jit(solution)/shard_map/ppermute | solution.py:284
  25.5 6.8 %all-to-all-start = ((bf16[4,128,1024]{2,1,0:T(8,128)(2,1)}), bf16[4,128,1024]{2,1,0:T(8,128)(2,1)S(1)}, u32[]{:S(2)}, u32[]{:S(2)}) async-start(bf16[4,128,1024]{2,1,0:T(8,128)(2,1)} %bitcast.1), calls=%async_computation | async-start | bytes 2097152 | tf_op jit(solution)/shard_map/all_to_all | solution.py:288
  32.3 1.6 collective-permute-start.5
  33.8 1.7 collective-permute-start.4
  35.5 11.2 %collective-permute-done.5.kv3 = bf16[8,144,256]{2,1,0:T(8,128)(2,1)S(1)} collective-permute-done((bf16[8,144,256]{2,1,0:T(8,128)(2,1)S(1)}, bf16[8,144,256]{2,1,0:T(8,128)(2,1)S(1)}, u32[]{:S(2)}, u32[]{:S(2)}) %collective-permute-start.5) | collective-permute-done | bytes 589856 | tf_op jit(solution)/shard_map/ppermute | solution.py:298
  46.7 0.6 collective-permute-start.6
  47.3 0.0 collective-permute-done.4.kv1
  47.3 0.2 copy-done.2
  47.5 0.6 copy-done.3
  48.1 2.7 %collective-permute-start.7 = (bf16[4,144,256]{2,1,0:T(8,128)(2,1)S(1)}, bf16[4,144,256]{2,1,0:T(8,128)(2,1)S(1)}, u32[]{:S(2)}, u32[]{:S(2)}) collective-permute-start(bf16[4,144,256]{2,1,0:T(8,128)(2,1)S(1)} %slice.53), channel_id=1, source_target_pairs={{0,48},{16,0},{32,16},{48,32},{1,49},{17,1},{33,17},{49,33},{2,50}... | collective-permute-start | bytes 884744 | tf_op jit(solution)/shard_map/ppermute | solution.py:300
  50.9 1.6 copy.14
  52.5 1.3 copy.15
  53.8 0.9 collective-permute-done.6
  54.7 0.4 collective-permute-done.7
  55.2 0.0 all-to-all-done.q_ref
  55.2 0.0 copy-start
  55.2 0.8 copy-done.4
  56.0 6.9 %all-to-all-start.2 = ((bf16[4,128,1024]{2,1,0:T(8,128)(2,1)}), bf16[4,128,1024]{2,1,0:T(8,128)(2,1)S(1)}, u32[]{:S(2)}, u32[]{:S(2)}) async-start(bf16[4,128,1024]{2,1,0:T(8,128)(2,1)} %bitcast.22), calls=%async_computation.2 | async-start | bytes 2097152 | tf_op jit(solution)/shard_map/all_to_all | solution.py:288
  62.9 21.5 %forward.1 = (bf16[4,128,1024]{2,1,0:T(8,128)(2,1)}, f32[4,1,1024]{2,1,0:T(1,128)}, bf16[18,512,1024]{2,1,0:T(8,128)(2,1)}) custom-call(s32[3]{0:T(128)} %pad_add_fusion.turn, bf16[4,128,1024]{2,1,0:T(8,128)(2,1)} %copy-done, bf16[8,144,256]{2,1,0:T(8,128)(2,1)} %copy-done.5, bf16[8,144,256]{2,1,0:T(8,128)(2,1)} %copy-done.3, ...), custom_call_target="tpu_custom_call" | custom-call | flops 9663676416 | bytes 25165824 | tf_op jit(solution)/shard_map/forward/pallas_call | solution.py:234
  84.4 2.5 %all-to-all-done.2.g_ref = bf16[4,128,1024]{2,1,0:T(8,128)(2,1)S(1)} async-done(((bf16[4,128,1024]{2,1,0:T(8,128)(2,1)}), bf16[4,128,1024]{2,1,0:T(8,128)(2,1)S(1)}, u32[]{:S(2)}, u32[]{:S(2)}) %all-to-all-start.2) | async-done | bytes 1048608 | tf_op jit(solution)/shard_map/all_to_all | solution.py:288
  86.9 4.7 %all-to-all-start.1 = ((bf16[4,128,1024]{2,1,0:T(8,128)(2,1)}), bf16[4,128,1024]{2,1,0:T(8,128)(2,1)S(1)}, u32[]{:S(2)}, u32[]{:S(2)}) async-start(bf16[4,128,1024]{2,1,0:T(8,128)(2,1)} %get-tuple-element.23.o_ref), calls=%async_computation.1 | async-start | bytes 2097152 | tf_op jit(solution)/shard_map/all_to_all | solution.py:288
  91.6 0.0 copy-done.1
  91.6 26.7 %backward.1 = (bf16[4,128,1024]{2,1,0:T(8,128)(2,1)}, bf16[4,128,256]{2,1,0:T(8,128)(2,1)}, bf16[4,128,256]{2,1,0:T(8,128)(2,1)}, bf16[4,128,256]{2,1,0:T(8,128)...) custom-call(s32[3]{0:T(128)} %pad_add_fusion.turn, ...), custom_call_target="tpu_custom_call" | custom-call | flops 19327352832 | bytes 25165824 | tf_op jit(solution)/shard_map/backward/pallas_call | solution.py:255
  118.3 0.0 all-to-all-done.1
  118.3 7.2 %all-to-all-start.3 = ((bf16[4,128,1024]{2,1,0:T(8,128)(2,1)}), bf16[4,128,1024]{2,1,0:T(8,128)(2,1)S(1)}, u32[]{:S(2)}, u32[]{:S(2)}) async-start(bf16[4,128,1024]{2,1,0:T(8,128)(2,1)} %get-tuple-element.28), calls=%async_computation.3 | async-start | bytes 2097152 | tf_op jit(solution)/shard_map/all_to_all | solution.py:288
  125.5 1.6 collective-permute-start.8
  127.1 2.0 %collective-permute-start.12 = (bf16[4,128,256]{2,1,0:T(8,128)(2,1)}, bf16[4,128,256]{2,1,0:T(8,128)(2,1)S(1)}, u32[]{:S(2)}, u32[]{:S(2)}) collective-permute-start(bf16[4,128,256]{2,1,0:T(8,128)(2,1)} %get-tuple-element.36), channel_id=1, source_target_pairs={{0,48},{16,0},{32,16},{48,32},{1,49},{17,1},{33,17},{49,33},{2,50}... | collective-permute-start | bytes 786440 | tf_op jit(solution)/shard_map/ppermute | solution.py:311
  129.2 2.0 %collective-permute-start.10 = (bf16[4,128,256]{2,1,0:T(8,128)(2,1)}, bf16[4,128,256]{2,1,0:T(8,128)(2,1)S(1)}, u32[]{:S(2)}, u32[]{:S(2)}) collective-permute-start(bf16[4,128,256]{2,1,0:T(8,128)(2,1)} %get-tuple-element.32), channel_id=1, source_target_pairs={{0,48},{16,0},{32,16},{48,32},{1,49},{17,1},{33,17},{49,33},{2,50}... | collective-permute-start | bytes 786440 | tf_op jit(solution)/shard_map/ppermute | solution.py:314
  131.2 4.4 %collective-permute-done.8 = bf16[4,128,256]{2,1,0:T(8,128)(2,1)S(1)} collective-permute-done((bf16[4,128,256]{2,1,0:T(8,128)(2,1)}, bf16[4,128,256]{2,1,0:T(8,128)(2,1)S(1)}, u32[]{:S(2)}, u32[]{:S(2)}) %collective-permute-start.8) | collective-permute-done | bytes 262176 | tf_op jit(solution)/shard_map/ppermute | solution.py:310
  135.6 1.0 add_convert_fusion.4
  136.6 0.9 collective-permute-start.9
  137.6 1.2 collective-permute-start.11
  138.8 0.0 collective-permute-done.12
  138.8 1.0 add_convert_fusion.2
  139.9 2.1 %collective-permute-start.13 = (bf16[4,128,256]{2,1,0:T(8,128)(2,1)S(1)}, bf16[4,128,256]{2,1,0:T(8,128)(2,1)S(1)}, u32[]{:S(2)}, u32[]{:S(2)}) collective-permute-start(bf16[4,128,256]{2,1,0:T(8,128)(2,1)S(1)} %add_convert_fusion.2), channel_id=1, source_target_pairs={{0,48},{16,0},{32,16},{48,32},{1,49},{17,1},{33,17},{49,33},{2,50}... | collective-permute-start | bytes 786440 | tf_op jit(solution)/shard_map/ppermute | solution.py:315
  141.9 0.0 collective-permute-done.10
  141.9 2.4 %collective-permute-done.9 = bf16[4,128,256]{2,1,0:T(8,128)(2,1)S(1)} collective-permute-done((bf16[4,128,256]{2,1,0:T(8,128)(2,1)S(1)}, bf16[4,128,256]{2,1,0:T(8,128)(2,1)S(1)}, u32[]{:S(2)}, u32[]{:S(2)}) %collective-permute-start.9) | collective-permute-done | bytes 262176 | tf_op jit(solution)/shard_map/ppermute | solution.py:312
  144.3 1.1 add_convert_fusion.3
  145.4 1.7 %collective-permute-done.11 = bf16[4,128,256]{2,1,0:T(8,128)(2,1)S(1)} collective-permute-done((bf16[4,128,256]{2,1,0:T(8,128)(2,1)}, bf16[4,128,256]{2,1,0:T(8,128)(2,1)S(1)}, u32[]{:S(2)}, u32[]{:S(2)}) %collective-permute-start.11) | collective-permute-done | bytes 262176 | tf_op jit(solution)/shard_map/ppermute | solution.py:312
  147.1 0.0 collective-permute-done.13
  147.1 1.1 add_convert_fusion.1
  148.2 0.8 pad_maximum_fusion
  149.0 0.0 all-to-all-done.3
  149.0 7.5 %all-to-all-start.4 = ((bf16[8,128,256]{2,1,0:T(8,128)(2,1)}), bf16[8,128,256]{2,1,0:T(8,128)(2,1)}, u32[]{:S(2)}, u32[]{:S(2)}) async-start(bf16[8,128,256]{2,1,0:T(8,128)(2,1)} %pad_maximum_fusion), calls=%async_computation.4 | async-start | bytes 1048576 | tf_op jit(solution)/shard_map/all_to_all | solution.py:357
  156.5 0.7 copy.13
  157.2 1.3 copy.19
  158.5 0.7 copy.16
  159.2 1.3 copy.20
  160.5 9.5 %all-to-all-done.4 = bf16[8,128,256]{2,1,0:T(8,128)(2,1)} async-done(((bf16[8,128,256]{2,1,0:T(8,128)(2,1)}), bf16[8,128,256]{2,1,0:T(8,128)(2,1)}, u32[]{:S(2)}, u32[]{:S(2)}) %all-to-all-start.4) | async-done | bytes 524320 | tf_op jit(solution)/shard_map/all_to_all | solution.py:357
  169.9 1.1 fusion
  171.1 0.7 maximum_bitcast_fusion.1
  171.8 0.7 maximum_bitcast_fusion
  (21 shorter events, 0.3 us)
Async XLA Ops:
  2.3 14.4 %collective-permute-start = (bf16[144,256]{1,0:T(8,128)(2,1)S(1)}, bf16[144,256]{1,0:T(8,128)(2,1)S(1)}, u32[]{:S(2)}, u32[]{:S(2)}) collective-permute-start(bf16[144,256]{1,0:T(8,128)(2,1)S(1)} %get-tuple-element.59), channel_id=1, source_target_pairs={{0,192},{64,0},{128,64},{192,128},{1,193},{65,1},{129,65},{193,129... | collective-permute-start | bytes 221192 | tf_op jit(solution)/shard_map/ppermute | solution.py:280
  8.7 9.7 %collective-permute-start.1 = (bf16[144,256]{1,0:T(8,128)(2,1)S(1)}, bf16[144,256]{1,0:T(8,128)(2,1)S(1)}, u32[]{:S(2)}, u32[]{:S(2)}) collective-permute-start(bf16[144,256]{1,0:T(8,128)(2,1)S(1)} %get-tuple-element.60), channel_id=1, source_target_pairs={{0,128},{64,192},{128,0},{192,64},{1,129},{65,193},{129,1},{193,65... | collective-permute-start | bytes 221192 | tf_op jit(solution)/shard_map/ppermute | solution.py:280
  9.7 8.7 %collective-permute-start.2 = (bf16[144,256]{1,0:T(8,128)(2,1)S(1)}, bf16[144,256]{1,0:T(8,128)(2,1)S(1)}, u32[]{:S(2)}, u32[]{:S(2)}) collective-permute-start(bf16[144,256]{1,0:T(8,128)(2,1)S(1)} %get-tuple-element.61), channel_id=1, source_target_pairs={{0,64},{64,128},{128,192},{192,0},{1,65},{65,129},{129,193},{193,1... | collective-permute-start | bytes 221192 | tf_op jit(solution)/shard_map/ppermute | solution.py:280
  18.4 7.1 %collective-permute-start.3 = (bf16[4,144,256]{2,1,0:T(8,128)(2,1)S(1)}, bf16[4,144,256]{2,1,0:T(8,128)(2,1)S(1)}, u32[]{:S(2)}, u32[]{:S(2)}) collective-permute-start(bf16[4,144,256]{2,1,0:T(8,128)(2,1)S(1)} %pad_maximum_fusion.1), channel_id=1, source_target_pairs={{0,1},{1,0},{2,3},{3,2},{4,5},{5,4},{6,7},{7,6},{8,9},{9,8},{10,11... | collective-permute-start | bytes 884744 | tf_op jit(solution)/shard_map/ppermute | solution.py:284
  25.5 21.8 %copy-start.5 = (bf16[8,144,256]{2,1,0:T(8,128)(2,1)}, bf16[8,144,256]{2,1,0:T(8,128)(2,1)S(1)}, u32[]{:S(2)}) copy-start(bf16[8,144,256]{2,1,0:T(8,128)(2,1)S(1)} %constant_dynamic-update-slice_fusion.kv0) | copy-start | bytes 1769476
  25.5 29.7 %all-to-all-start = ((bf16[4,128,1024]{2,1,0:T(8,128)(2,1)}), bf16[4,128,1024]{2,1,0:T(8,128)(2,1)S(1)}, u32[]{:S(2)}, u32[]{:S(2)}) async-start(bf16[4,128,1024]{2,1,0:T(8,128)(2,1)} %bitcast.1), calls=%async_computation | async-start | bytes 2097152 | tf_op jit(solution)/shard_map/all_to_all | solution.py:288
  32.3 14.4 %collective-permute-start.5 = (bf16[8,144,256]{2,1,0:T(8,128)(2,1)S(1)}, bf16[8,144,256]{2,1,0:T(8,128)(2,1)S(1)}, u32[]{:S(2)}, u32[]{:S(2)}) collective-permute-start(bf16[8,144,256]{2,1,0:T(8,128)(2,1)S(1)} %constant_dynamic-update-slice_fusion.kv0), channel_id=1, source_target_pairs={{0,16},{16,32},{32,48},{48,0},{1,17},{17,33},{33,49},{49,1},{2,18}... | collective-permute-start | bytes 1769480 | tf_op jit(solution)/shard_map/ppermute | solution.py:298
  33.8 13.5 %collective-permute-start.4 = (bf16[8,144,256]{2,1,0:T(8,128)(2,1)S(1)}, bf16[8,144,256]{2,1,0:T(8,128)(2,1)S(1)}, u32[]{:S(2)}, u32[]{:S(2)}) collective-permute-start(bf16[8,144,256]{2,1,0:T(8,128)(2,1)S(1)} %constant_dynamic-update-slice_fusion.kv0), channel_id=1, source_target_pairs={{0,48},{16,0},{32,16},{48,32},{1,49},{17,1},{33,17},{49,33},{2,50}... | collective-permute-start | bytes 1769480 | tf_op jit(solution)/shard_map/ppermute | solution.py:297
  46.7 0.8 copy-start.2
  46.7 8.0 %collective-permute-start.6 = (bf16[4,144,256]{2,1,0:T(8,128)(2,1)S(1)}, bf16[4,144,256]{2,1,0:T(8,128)(2,1)S(1)}, u32[]{:S(2)}, u32[]{:S(2)}) collective-permute-start(bf16[4,144,256]{2,1,0:T(8,128)(2,1)S(1)} %slice.52), channel_id=1, source_target_pairs={{0,16},{16,32},{32,48},{48,0},{1,17},{17,33},{33,49},{49,1},{2,18}... | collective-permute-start | bytes 884744 | tf_op jit(solution)/shard_map/ppermute | solution.py:300
  47.3 0.8 copy-start.3
  48.1 7.0 %collective-permute-start.7 = (bf16[4,144,256]{2,1,0:T(8,128)(2,1)S(1)}, bf16[4,144,256]{2,1,0:T(8,128)(2,1)S(1)}, u32[]{:S(2)}, u32[]{:S(2)}) collective-permute-start(bf16[4,144,256]{2,1,0:T(8,128)(2,1)S(1)} %slice.53), channel_id=1, source_target_pairs={{0,48},{16,0},{32,16},{48,32},{1,49},{17,1},{33,17},{49,33},{2,50}... | collective-permute-start | bytes 884744 | tf_op jit(solution)/shard_map/ppermute | solution.py:300
  55.1 0.8 copy-start.4
  55.2 7.7 %copy-start = (bf16[4,128,1024]{2,1,0:T(8,128)(2,1)}, bf16[4,128,1024]{2,1,0:T(8,128)(2,1)S(1)}, u32[]{:S(2)}) copy-start(bf16[4,128,1024]{2,1,0:T(8,128)(2,1)S(1)} %all-to-all-done.q_ref) | copy-start | bytes 3145732
  56.0 31.0 %all-to-all-start.2 = ((bf16[4,128,1024]{2,1,0:T(8,128)(2,1)}), bf16[4,128,1024]{2,1,0:T(8,128)(2,1)S(1)}, u32[]{:S(2)}, u32[]{:S(2)}) async-start(bf16[4,128,1024]{2,1,0:T(8,128)(2,1)} %bitcast.22), calls=%async_computation.2 | async-start | bytes 2097152 | tf_op jit(solution)/shard_map/all_to_all | solution.py:288
  86.9 4.7 %copy-start.1 = (bf16[4,128,1024]{2,1,0:T(8,128)(2,1)}, bf16[4,128,1024]{2,1,0:T(8,128)(2,1)S(1)}, u32[]{:S(2)}) copy-start(bf16[4,128,1024]{2,1,0:T(8,128)(2,1)S(1)} %all-to-all-done.2.g_ref) | copy-start | bytes 3145732
  86.9 31.4 %all-to-all-start.1 = ((bf16[4,128,1024]{2,1,0:T(8,128)(2,1)}), bf16[4,128,1024]{2,1,0:T(8,128)(2,1)S(1)}, u32[]{:S(2)}, u32[]{:S(2)}) async-start(bf16[4,128,1024]{2,1,0:T(8,128)(2,1)} %get-tuple-element.23.o_ref), calls=%async_computation.1 | async-start | bytes 2097152 | tf_op jit(solution)/shard_map/all_to_all | solution.py:288
  118.3 30.7 %all-to-all-start.3 = ((bf16[4,128,1024]{2,1,0:T(8,128)(2,1)}), bf16[4,128,1024]{2,1,0:T(8,128)(2,1)S(1)}, u32[]{:S(2)}, u32[]{:S(2)}) async-start(bf16[4,128,1024]{2,1,0:T(8,128)(2,1)} %get-tuple-element.28), calls=%async_computation.3 | async-start | bytes 2097152 | tf_op jit(solution)/shard_map/all_to_all | solution.py:288
  125.5 10.1 %collective-permute-start.8 = (bf16[4,128,256]{2,1,0:T(8,128)(2,1)}, bf16[4,128,256]{2,1,0:T(8,128)(2,1)S(1)}, u32[]{:S(2)}, u32[]{:S(2)}) collective-permute-start(bf16[4,128,256]{2,1,0:T(8,128)(2,1)} %get-tuple-element.31), channel_id=1, source_target_pairs={{0,16},{16,32},{32,48},{48,0},{1,17},{17,33},{33,49},{49,1},{2,18}... | collective-permute-start | bytes 786440 | tf_op jit(solution)/shard_map/ppermute | solution.py:310
  127.1 11.7 %collective-permute-start.12 = (bf16[4,128,256]{2,1,0:T(8,128)(2,1)}, bf16[4,128,256]{2,1,0:T(8,128)(2,1)S(1)}, u32[]{:S(2)}, u32[]{:S(2)}) collective-permute-start(bf16[4,128,256]{2,1,0:T(8,128)(2,1)} %get-tuple-element.36), channel_id=1, source_target_pairs={{0,48},{16,0},{32,16},{48,32},{1,49},{17,1},{33,17},{49,33},{2,50}... | collective-permute-start | bytes 786440 | tf_op jit(solution)/shard_map/ppermute | solution.py:311
  129.2 12.8 %collective-permute-start.10 = (bf16[4,128,256]{2,1,0:T(8,128)(2,1)}, bf16[4,128,256]{2,1,0:T(8,128)(2,1)S(1)}, u32[]{:S(2)}, u32[]{:S(2)}) collective-permute-start(bf16[4,128,256]{2,1,0:T(8,128)(2,1)} %get-tuple-element.32), channel_id=1, source_target_pairs={{0,48},{16,0},{32,16},{48,32},{1,49},{17,1},{33,17},{49,33},{2,50}... | collective-permute-start | bytes 786440 | tf_op jit(solution)/shard_map/ppermute | solution.py:314
  136.6 7.7 %collective-permute-start.9 = (bf16[4,128,256]{2,1,0:T(8,128)(2,1)S(1)}, bf16[4,128,256]{2,1,0:T(8,128)(2,1)S(1)}, u32[]{:S(2)}, u32[]{:S(2)}) collective-permute-start(bf16[4,128,256]{2,1,0:T(8,128)(2,1)S(1)} %add_convert_fusion.4), channel_id=1, source_target_pairs={{0,16},{16,32},{32,48},{48,0},{1,17},{17,33},{33,49},{49,1},{2,18}... | collective-permute-start | bytes 786440 | tf_op jit(solution)/shard_map/ppermute | solution.py:312
  137.6 9.5 %collective-permute-start.11 = (bf16[4,128,256]{2,1,0:T(8,128)(2,1)}, bf16[4,128,256]{2,1,0:T(8,128)(2,1)S(1)}, u32[]{:S(2)}, u32[]{:S(2)}) collective-permute-start(bf16[4,128,256]{2,1,0:T(8,128)(2,1)} %get-tuple-element.34), channel_id=1, source_target_pairs={{0,16},{16,32},{32,48},{48,0},{1,17},{17,33},{33,49},{49,1},{2,18}... | collective-permute-start | bytes 786440 | tf_op jit(solution)/shard_map/ppermute | solution.py:312
  139.9 7.3 %collective-permute-start.13 = (bf16[4,128,256]{2,1,0:T(8,128)(2,1)S(1)}, bf16[4,128,256]{2,1,0:T(8,128)(2,1)S(1)}, u32[]{:S(2)}, u32[]{:S(2)}) collective-permute-start(bf16[4,128,256]{2,1,0:T(8,128)(2,1)S(1)} %add_convert_fusion.2), channel_id=1, source_target_pairs={{0,48},{16,0},{32,16},{48,32},{1,49},{17,1},{33,17},{49,33},{2,50}... | collective-permute-start | bytes 786440 | tf_op jit(solution)/shard_map/ppermute | solution.py:315
  149.0 20.9 %all-to-all-start.4 = ((bf16[8,128,256]{2,1,0:T(8,128)(2,1)}), bf16[8,128,256]{2,1,0:T(8,128)(2,1)}, u32[]{:S(2)}, u32[]{:S(2)}) async-start(bf16[8,128,256]{2,1,0:T(8,128)(2,1)} %pad_maximum_fusion), calls=%async_computation.4 | async-start | bytes 1048576 | tf_op jit(solution)/shard_map/all_to_all | solution.py:357

commit v7 on v6

--- a/solution.py
+++ b/solution.py
@@ -219,7 +219,7 @@
 NARROW = jax.ShapeDtypeStruct((NH, ROWS, 2 * DH), BF16)
 WEIGHTS = jax.ShapeDtypeStruct((TILES, BLOCK, COLS), BF16)
 STATS = jax.ShapeDtypeStruct((NH, 1, COLS), F32)
-PARAMS = pltpu.CompilerParams(vmem_limit_bytes=56 * 1024 * 1024)
+PARAMS = pltpu.CompilerParams(vmem_limit_bytes=62 * 1024 * 1024)
 
 
 def cost(matmuls, exps):

time: 173 us -> 172 us (level)
  local copies, waits for them, and re-layouts: 12.5 us -> 14.7 us
    unnamed x20 -> x16, local copies, waits for them, and re-layouts: 7.51 us -> 8.38 us
  transfers between devices with their start and end apart: 19 -> 19, of which waited for: 10 -> 10; matrix products, arithmetic and copies ran while one was open for 9% -> 11% of each run, Pallas kernels for 28% -> 28%
where the time goes in v7:
time: 172 us; the launch traced here: 171 us
  starting transfers between devices  60 us (35%)
  Pallas kernels  48.2 us (28%)
  waiting for transfers between devices  39.2 us (23%)
  local copies, waits for them, and re-layouts  14.7 us (9%)
  other arithmetic  7.75 us (5%)
    pallas_call x1, Pallas kernels, run_backward(): pl.pallas_call(backward, name='backward', out_shape=(WIDE,) + (NARROW,) *...  26.7 us
    all_to_all x4, starting transfers between devices, exchange(): return lax.all_to_all(x, 'zhi', split_axis=0, concat_axis=0, tiled=True)  24.7 us
    pallas_call x1, Pallas kernels, run_forward(): pl.pallas_call(forward, name='forward', out_shape=(WIDE, STATS, WEIGHTS),...  21.5 us
    ppermute x1, waiting for transfers between devices, gather_y(): down = lax.ppermute(kv, 'y', ring(1))  11.2 us
    ppermute x3, starting transfers between devices, hop(): return lax.ppermute(x, 'zhi', [(i, (i + step) % NH) for i in range(NH)])  10.2 us
    unnamed x16, local copies, waits for them, and re-layouts  8.38 us
    all_to_all x1, waiting for transfers between devices, shards(): lax.all_to_all(dkv, ('zhi', 'outer'), split_axis=0, concat_axis=0, tiled=...  7.75 us
    all_to_all x1, starting transfers between devices, shards(): lax.all_to_all(dkv, ('zhi', 'outer'), split_axis=0, concat_axis=0, tiled=...  7.18 us
  transfers between devices with their start and end apart: 19, of which 10 were waited for; matrix products, arithmetic and copies ran while one was open for 11% of the time, Pallas kernels for 28%

profile of v7, /device:TPU:2, one launch (start us, length us, event | category | flops | bytes accessed | tf_op | source)
XLA Modules:
  0.0 171.2 jit_solution(6554967690015592494)
XLA Ops:
  0.6 0.7 fusion.3
  1.3 0.9 dynamic-slice_bitcast_fusion
  2.3 6.4 %collective-permute-start = (bf16[144,256]{1,0:T(8,128)(2,1)S(1)}, bf16[144,256]{1,0:T(8,128)(2,1)S(1)}, u32[]{:S(2)}, u32[]{:S(2)}) collective-permute-start(bf16[144,256]{1,0:T(8,128)(2,1)S(1)} %get-tuple-element.59), channel_id=1, source_target_pairs={{0,192},{64,0},{128,64},{192,128},{1,193},{65,1},{129,65},{193,129... | collective-permute-start | bytes 221192 | tf_op jit(solution)/shard_map/ppermute | solution.py:280
  8.7 1.0 collective-permute-start.1
  9.7 2.8 %collective-permute-start.2 = (bf16[144,256]{1,0:T(8,128)(2,1)S(1)}, bf16[144,256]{1,0:T(8,128)(2,1)S(1)}, u32[]{:S(2)}, u32[]{:S(2)}) collective-permute-start(bf16[144,256]{1,0:T(8,128)(2,1)S(1)} %get-tuple-element.61), channel_id=1, source_target_pairs={{0,64},{64,128},{128,192},{192,0},{1,65},{65,129},{129,193},{193,1... | collective-permute-start | bytes 221192 | tf_op jit(solution)/shard_map/ppermute | solution.py:280
  13.1 1.6 copy.11
  14.8 1.3 copy.12
  16.1 0.6 pad_add_fusion.turn
  16.7 0.0 collective-permute-done
  16.7 1.7 collective-permute-done.1
  18.4 0.0 collective-permute-done.2
  18.4 1.7 collective-permute-start.3
  20.1 5.3 %collective-permute-done.3 = bf16[4,144,256]{2,1,0:T(8,128)(2,1)S(1)} collective-permute-done((bf16[4,144,256]{2,1,0:T(8,128)(2,1)S(1)}, bf16[4,144,256]{2,1,0:T(8,128)(2,1)S(1)}, u32[]{:S(2)}, u32[]{:S(2)}) %collective-permute-start.3) | collective-permute-done | bytes 294944 | tf_op jit(solution)/shard_map/ppermute | solution.py:284
  25.5 0.0 copy-start.3
  25.5 6.8 %all-to-all-start = ((bf16[4,128,1024]{2,1,0:T(8,128)(2,1)}), bf16[4,128,1024]{2,1,0:T(8,128)(2,1)S(1)}, u32[]{:S(2)}, u32[]{:S(2)}) async-start(bf16[4,128,1024]{2,1,0:T(8,128)(2,1)} %bitcast.1), calls=%async_computation | async-start | bytes 2097152 | tf_op jit(solution)/shard_map/all_to_all | solution.py:288
  32.3 1.6 collective-permute-start.5
  33.8 1.7 collective-permute-start.4
  35.5 11.2 %collective-permute-done.5.kv3 = bf16[8,144,256]{2,1,0:T(8,128)(2,1)S(1)} collective-permute-done((bf16[8,144,256]{2,1,0:T(8,128)(2,1)S(1)}, bf16[8,144,256]{2,1,0:T(8,128)(2,1)S(1)}, u32[]{:S(2)}, u32[]{:S(2)}) %collective-permute-start.5) | collective-permute-done | bytes 589856 | tf_op jit(solution)/shard_map/ppermute | solution.py:298
  46.7 0.6 collective-permute-start.6
  47.3 0.0 collective-permute-done.4.kv1
  47.3 0.2 copy-done.1
  47.5 0.6 copy-done.2
  48.1 2.7 %collective-permute-start.7 = (bf16[4,144,256]{2,1,0:T(8,128)(2,1)S(1)}, bf16[4,144,256]{2,1,0:T(8,128)(2,1)S(1)}, u32[]{:S(2)}, u32[]{:S(2)}) collective-permute-start(bf16[4,144,256]{2,1,0:T(8,128)(2,1)S(1)} %slice.53), channel_id=1, source_target_pairs={{0,48},{16,0},{32,16},{48,32},{1,49},{17,1},{33,17},{49,33},{2,50}... | collective-permute-start | bytes 884744 | tf_op jit(solution)/shard_map/ppermute | solution.py:300
  50.9 1.6 copy.14
  52.5 1.3 copy.15
  53.8 0.9 collective-permute-done.6
  54.7 0.7 constant_dynamic-update-slice_fusion.6
  55.5 0.0 collective-permute-done.7
  55.5 0.8 constant_dynamic-update-slice_fusion.5.kv2
  56.2 0.0 all-to-all-done.q_ref
  56.2 6.9 %all-to-all-start.2 = ((bf16[4,128,1024]{2,1,0:T(8,128)(2,1)}), bf16[4,128,1024]{2,1,0:T(8,128)(2,1)}, u32[]{:S(2)}, u32[]{:S(2)}) async-start(bf16[4,128,1024]{2,1,0:T(8,128)(2,1)} %bitcast.22), calls=%async_computation.2 | async-start | bytes 2097152 | tf_op jit(solution)/shard_map/all_to_all | solution.py:288
  63.1 21.5 %forward.1 = (bf16[4,128,1024]{2,1,0:T(8,128)(2,1)}, f32[4,1,1024]{2,1,0:T(1,128)}, bf16[18,512,1024]{2,1,0:T(8,128)(2,1)}) custom-call(s32[3]{0:T(128)} %pad_add_fusion.turn, bf16[4,128,1024]{2,1,0:T(8,128)(2,1)} %copy-done, bf16[8,144,256]{2,1,0:T(8,128)(2,1)} %copy-done.3, bf16[8,144,256]{2,1,0:T(8,128)(2,1)} %copy-done.2, ...), custom_call_target="tpu_custom_call" | custom-call | flops 9663676416 | bytes 25165824 | tf_op jit(solution)/shard_map/forward/pallas_call | solution.py:234
  84.6 3.4 %all-to-all-done.2.g_ref = bf16[4,128,1024]{2,1,0:T(8,128)(2,1)} async-done(((bf16[4,128,1024]{2,1,0:T(8,128)(2,1)}), bf16[4,128,1024]{2,1,0:T(8,128)(2,1)}, u32[]{:S(2)}, u32[]{:S(2)}) %all-to-all-start.2) | async-done | bytes 1048608 | tf_op jit(solution)/shard_map/all_to_all | solution.py:288
  88.0 3.9 %all-to-all-start.1 = ((bf16[4,128,1024]{2,1,0:T(8,128)(2,1)}), bf16[4,128,1024]{2,1,0:T(8,128)(2,1)S(1)}, u32[]{:S(2)}, u32[]{:S(2)}) async-start(bf16[4,128,1024]{2,1,0:T(8,128)(2,1)} %get-tuple-element.23.o_ref), calls=%async_computation.1 | async-start | bytes 2097152 | tf_op jit(solution)/shard_map/all_to_all | solution.py:288
  91.9 26.7 %backward.1 = (bf16[4,128,1024]{2,1,0:T(8,128)(2,1)}, bf16[4,128,256]{2,1,0:T(8,128)(2,1)}, bf16[4,128,256]{2,1,0:T(8,128)(2,1)}, bf16[4,128,256]{2,1,0:T(8,128)...) custom-call(s32[3]{0:T(128)} %pad_add_fusion.turn, ...), custom_call_target="tpu_custom_call" | custom-call | flops 19327352832 | bytes 25165824 | tf_op jit(solution)/shard_map/backward/pallas_call | solution.py:255
  118.5 0.0 all-to-all-done.1
  118.5 7.2 %all-to-all-start.3 = ((bf16[4,128,1024]{2,1,0:T(8,128)(2,1)}), bf16[4,128,1024]{2,1,0:T(8,128)(2,1)S(1)}, u32[]{:S(2)}, u32[]{:S(2)}) async-start(bf16[4,128,1024]{2,1,0:T(8,128)(2,1)} %get-tuple-element.28), calls=%async_computation.3 | async-start | bytes 2097152 | tf_op jit(solution)/shard_map/all_to_all | solution.py:288
  125.8 1.3 collective-permute-start.8
  127.1 2.1 %collective-permute-start.12 = (bf16[4,128,256]{2,1,0:T(8,128)(2,1)}, bf16[4,128,256]{2,1,0:T(8,128)(2,1)S(1)}, u32[]{:S(2)}, u32[]{:S(2)}) collective-permute-start(bf16[4,128,256]{2,1,0:T(8,128)(2,1)} %get-tuple-element.36), channel_id=1, source_target_pairs={{0,48},{16,0},{32,16},{48,32},{1,49},{17,1},{33,17},{49,33},{2,50}... | collective-permute-start | bytes 786440 | tf_op jit(solution)/shard_map/ppermute | solution.py:311
  129.1 2.0 %collective-permute-start.10 = (bf16[4,128,256]{2,1,0:T(8,128)(2,1)}, bf16[4,128,256]{2,1,0:T(8,128)(2,1)S(1)}, u32[]{:S(2)}, u32[]{:S(2)}) collective-permute-start(bf16[4,128,256]{2,1,0:T(8,128)(2,1)} %get-tuple-element.32), channel_id=1, source_target_pairs={{0,48},{16,0},{32,16},{48,32},{1,49},{17,1},{33,17},{49,33},{2,50}... | collective-permute-start | bytes 786440 | tf_op jit(solution)/shard_map/ppermute | solution.py:314
  131.1 4.4 %collective-permute-done.8 = bf16[4,128,256]{2,1,0:T(8,128)(2,1)S(1)} collective-permute-done((bf16[4,128,256]{2,1,0:T(8,128)(2,1)}, bf16[4,128,256]{2,1,0:T(8,128)(2,1)S(1)}, u32[]{:S(2)}, u32[]{:S(2)}) %collective-permute-start.8) | collective-permute-done | bytes 262176 | tf_op jit(solution)/shard_map/ppermute | solution.py:310
  135.6 1.0 add_convert_fusion.4
  136.6 0.9 collective-permute-start.9
  137.5 1.2 collective-permute-start.11
  138.7 0.0 collective-permute-done.12
  138.8 1.0 add_convert_fusion.2
  139.8 2.1 %collective-permute-start.13 = (bf16[4,128,256]{2,1,0:T(8,128)(2,1)S(1)}, bf16[4,128,256]{2,1,0:T(8,128)(2,1)S(1)}, u32[]{:S(2)}, u32[]{:S(2)}) collective-permute-start(bf16[4,128,256]{2,1,0:T(8,128)(2,1)S(1)} %add_convert_fusion.2), channel_id=1, source_target_pairs={{0,48},{16,0},{32,16},{48,32},{1,49},{17,1},{33,17},{49,33},{2,50}... | collective-permute-start | bytes 786440 | tf_op jit(solution)/shard_map/ppermute | solution.py:315
  141.8 0.0 collective-permute-done.10
  141.8 2.4 %collective-permute-done.9 = bf16[4,128,256]{2,1,0:T(8,128)(2,1)S(1)} collective-permute-done((bf16[4,128,256]{2,1,0:T(8,128)(2,1)S(1)}, bf16[4,128,256]{2,1,0:T(8,128)(2,1)S(1)}, u32[]{:S(2)}, u32[]{:S(2)}) %collective-permute-start.9) | collective-permute-done | bytes 262176 | tf_op jit(solution)/shard_map/ppermute | solution.py:312
  144.2 1.1 add_convert_fusion.3
  145.3 1.7 %collective-permute-done.11 = bf16[4,128,256]{2,1,0:T(8,128)(2,1)S(1)} collective-permute-done((bf16[4,128,256]{2,1,0:T(8,128)(2,1)}, bf16[4,128,256]{2,1,0:T(8,128)(2,1)S(1)}, u32[]{:S(2)}, u32[]{:S(2)}) %collective-permute-start.11) | collective-permute-done | bytes 262176 | tf_op jit(solution)/shard_map/ppermute | solution.py:312
  147.0 0.0 collective-permute-done.13
  147.1 1.1 add_convert_fusion.1
  148.1 0.8 pad_maximum_fusion
  149.0 0.4 all-to-all-done.3
  149.3 7.2 %all-to-all-start.4 = ((bf16[8,128,256]{2,1,0:T(8,128)(2,1)}), bf16[8,128,256]{2,1,0:T(8,128)(2,1)S(1)}, u32[]{:S(2)}, u32[]{:S(2)}) async-start(bf16[8,128,256]{2,1,0:T(8,128)(2,1)} %pad_maximum_fusion), calls=%async_computation.4 | async-start | bytes 1048576 | tf_op jit(solution)/shard_map/all_to_all | solution.py:357
  156.5 1.3 copy.13
  157.8 2.3 %copy.19 = bf16[1,128,4096]{2,1,0:T(8,128)(2,1)} copy(bf16[1,128,4096]{1,2,0:T(8,128)(2,1)} %bitcast.89) | data formatting | bytes 2097152
  160.1 0.7 copy.16
  160.7 1.3 copy.20
  162.0 7.8 %all-to-all-done.4 = bf16[8,128,256]{2,1,0:T(8,128)(2,1)S(1)} async-done(((bf16[8,128,256]{2,1,0:T(8,128)(2,1)}), bf16[8,128,256]{2,1,0:T(8,128)(2,1)S(1)}, u32[]{:S(2)}, u32[]{:S(2)}) %all-to-all-start.4) | async-done | bytes 524320 | tf_op jit(solution)/shard_map/all_to_all | solution.py:357
  169.8 0.1 fusion
  169.9 0.7 maximum_bitcast_fusion.1
  170.6 0.7 maximum_bitcast_fusion
  (17 shorter events, 0.2 us)
Async XLA Ops:
  2.3 14.4 %collective-permute-start = (bf16[144,256]{1,0:T(8,128)(2,1)S(1)}, bf16[144,256]{1,0:T(8,128)(2,1)S(1)}, u32[]{:S(2)}, u32[]{:S(2)}) collective-permute-start(bf16[144,256]{1,0:T(8,128)(2,1)S(1)} %get-tuple-element.59), channel_id=1, source_target_pairs={{0,192},{64,0},{128,64},{192,128},{1,193},{65,1},{129,65},{193,129... | collective-permute-start | bytes 221192 | tf_op jit(solution)/shard_map/ppermute | solution.py:280
  8.7 9.7 %collective-permute-start.1 = (bf16[144,256]{1,0:T(8,128)(2,1)S(1)}, bf16[144,256]{1,0:T(8,128)(2,1)S(1)}, u32[]{:S(2)}, u32[]{:S(2)}) collective-permute-start(bf16[144,256]{1,0:T(8,128)(2,1)S(1)} %get-tuple-element.60), channel_id=1, source_target_pairs={{0,128},{64,192},{128,0},{192,64},{1,129},{65,193},{129,1},{193,65... | collective-permute-start | bytes 221192 | tf_op jit(solution)/shard_map/ppermute | solution.py:280
  9.7 8.7 %collective-permute-start.2 = (bf16[144,256]{1,0:T(8,128)(2,1)S(1)}, bf16[144,256]{1,0:T(8,128)(2,1)S(1)}, u32[]{:S(2)}, u32[]{:S(2)}) collective-permute-start(bf16[144,256]{1,0:T(8,128)(2,1)S(1)} %get-tuple-element.61), channel_id=1, source_target_pairs={{0,64},{64,128},{128,192},{192,0},{1,65},{65,129},{129,193},{193,1... | collective-permute-start | bytes 221192 | tf_op jit(solution)/shard_map/ppermute | solution.py:280
  18.4 7.1 %collective-permute-start.3 = (bf16[4,144,256]{2,1,0:T(8,128)(2,1)S(1)}, bf16[4,144,256]{2,1,0:T(8,128)(2,1)S(1)}, u32[]{:S(2)}, u32[]{:S(2)}) collective-permute-start(bf16[4,144,256]{2,1,0:T(8,128)(2,1)S(1)} %pad_maximum_fusion.1), channel_id=1, source_target_pairs={{0,1},{1,0},{2,3},{3,2},{4,5},{5,4},{6,7},{7,6},{8,9},{9,8},{10,11... | collective-permute-start | bytes 884744 | tf_op jit(solution)/shard_map/ppermute | solution.py:284
  25.5 21.8 %copy-start.3 = (bf16[8,144,256]{2,1,0:T(8,128)(2,1)}, bf16[8,144,256]{2,1,0:T(8,128)(2,1)S(1)}, u32[]{:S(2)}) copy-start(bf16[8,144,256]{2,1,0:T(8,128)(2,1)S(1)} %constant_dynamic-update-slice_fusion.kv0) | copy-start | bytes 1769476
  25.5 30.7 %all-to-all-start = ((bf16[4,128,1024]{2,1,0:T(8,128)(2,1)}), bf16[4,128,1024]{2,1,0:T(8,128)(2,1)S(1)}, u32[]{:S(2)}, u32[]{:S(2)}) async-start(bf16[4,128,1024]{2,1,0:T(8,128)(2,1)} %bitcast.1), calls=%async_computation | async-start | bytes 2097152 | tf_op jit(solution)/shard_map/all_to_all | solution.py:288
  32.3 14.4 %collective-permute-start.5 = (bf16[8,144,256]{2,1,0:T(8,128)(2,1)S(1)}, bf16[8,144,256]{2,1,0:T(8,128)(2,1)S(1)}, u32[]{:S(2)}, u32[]{:S(2)}) collective-permute-start(bf16[8,144,256]{2,1,0:T(8,128)(2,1)S(1)} %constant_dynamic-update-slice_fusion.kv0), channel_id=1, source_target_pairs={{0,16},{16,32},{32,48},{48,0},{1,17},{17,33},{33,49},{49,1},{2,18}... | collective-permute-start | bytes 1769480 | tf_op jit(solution)/shard_map/ppermute | solution.py:298
  33.8 13.5 %collective-permute-start.4 = (bf16[8,144,256]{2,1,0:T(8,128)(2,1)S(1)}, bf16[8,144,256]{2,1,0:T(8,128)(2,1)S(1)}, u32[]{:S(2)}, u32[]{:S(2)}) collective-permute-start(bf16[8,144,256]{2,1,0:T(8,128)(2,1)S(1)} %constant_dynamic-update-slice_fusion.kv0), channel_id=1, source_target_pairs={{0,48},{16,0},{32,16},{48,32},{1,49},{17,1},{33,17},{49,33},{2,50}... | collective-permute-start | bytes 1769480 | tf_op jit(solution)/shard_map/ppermute | solution.py:297
  46.7 0.8 copy-start.1
  46.7 8.0 %collective-permute-start.6 = (bf16[4,144,256]{2,1,0:T(8,128)(2,1)S(1)}, bf16[4,144,256]{2,1,0:T(8,128)(2,1)S(1)}, u32[]{:S(2)}, u32[]{:S(2)}) collective-permute-start(bf16[4,144,256]{2,1,0:T(8,128)(2,1)S(1)} %slice.52), channel_id=1, source_target_pairs={{0,16},{16,32},{32,48},{48,0},{1,17},{17,33},{33,49},{49,1},{2,18}... | collective-permute-start | bytes 884744 | tf_op jit(solution)/shard_map/ppermute | solution.py:300
  47.3 0.8 copy-start.2
  48.1 7.3 %collective-permute-start.7 = (bf16[4,144,256]{2,1,0:T(8,128)(2,1)S(1)}, bf16[4,144,256]{2,1,0:T(8,128)(2,1)S(1)}, u32[]{:S(2)}, u32[]{:S(2)}) collective-permute-start(bf16[4,144,256]{2,1,0:T(8,128)(2,1)S(1)} %slice.53), channel_id=1, source_target_pairs={{0,48},{16,0},{32,16},{48,32},{1,49},{17,1},{33,17},{49,33},{2,50}... | collective-permute-start | bytes 884744 | tf_op jit(solution)/shard_map/ppermute | solution.py:300
  56.2 6.9 %copy-start = (bf16[4,128,1024]{2,1,0:T(8,128)(2,1)}, bf16[4,128,1024]{2,1,0:T(8,128)(2,1)S(1)}, u32[]{:S(2)}) copy-start(bf16[4,128,1024]{2,1,0:T(8,128)(2,1)S(1)} %all-to-all-done.q_ref) | copy-start | bytes 3145732
  56.2 31.8 %all-to-all-start.2 = ((bf16[4,128,1024]{2,1,0:T(8,128)(2,1)}), bf16[4,128,1024]{2,1,0:T(8,128)(2,1)}, u32[]{:S(2)}, u32[]{:S(2)}) async-start(bf16[4,128,1024]{2,1,0:T(8,128)(2,1)} %bitcast.22), calls=%async_computation.2 | async-start | bytes 2097152 | tf_op jit(solution)/shard_map/all_to_all | solution.py:288
  88.0 30.5 %all-to-all-start.1 = ((bf16[4,128,1024]{2,1,0:T(8,128)(2,1)}), bf16[4,128,1024]{2,1,0:T(8,128)(2,1)S(1)}, u32[]{:S(2)}, u32[]{:S(2)}) async-start(bf16[4,128,1024]{2,1,0:T(8,128)(2,1)} %get-tuple-element.23.o_ref), calls=%async_computation.1 | async-start | bytes 2097152 | tf_op jit(solution)/shard_map/all_to_all | solution.py:288
  118.5 30.8 %all-to-all-start.3 = ((bf16[4,128,1024]{2,1,0:T(8,128)(2,1)}), bf16[4,128,1024]{2,1,0:T(8,128)(2,1)S(1)}, u32[]{:S(2)}, u32[]{:S(2)}) async-start(bf16[4,128,1024]{2,1,0:T(8,128)(2,1)} %get-tuple-element.28), calls=%async_computation.3 | async-start | bytes 2097152 | tf_op jit(solution)/shard_map/all_to_all | solution.py:288
  125.8 9.8 %collective-permute-start.8 = (bf16[4,128,256]{2,1,0:T(8,128)(2,1)}, bf16[4,128,256]{2,1,0:T(8,128)(2,1)S(1)}, u32[]{:S(2)}, u32[]{:S(2)}) collective-permute-start(bf16[4,128,256]{2,1,0:T(8,128)(2,1)} %get-tuple-element.31), channel_id=1, source_target_pairs={{0,16},{16,32},{32,48},{48,0},{1,17},{17,33},{33,49},{49,1},{2,18}... | collective-permute-start | bytes 786440 | tf_op jit(solution)/shard_map/ppermute | solution.py:310
  127.1 11.7 %collective-permute-start.12 = (bf16[4,128,256]{2,1,0:T(8,128)(2,1)}, bf16[4,128,256]{2,1,0:T(8,128)(2,1)S(1)}, u32[]{:S(2)}, u32[]{:S(2)}) collective-permute-start(bf16[4,128,256]{2,1,0:T(8,128)(2,1)} %get-tuple-element.36), channel_id=1, source_target_pairs={{0,48},{16,0},{32,16},{48,32},{1,49},{17,1},{33,17},{49,33},{2,50}... | collective-permute-start | bytes 786440 | tf_op jit(solution)/shard_map/ppermute | solution.py:311
  129.1 12.7 %collective-permute-start.10 = (bf16[4,128,256]{2,1,0:T(8,128)(2,1)}, bf16[4,128,256]{2,1,0:T(8,128)(2,1)S(1)}, u32[]{:S(2)}, u32[]{:S(2)}) collective-permute-start(bf16[4,128,256]{2,1,0:T(8,128)(2,1)} %get-tuple-element.32), channel_id=1, source_target_pairs={{0,48},{16,0},{32,16},{48,32},{1,49},{17,1},{33,17},{49,33},{2,50}... | collective-permute-start | bytes 786440 | tf_op jit(solution)/shard_map/ppermute | solution.py:314
  136.6 7.7 %collective-permute-start.9 = (bf16[4,128,256]{2,1,0:T(8,128)(2,1)S(1)}, bf16[4,128,256]{2,1,0:T(8,128)(2,1)S(1)}, u32[]{:S(2)}, u32[]{:S(2)}) collective-permute-start(bf16[4,128,256]{2,1,0:T(8,128)(2,1)S(1)} %add_convert_fusion.4), channel_id=1, source_target_pairs={{0,16},{16,32},{32,48},{48,0},{1,17},{17,33},{33,49},{49,1},{2,18}... | collective-permute-start | bytes 786440 | tf_op jit(solution)/shard_map/ppermute | solution.py:312
  137.5 9.5 %collective-permute-start.11 = (bf16[4,128,256]{2,1,0:T(8,128)(2,1)}, bf16[4,128,256]{2,1,0:T(8,128)(2,1)S(1)}, u32[]{:S(2)}, u32[]{:S(2)}) collective-permute-start(bf16[4,128,256]{2,1,0:T(8,128)(2,1)} %get-tuple-element.34), channel_id=1, source_target_pairs={{0,16},{16,32},{32,48},{48,0},{1,17},{17,33},{33,49},{49,1},{2,18}... | collective-permute-start | bytes 786440 | tf_op jit(solution)/shard_map/ppermute | solution.py:312
  139.8 7.3 %collective-permute-start.13 = (bf16[4,128,256]{2,1,0:T(8,128)(2,1)S(1)}, bf16[4,128,256]{2,1,0:T(8,128)(2,1)S(1)}, u32[]{:S(2)}, u32[]{:S(2)}) collective-permute-start(bf16[4,128,256]{2,1,0:T(8,128)(2,1)S(1)} %add_convert_fusion.2), channel_id=1, source_target_pairs={{0,48},{16,0},{32,16},{48,32},{1,49},{17,1},{33,17},{49,33},{2,50}... | collective-permute-start | bytes 786440 | tf_op jit(solution)/shard_map/ppermute | solution.py:315
  149.3 20.5 %all-to-all-start.4 = ((bf16[8,128,256]{2,1,0:T(8,128)(2,1)}), bf16[8,128,256]{2,1,0:T(8,128)(2,1)S(1)}, u32[]{:S(2)}, u32[]{:S(2)}) async-start(bf16[8,128,256]{2,1,0:T(8,128)(2,1)} %pad_maximum_fusion), calls=%async_computation.4 | async-start | bytes 1048576 | tf_op jit(solution)/shard_map/all_to_all | solution.py:357

commit v8 on v7

--- a/solution.py
+++ b/solution.py
@@ -219,7 +219,7 @@
 NARROW = jax.ShapeDtypeStruct((NH, ROWS, 2 * DH), BF16)
 WEIGHTS = jax.ShapeDtypeStruct((TILES, BLOCK, COLS), BF16)
 STATS = jax.ShapeDtypeStruct((NH, 1, COLS), F32)
-PARAMS = pltpu.CompilerParams(vmem_limit_bytes=62 * 1024 * 1024)
+PARAMS = pltpu.CompilerParams(vmem_limit_bytes=63 * 1024 * 1024)
 
 
 def cost(matmuls, exps):
@@ -332,7 +332,9 @@
 
 def shards(queries, keys, values, grad_out, positions):
     here = lax.axis_index("zhi").astype(jnp.int32)
-    marks = jnp.concatenate([positions[0] // 64, positions[0] % 64]).astype(BF16)
+    marks = jnp.concatenate(
+        [lax.shift_right_logical(positions[0], 6), jnp.bitwise_and(positions[0], 63)]
+    ).astype(BF16)
     marks = jnp.broadcast_to(marks, (PADDED - ROWS, 2 * DH))
     own = lax.shift_right_logical(positions[0, 0], int(math.log2(2 * BLOCK)))
     own = jnp.where(here < NH // 2, own, NH - 1 - own).astype(jnp.int32)

time: 172 us -> 173 us (level)
    unnamed x16 -> x14, local copies, waits for them, and re-layouts: 8.38 us -> 7.42 us
  transfers between devices with their start and end apart: 19 -> 19, of which waited for: 10 -> 9; matrix products, arithmetic and copies ran while one was open for 11% -> 10% of each run, Pallas kernels for 28% -> 28%
where the time goes in v8:
time: 173 us; the launch traced here: 172 us
  starting transfers between devices  59.6 us (34%)
  Pallas kernels  48.1 us (28%)
  waiting for transfers between devices  40.8 us (24%)
  local copies, waits for them, and re-layouts  14.1 us (8%)
  other arithmetic  7.83 us (5%)
    pallas_call x1, Pallas kernels, run_backward(): pl.pallas_call(backward, name='backward', out_shape=(WIDE,) + (NARROW,) *...  26.6 us
    all_to_all x4, starting transfers between devices, exchange(): return lax.all_to_all(x, 'zhi', split_axis=0, concat_axis=0, tiled=True)  25.1 us
    pallas_call x1, Pallas kernels, run_forward(): pl.pallas_call(forward, name='forward', out_shape=(WIDE, STATS, WEIGHTS),...  21.5 us
    ppermute x1, waiting for transfers between devices, gather_y(): down = lax.ppermute(kv, 'y', ring(1))  11.2 us
    ppermute x3, starting transfers between devices, hop(): return lax.ppermute(x, 'zhi', [(i, (i + step) % NH) for i in range(NH)])  10.2 us
    all_to_all x1, waiting for transfers between devices, shards(): lax.all_to_all(dkv, ('zhi', 'outer'), split_axis=0, concat_axis=0, tiled=...  8.39 us
    all_to_all x1, starting transfers between devices, shards(): lax.all_to_all(dkv, ('zhi', 'outer'), split_axis=0, concat_axis=0, tiled=...  7.53 us
    unnamed x14, local copies, waits for them, and re-layouts  7.42 us
  transfers between devices with their start and end apart: 19, of which 9 were waited for; matrix products, arithmetic and copies ran while one was open for 10% of the time, Pallas kernels for 28%

profile of v8, /device:TPU:2, one launch (start us, length us, event | category | flops | bytes accessed | tf_op | source)
XLA Modules:
  0.0 171.9 jit_solution(3355240669687458675)
XLA Ops:
  0.6 0.7 convert_bitcast_fusion.1
  1.3 0.9 dynamic-slice_bitcast_fusion
  2.3 6.4 %collective-permute-start = (bf16[144,256]{1,0:T(8,128)(2,1)S(1)}, bf16[144,256]{1,0:T(8,128)(2,1)S(1)}, u32[]{:S(2)}, u32[]{:S(2)}) collective-permute-start(bf16[144,256]{1,0:T(8,128)(2,1)S(1)} %get-tuple-element.59), channel_id=1, source_target_pairs={{0,192},{64,0},{128,64},{192,128},{1,193},{65,1},{129,65},{193,129... | collective-permute-start | bytes 221192 | tf_op jit(solution)/shard_map/ppermute | solution.py:280
  8.7 1.0 collective-permute-start.1
  9.6 2.8 %collective-permute-start.2 = (bf16[144,256]{1,0:T(8,128)(2,1)S(1)}, bf16[144,256]{1,0:T(8,128)(2,1)S(1)}, u32[]{:S(2)}, u32[]{:S(2)}) collective-permute-start(bf16[144,256]{1,0:T(8,128)(2,1)S(1)} %get-tuple-element.61), channel_id=1, source_target_pairs={{0,64},{64,128},{128,192},{192,0},{1,65},{65,129},{129,193},{193,1... | collective-permute-start | bytes 221192 | tf_op jit(solution)/shard_map/ppermute | solution.py:280
  13.1 1.6 copy.11
  14.8 1.3 copy.12
  16.1 0.7 pad_add_fusion.turn
  16.7 0.0 collective-permute-done
  16.7 1.6 collective-permute-done.1
  18.4 0.0 collective-permute-done.2
  18.4 1.7 collective-permute-start.3
  20.1 5.3 %collective-permute-done.3 = bf16[4,144,256]{2,1,0:T(8,128)(2,1)S(1)} collective-permute-done((bf16[4,144,256]{2,1,0:T(8,128)(2,1)S(1)}, bf16[4,144,256]{2,1,0:T(8,128)(2,1)S(1)}, u32[]{:S(2)}, u32[]{:S(2)}) %collective-permute-start.3) | collective-permute-done | bytes 294944 | tf_op jit(solution)/shard_map/ppermute | solution.py:284
  25.5 0.0 copy-start.2
  25.5 6.8 %all-to-all-start = ((bf16[4,128,1024]{2,1,0:T(8,128)(2,1)}), bf16[4,128,1024]{2,1,0:T(8,128)(2,1)}, u32[]{:S(2)}, u32[]{:S(2)}) async-start(bf16[4,128,1024]{2,1,0:T(8,128)(2,1)} %bitcast.1), calls=%async_computation | async-start | bytes 2097152 | tf_op jit(solution)/shard_map/all_to_all | solution.py:288
  32.3 1.6 collective-permute-start.5
  33.8 1.7 collective-permute-start.4
  35.5 11.2 %collective-permute-done.5.kv3 = bf16[8,144,256]{2,1,0:T(8,128)(2,1)S(1)} collective-permute-done((bf16[8,144,256]{2,1,0:T(8,128)(2,1)S(1)}, bf16[8,144,256]{2,1,0:T(8,128)(2,1)S(1)}, u32[]{:S(2)}, u32[]{:S(2)}) %collective-permute-start.5) | collective-permute-done | bytes 589856 | tf_op jit(solution)/shard_map/ppermute | solution.py:298
  46.7 0.5 collective-permute-start.6
  47.2 0.0 copy-done.2
  47.2 0.0 collective-permute-done.4.kv1
  47.2 0.8 copy-done.1
  48.0 2.8 %collective-permute-start.7 = (bf16[4,144,256]{2,1,0:T(8,128)(2,1)S(1)}, bf16[4,144,256]{2,1,0:T(8,128)(2,1)S(1)}, u32[]{:S(2)}, u32[]{:S(2)}) collective-permute-start(bf16[4,144,256]{2,1,0:T(8,128)(2,1)S(1)} %slice.53), channel_id=1, source_target_pairs={{0,48},{16,0},{32,16},{48,32},{1,49},{17,1},{33,17},{49,33},{2,50}... | collective-permute-start | bytes 884744 | tf_op jit(solution)/shard_map/ppermute | solution.py:300
  50.9 1.6 copy.14
  52.5 1.3 copy.15
  53.8 0.9 collective-permute-done.6
  54.7 0.7 constant_dynamic-update-slice_fusion.6
  55.5 0.0 collective-permute-done.7
  55.5 0.7 constant_dynamic-update-slice_fusion.5.kv2
  56.2 0.0 all-to-all-done.q_ref
  56.2 6.9 %all-to-all-start.2 = ((bf16[4,128,1024]{2,1,0:T(8,128)(2,1)}), bf16[4,128,1024]{2,1,0:T(8,128)(2,1)}, u32[]{:S(2)}, u32[]{:S(2)}) async-start(bf16[4,128,1024]{2,1,0:T(8,128)(2,1)} %bitcast.23), calls=%async_computation.2 | async-start | bytes 2097152 | tf_op jit(solution)/shard_map/all_to_all | solution.py:288
  63.1 21.5 %forward.1 = (bf16[4,128,1024]{2,1,0:T(8,128)(2,1)}, f32[4,1,1024]{2,1,0:T(1,128)}, bf16[18,512,1024]{2,1,0:T(8,128)(2,1)}) custom-call(s32[3]{0:T(128)} %pad_add_fusion.turn, bf16[4,128,1024]{2,1,0:T(8,128)(2,1)} %all-to-all-done.q_ref, bf16[8,144,256]{2,1,0:T(8,128)(2,1)} %copy-done.2, bf16[8,144,256]{2,1,0:T(8,128)(2,1)} %copy-done.1, ...), custom_call_target="tpu_custom_call" | custom-call | flops 9663676416 | bytes 25165824 | tf_op jit(solution)/shard_map/forward/pallas_call | solution.py:234
  84.6 3.6 %all-to-all-done.2.g_ref = bf16[4,128,1024]{2,1,0:T(8,128)(2,1)} async-done(((bf16[4,128,1024]{2,1,0:T(8,128)(2,1)}), bf16[4,128,1024]{2,1,0:T(8,128)(2,1)}, u32[]{:S(2)}, u32[]{:S(2)}) %all-to-all-start.2) | async-done | bytes 1048608 | tf_op jit(solution)/shard_map/all_to_all | solution.py:288
  88.2 4.4 %all-to-all-start.1 = ((bf16[4,128,1024]{2,1,0:T(8,128)(2,1)}), bf16[4,128,1024]{2,1,0:T(8,128)(2,1)}, u32[]{:S(2)}, u32[]{:S(2)}) async-start(bf16[4,128,1024]{2,1,0:T(8,128)(2,1)} %get-tuple-element.23.o_ref), calls=%async_computation.1 | async-start | bytes 2097152 | tf_op jit(solution)/shard_map/all_to_all | solution.py:288
  92.6 26.6 %backward.1 = (bf16[4,128,1024]{2,1,0:T(8,128)(2,1)}, bf16[4,128,256]{2,1,0:T(8,128)(2,1)}, bf16[4,128,256]{2,1,0:T(8,128)(2,1)}, bf16[4,128,256]{2,1,0:T(8,128)...) custom-call(s32[3]{0:T(128)} %pad_add_fusion.turn, ...), custom_call_target="tpu_custom_call" | custom-call | flops 19327352832 | bytes 25165824 | tf_op jit(solution)/shard_map/backward/pallas_call | solution.py:255
  119.3 0.0 all-to-all-done.1
  119.3 7.0 %all-to-all-start.3 = ((bf16[4,128,1024]{2,1,0:T(8,128)(2,1)}), bf16[4,128,1024]{2,1,0:T(8,128)(2,1)S(1)}, u32[]{:S(2)}, u32[]{:S(2)}) async-start(bf16[4,128,1024]{2,1,0:T(8,128)(2,1)} %get-tuple-element.28), calls=%async_computation.3 | async-start | bytes 2097152 | tf_op jit(solution)/shard_map/all_to_all | solution.py:288
  126.2 0.6 collective-permute-start.8
  126.8 2.6 %collective-permute-start.12 = (bf16[4,128,256]{2,1,0:T(8,128)(2,1)}, bf16[4,128,256]{2,1,0:T(8,128)(2,1)S(1)}, u32[]{:S(2)}, u32[]{:S(2)}) collective-permute-start(bf16[4,128,256]{2,1,0:T(8,128)(2,1)} %get-tuple-element.36), channel_id=1, source_target_pairs={{0,48},{16,0},{32,16},{48,32},{1,49},{17,1},{33,17},{49,33},{2,50}... | collective-permute-start | bytes 786440 | tf_op jit(solution)/shard_map/ppermute | solution.py:311
  129.5 1.8 %collective-permute-start.10 = (bf16[4,128,256]{2,1,0:T(8,128)(2,1)}, bf16[4,128,256]{2,1,0:T(8,128)(2,1)S(1)}, u32[]{:S(2)}, u32[]{:S(2)}) collective-permute-start(bf16[4,128,256]{2,1,0:T(8,128)(2,1)} %get-tuple-element.32), channel_id=1, source_target_pairs={{0,48},{16,0},{32,16},{48,32},{1,49},{17,1},{33,17},{49,33},{2,50}... | collective-permute-start | bytes 786440 | tf_op jit(solution)/shard_map/ppermute | solution.py:314
  131.3 4.9 %collective-permute-done.8 = bf16[4,128,256]{2,1,0:T(8,128)(2,1)S(1)} collective-permute-done((bf16[4,128,256]{2,1,0:T(8,128)(2,1)}, bf16[4,128,256]{2,1,0:T(8,128)(2,1)S(1)}, u32[]{:S(2)}, u32[]{:S(2)}) %collective-permute-start.8) | collective-permute-done | bytes 262176 | tf_op jit(solution)/shard_map/ppermute | solution.py:310
  136.2 1.0 add_convert_fusion.4
  137.2 0.1 collective-permute-start.9
  137.3 1.4 collective-permute-start.11
  138.8 0.0 collective-permute-done.12
  138.8 1.0 add_convert_fusion.2
  139.8 1.9 %collective-permute-start.13 = (bf16[4,128,256]{2,1,0:T(8,128)(2,1)S(1)}, bf16[4,128,256]{2,1,0:T(8,128)(2,1)S(1)}, u32[]{:S(2)}, u32[]{:S(2)}) collective-permute-start(bf16[4,128,256]{2,1,0:T(8,128)(2,1)S(1)} %add_convert_fusion.2), channel_id=1, source_target_pairs={{0,48},{16,0},{32,16},{48,32},{1,49},{17,1},{33,17},{49,33},{2,50}... | collective-permute-start | bytes 786440 | tf_op jit(solution)/shard_map/ppermute | solution.py:315
  141.7 0.0 collective-permute-done.10
  141.7 3.1 %collective-permute-done.9 = bf16[4,128,256]{2,1,0:T(8,128)(2,1)S(1)} collective-permute-done((bf16[4,128,256]{2,1,0:T(8,128)(2,1)S(1)}, bf16[4,128,256]{2,1,0:T(8,128)(2,1)S(1)}, u32[]{:S(2)}, u32[]{:S(2)}) %collective-permute-start.9) | collective-permute-done | bytes 262176 | tf_op jit(solution)/shard_map/ppermute | solution.py:312
  144.9 1.1 add_convert_fusion.3
  146.0 1.7 %collective-permute-done.11 = bf16[4,128,256]{2,1,0:T(8,128)(2,1)S(1)} collective-permute-done((bf16[4,128,256]{2,1,0:T(8,128)(2,1)}, bf16[4,128,256]{2,1,0:T(8,128)(2,1)S(1)}, u32[]{:S(2)}, u32[]{:S(2)}) %collective-permute-start.11) | collective-permute-done | bytes 262176 | tf_op jit(solution)/shard_map/ppermute | solution.py:312
  147.7 0.0 collective-permute-done.13
  147.7 1.1 add_convert_fusion.1
  148.8 0.9 pad_maximum_fusion
  149.6 0.0 all-to-all-done.3
  149.6 7.5 %all-to-all-start.4 = ((bf16[8,128,256]{2,1,0:T(8,128)(2,1)}), bf16[8,128,256]{2,1,0:T(8,128)(2,1)S(1)}, u32[]{:S(2)}, u32[]{:S(2)}) async-start(bf16[8,128,256]{2,1,0:T(8,128)(2,1)} %pad_maximum_fusion), calls=%async_computation.4 | async-start | bytes 1048576 | tf_op jit(solution)/shard_map/all_to_all | solution.py:359
  157.2 1.6 copy.13
  158.8 1.3 copy.19
  160.1 0.7 copy.16
  160.7 1.3 copy.20
  162.1 8.4 %all-to-all-done.4 = bf16[8,128,256]{2,1,0:T(8,128)(2,1)S(1)} async-done(((bf16[8,128,256]{2,1,0:T(8,128)(2,1)}), bf16[8,128,256]{2,1,0:T(8,128)(2,1)S(1)}, u32[]{:S(2)}, u32[]{:S(2)}) %all-to-all-start.4) | async-done | bytes 524320 | tf_op jit(solution)/shard_map/all_to_all | solution.py:359
  170.4 0.1 fusion
  170.6 0.7 maximum_bitcast_fusion.1
  171.2 0.7 maximum_bitcast_fusion
  (15 shorter events, 0.2 us)
Async XLA Ops:
  2.3 14.5 %collective-permute-start = (bf16[144,256]{1,0:T(8,128)(2,1)S(1)}, bf16[144,256]{1,0:T(8,128)(2,1)S(1)}, u32[]{:S(2)}, u32[]{:S(2)}) collective-permute-start(bf16[144,256]{1,0:T(8,128)(2,1)S(1)} %get-tuple-element.59), channel_id=1, source_target_pairs={{0,192},{64,0},{128,64},{192,128},{1,193},{65,1},{129,65},{193,129... | collective-permute-start | bytes 221192 | tf_op jit(solution)/shard_map/ppermute | solution.py:280
  8.7 9.7 %collective-permute-start.1 = (bf16[144,256]{1,0:T(8,128)(2,1)S(1)}, bf16[144,256]{1,0:T(8,128)(2,1)S(1)}, u32[]{:S(2)}, u32[]{:S(2)}) collective-permute-start(bf16[144,256]{1,0:T(8,128)(2,1)S(1)} %get-tuple-element.60), channel_id=1, source_target_pairs={{0,128},{64,192},{128,0},{192,64},{1,129},{65,193},{129,1},{193,65... | collective-permute-start | bytes 221192 | tf_op jit(solution)/shard_map/ppermute | solution.py:280
  9.6 8.7 %collective-permute-start.2 = (bf16[144,256]{1,0:T(8,128)(2,1)S(1)}, bf16[144,256]{1,0:T(8,128)(2,1)S(1)}, u32[]{:S(2)}, u32[]{:S(2)}) collective-permute-start(bf16[144,256]{1,0:T(8,128)(2,1)S(1)} %get-tuple-element.61), channel_id=1, source_target_pairs={{0,64},{64,128},{128,192},{192,0},{1,65},{65,129},{129,193},{193,1... | collective-permute-start | bytes 221192 | tf_op jit(solution)/shard_map/ppermute | solution.py:280
  18.4 7.1 %collective-permute-start.3 = (bf16[4,144,256]{2,1,0:T(8,128)(2,1)S(1)}, bf16[4,144,256]{2,1,0:T(8,128)(2,1)S(1)}, u32[]{:S(2)}, u32[]{:S(2)}) collective-permute-start(bf16[4,144,256]{2,1,0:T(8,128)(2,1)S(1)} %pad_maximum_fusion.1), channel_id=1, source_target_pairs={{0,1},{1,0},{2,3},{3,2},{4,5},{5,4},{6,7},{7,6},{8,9},{9,8},{10,11... | collective-permute-start | bytes 884744 | tf_op jit(solution)/shard_map/ppermute | solution.py:284
  25.5 21.7 %copy-start.2 = (bf16[8,144,256]{2,1,0:T(8,128)(2,1)}, bf16[8,144,256]{2,1,0:T(8,128)(2,1)S(1)}, u32[]{:S(2)}) copy-start(bf16[8,144,256]{2,1,0:T(8,128)(2,1)S(1)} %constant_dynamic-update-slice_fusion.kv0) | copy-start | bytes 1769476
  25.5 30.7 %all-to-all-start = ((bf16[4,128,1024]{2,1,0:T(8,128)(2,1)}), bf16[4,128,1024]{2,1,0:T(8,128)(2,1)}, u32[]{:S(2)}, u32[]{:S(2)}) async-start(bf16[4,128,1024]{2,1,0:T(8,128)(2,1)} %bitcast.1), calls=%async_computation | async-start | bytes 2097152 | tf_op jit(solution)/shard_map/all_to_all | solution.py:288
  32.3 14.4 %collective-permute-start.5 = (bf16[8,144,256]{2,1,0:T(8,128)(2,1)S(1)}, bf16[8,144,256]{2,1,0:T(8,128)(2,1)S(1)}, u32[]{:S(2)}, u32[]{:S(2)}) collective-permute-start(bf16[8,144,256]{2,1,0:T(8,128)(2,1)S(1)} %constant_dynamic-update-slice_fusion.kv0), channel_id=1, source_target_pairs={{0,16},{16,32},{32,48},{48,0},{1,17},{17,33},{33,49},{49,1},{2,18}... | collective-permute-start | bytes 1769480 | tf_op jit(solution)/shard_map/ppermute | solution.py:298
  33.8 13.4 %collective-permute-start.4 = (bf16[8,144,256]{2,1,0:T(8,128)(2,1)S(1)}, bf16[8,144,256]{2,1,0:T(8,128)(2,1)S(1)}, u32[]{:S(2)}, u32[]{:S(2)}) collective-permute-start(bf16[8,144,256]{2,1,0:T(8,128)(2,1)S(1)} %constant_dynamic-update-slice_fusion.kv0), channel_id=1, source_target_pairs={{0,48},{16,0},{32,16},{48,32},{1,49},{17,1},{33,17},{49,33},{2,50}... | collective-permute-start | bytes 1769480 | tf_op jit(solution)/shard_map/ppermute | solution.py:297
  46.7 16.4 %copy-start = (bf16[8,144,256]{2,1,0:T(8,128)(2,1)}, bf16[8,144,256]{2,1,0:T(8,128)(2,1)S(1)}, u32[]{:S(2)}) copy-start(bf16[8,144,256]{2,1,0:T(8,128)(2,1)S(1)} %collective-permute-done.5.kv3) | copy-start | bytes 1769476
  46.7 8.0 %collective-permute-start.6 = (bf16[4,144,256]{2,1,0:T(8,128)(2,1)S(1)}, bf16[4,144,256]{2,1,0:T(8,128)(2,1)S(1)}, u32[]{:S(2)}, u32[]{:S(2)}) collective-permute-start(bf16[4,144,256]{2,1,0:T(8,128)(2,1)S(1)} %slice.52), channel_id=1, source_target_pairs={{0,16},{16,32},{32,48},{48,0},{1,17},{17,33},{33,49},{49,1},{2,18}... | collective-permute-start | bytes 884744 | tf_op jit(solution)/shard_map/ppermute | solution.py:300
  47.2 0.8 copy-start.1
  48.0 7.4 %collective-permute-start.7 = (bf16[4,144,256]{2,1,0:T(8,128)(2,1)S(1)}, bf16[4,144,256]{2,1,0:T(8,128)(2,1)S(1)}, u32[]{:S(2)}, u32[]{:S(2)}) collective-permute-start(bf16[4,144,256]{2,1,0:T(8,128)(2,1)S(1)} %slice.53), channel_id=1, source_target_pairs={{0,48},{16,0},{32,16},{48,32},{1,49},{17,1},{33,17},{49,33},{2,50}... | collective-permute-start | bytes 884744 | tf_op jit(solution)/shard_map/ppermute | solution.py:300
  56.2 32.0 %all-to-all-start.2 = ((bf16[4,128,1024]{2,1,0:T(8,128)(2,1)}), bf16[4,128,1024]{2,1,0:T(8,128)(2,1)}, u32[]{:S(2)}, u32[]{:S(2)}) async-start(bf16[4,128,1024]{2,1,0:T(8,128)(2,1)} %bitcast.23), calls=%async_computation.2 | async-start | bytes 2097152 | tf_op jit(solution)/shard_map/all_to_all | solution.py:288
  88.2 31.1 %all-to-all-start.1 = ((bf16[4,128,1024]{2,1,0:T(8,128)(2,1)}), bf16[4,128,1024]{2,1,0:T(8,128)(2,1)}, u32[]{:S(2)}, u32[]{:S(2)}) async-start(bf16[4,128,1024]{2,1,0:T(8,128)(2,1)} %get-tuple-element.23.o_ref), calls=%async_computation.1 | async-start | bytes 2097152 | tf_op jit(solution)/shard_map/all_to_all | solution.py:288
  119.3 30.4 %all-to-all-start.3 = ((bf16[4,128,1024]{2,1,0:T(8,128)(2,1)}), bf16[4,128,1024]{2,1,0:T(8,128)(2,1)S(1)}, u32[]{:S(2)}, u32[]{:S(2)}) async-start(bf16[4,128,1024]{2,1,0:T(8,128)(2,1)} %get-tuple-element.28), calls=%async_computation.3 | async-start | bytes 2097152 | tf_op jit(solution)/shard_map/all_to_all | solution.py:288
  126.2 10.0 %collective-permute-start.8 = (bf16[4,128,256]{2,1,0:T(8,128)(2,1)}, bf16[4,128,256]{2,1,0:T(8,128)(2,1)S(1)}, u32[]{:S(2)}, u32[]{:S(2)}) collective-permute-start(bf16[4,128,256]{2,1,0:T(8,128)(2,1)} %get-tuple-element.31), channel_id=1, source_target_pairs={{0,16},{16,32},{32,48},{48,0},{1,17},{17,33},{33,49},{49,1},{2,18}... | collective-permute-start | bytes 786440 | tf_op jit(solution)/shard_map/ppermute | solution.py:310
  126.8 11.9 %collective-permute-start.12 = (bf16[4,128,256]{2,1,0:T(8,128)(2,1)}, bf16[4,128,256]{2,1,0:T(8,128)(2,1)S(1)}, u32[]{:S(2)}, u32[]{:S(2)}) collective-permute-start(bf16[4,128,256]{2,1,0:T(8,128)(2,1)} %get-tuple-element.36), channel_id=1, source_target_pairs={{0,48},{16,0},{32,16},{48,32},{1,49},{17,1},{33,17},{49,33},{2,50}... | collective-permute-start | bytes 786440 | tf_op jit(solution)/shard_map/ppermute | solution.py:311
  129.5 12.3 %collective-permute-start.10 = (bf16[4,128,256]{2,1,0:T(8,128)(2,1)}, bf16[4,128,256]{2,1,0:T(8,128)(2,1)S(1)}, u32[]{:S(2)}, u32[]{:S(2)}) collective-permute-start(bf16[4,128,256]{2,1,0:T(8,128)(2,1)} %get-tuple-element.32), channel_id=1, source_target_pairs={{0,48},{16,0},{32,16},{48,32},{1,49},{17,1},{33,17},{49,33},{2,50}... | collective-permute-start | bytes 786440 | tf_op jit(solution)/shard_map/ppermute | solution.py:314
  137.2 7.7 %collective-permute-start.9 = (bf16[4,128,256]{2,1,0:T(8,128)(2,1)S(1)}, bf16[4,128,256]{2,1,0:T(8,128)(2,1)S(1)}, u32[]{:S(2)}, u32[]{:S(2)}) collective-permute-start(bf16[4,128,256]{2,1,0:T(8,128)(2,1)S(1)} %add_convert_fusion.4), channel_id=1, source_target_pairs={{0,16},{16,32},{32,48},{48,0},{1,17},{17,33},{33,49},{49,1},{2,18}... | collective-permute-start | bytes 786440 | tf_op jit(solution)/shard_map/ppermute | solution.py:312
  137.3 10.4 %collective-permute-start.11 = (bf16[4,128,256]{2,1,0:T(8,128)(2,1)}, bf16[4,128,256]{2,1,0:T(8,128)(2,1)S(1)}, u32[]{:S(2)}, u32[]{:S(2)}) collective-permute-start(bf16[4,128,256]{2,1,0:T(8,128)(2,1)} %get-tuple-element.34), channel_id=1, source_target_pairs={{0,16},{16,32},{32,48},{48,0},{1,17},{17,33},{33,49},{49,1},{2,18}... | collective-permute-start | bytes 786440 | tf_op jit(solution)/shard_map/ppermute | solution.py:312
  139.8 7.9 %collective-permute-start.13 = (bf16[4,128,256]{2,1,0:T(8,128)(2,1)S(1)}, bf16[4,128,256]{2,1,0:T(8,128)(2,1)S(1)}, u32[]{:S(2)}, u32[]{:S(2)}) collective-permute-start(bf16[4,128,256]{2,1,0:T(8,128)(2,1)S(1)} %add_convert_fusion.2), channel_id=1, source_target_pairs={{0,48},{16,0},{32,16},{48,32},{1,49},{17,1},{33,17},{49,33},{2,50}... | collective-permute-start | bytes 786440 | tf_op jit(solution)/shard_map/ppermute | solution.py:315
  149.6 20.8 %all-to-all-start.4 = ((bf16[8,128,256]{2,1,0:T(8,128)(2,1)}), bf16[8,128,256]{2,1,0:T(8,128)(2,1)S(1)}, u32[]{:S(2)}, u32[]{:S(2)}) async-start(bf16[8,128,256]{2,1,0:T(8,128)(2,1)} %pad_maximum_fusion), calls=%async_computation.4 | async-start | bytes 1048576 | tf_op jit(solution)/shard_map/all_to_all | solution.py:359
